TPU v7x, 256 devices: a whole 4x4x8 slice. The times are simulated.
256 devices in a mesh: blk: 64 (over y, z, core), mp: 4 (over x).
Axes of the slice: x: 4, y: 4, z: 8, core: 2. Of those that a mesh axis runs over, the one named last changes fastest.
Arguments:
- hidden_states: bfloat16 [8192, 4096], P('blk', 'mp'), may hold values from -6 to 6
- expert_ids: int32 [8192, 1], P('blk'), may hold values from 0 to 31; in each aligned block of 128 rows (0 to 127, 128 to 255, ...) at most 5 rows name the same one
- probs: bfloat16 [8192, 1], P('blk'), may hold values from 0.049804688 to 0.59765625
- cotangent: bfloat16 [8192, 4096], P('blk', 'mp'), may hold values from -6 to 6
- w_gate: bfloat16 [49152, 4096], P(('blk', 'mp')), may hold values from -0.09375 to 0.09375
- w_up: bfloat16 [49152, 4096], P(('blk', 'mp')), may hold values from -0.09375 to 0.09375
- w_down: bfloat16 [49152, 4096], P(('blk', 'mp')), may hold values from -0.15625 to 0.15625
Outputs:
- mixed: bfloat16 [8192, 4096], P('blk', 'mp')
- grad_hidden: bfloat16 [8192, 4096], P('blk', 'mp')
- grad_probs: float32 [8192, 1], P('blk')
- grad_w_gate: bfloat16 [49152, 4096], P(('blk', 'mp'))
- grad_w_up: bfloat16 [49152, 4096], P(('blk', 'mp'))
- grad_w_down: bfloat16 [49152, 4096], P(('blk', 'mp'))
Inputs may be any that keep to these rules, and one draw needn't show every extreme that they name: `expert_ids`: among the tokens of one index of blk (aligned blocks of 128 rows) no expert is named more than 5 times, and in every draw some expert is named exactly 5 times in some block.
All inputs are finite; a program needn't handle non-finite values.
Results may differ from a plain program's by a relative error of at most 0.017.
Values may be sent and summed in bfloat16 or wider, within the bound.
No kernel may reach another device: no remote copies, remote signals or barrier semaphores. Data moves between devices by JAX's collectives and lax.ppermute only.
A program may use at most 128 MiB of HBM per device.

v0:
```python
import jax
import jax.numpy as jnp
from jax import lax
from jax.sharding import PartitionSpec as P

FF = 1536
EXPERTS = 32
CAP = 5


def home_index(flat_ids, rank_in_group, capacity, copies):
    row_ids = flat_ids[:, None] * copies + jnp.arange(copies, dtype=jnp.int32)[None, :]
    return (row_ids * capacity + rank_in_group[:, None], jnp.ones(row_ids.shape, jnp.float32))


def collect(returned, row_index, is_valid):
    flat_rows = returned.reshape(-1, returned.shape[-1])
    taken = jnp.take(flat_rows, row_index, axis=0).astype(jnp.float32)
    return jnp.sum(taken * is_valid[:, :, None], axis=1)


def body(hidden_states, expert_ids, probs, cotangent, w_gate, w_up, w_down):
    blk_count = lax.axis_size("blk")
    mp_count = lax.axis_size("mp")
    token_count = hidden_states.shape[0]
    routed = expert_ids.shape[1]
    pair_count = token_count * routed
    model_width = w_gate.shape[1]
    dev_rows = w_gate.shape[0]
    blk_rows = dev_rows * mp_count
    capacity = CAP
    copies = FF // blk_rows
    blk_experts = 1
    dev_experts = 1
    block_rows = min(dev_rows, FF)
    flat_ids = expert_ids.reshape(pair_count)
    onehot = (flat_ids[:, None] == jnp.arange(EXPERTS, dtype=jnp.int32)[None, :]).astype(jnp.int32)
    rank_in_group = jnp.sum((jnp.cumsum(onehot, axis=0) - 1) * onehot, axis=1)
    slot_place = flat_ids * capacity + rank_in_group
    target = jnp.arange(EXPERTS * copies * capacity, dtype=jnp.int32)
    target_slot = target // capacity // copies * capacity + target % capacity
    select = (slot_place[None, :] == target_slot[:, None]).astype(jnp.bfloat16)

    def grouped(values):
        per_pair = jnp.repeat(values, routed, axis=0)
        placed = jnp.dot(select, per_pair, preferred_element_type=jnp.float32).astype(jnp.bfloat16)
        return placed.reshape((blk_count, blk_experts, capacity) + values.shape[1:])

    slot_probs = jnp.dot(select, probs, preferred_element_type=jnp.float32)[:, 0].astype(
        jnp.bfloat16
    )
    slot_probs = slot_probs.reshape(blk_count, blk_experts, capacity)
    features, grad_rows = (
        lax.all_gather(hidden_states, "mp", axis=1, tiled=True),
        lax.all_gather(cotangent, "mp", axis=1, tiled=True),
    )
    sent_x, sent_grad, sent_prob = (
        lax.all_to_all(grouped(features), "blk", split_axis=0, concat_axis=2, tiled=True),
        lax.all_to_all(grouped(grad_rows), "blk", split_axis=0, concat_axis=2, tiled=True),
        lax.all_to_all(slot_probs, "blk", split_axis=0, concat_axis=2, tiled=True),
    )
    slot_x = sent_x[0]
    slot_grad = sent_grad[0]
    slot_prob = sent_prob[0]
    gate_rows = w_gate.reshape(dev_experts, block_rows, model_width)
    up_rows = w_up.reshape(dev_experts, block_rows, model_width)
    down_rows = w_down.reshape(dev_experts, block_rows, model_width)
    gate_pre = jnp.einsum("end,ehd->enh", slot_x, gate_rows, preferred_element_type=jnp.float32)
    up_pre = jnp.einsum("end,ehd->enh", slot_x, up_rows, preferred_element_type=jnp.float32)
    sigmoid_gate = jax.nn.sigmoid(gate_pre)
    activated = gate_pre * sigmoid_gate
    gated = (activated * up_pre).astype(jnp.bfloat16)
    part_out = jnp.einsum("enh,ehd->end", gated, down_rows, preferred_element_type=jnp.float32)
    scaled = (slot_prob.astype(jnp.float32)[:, :, None] * slot_grad.astype(jnp.float32)).astype(
        jnp.bfloat16
    )
    grad_gated = jnp.einsum("end,ehd->enh", scaled, down_rows, preferred_element_type=jnp.float32)
    grad_gate_pre = (
        grad_gated * up_pre * sigmoid_gate * (1.0 + gate_pre * (1.0 - sigmoid_gate))
    ).astype(jnp.bfloat16)
    grad_up_pre = (grad_gated * activated).astype(jnp.bfloat16)
    part_dx = jnp.einsum(
        "enh,ehd->end", grad_gate_pre, gate_rows, preferred_element_type=jnp.float32
    )
    part_dx = part_dx + jnp.einsum(
        "enh,ehd->end", grad_up_pre, up_rows, preferred_element_type=jnp.float32
    )
    grad_w_gate = (
        jnp.einsum("enh,end->ehd", grad_gate_pre, slot_x, preferred_element_type=jnp.float32)
        .reshape(dev_rows, model_width)
        .astype(jnp.bfloat16)
    )
    grad_w_up = (
        jnp.einsum("enh,end->ehd", grad_up_pre, slot_x, preferred_element_type=jnp.float32)
        .reshape(dev_rows, model_width)
        .astype(jnp.bfloat16)
    )
    grad_w_down = (
        jnp.einsum("enh,end->ehd", gated, scaled, preferred_element_type=jnp.float32)
        .reshape(dev_rows, model_width)
        .astype(jnp.bfloat16)
    )
    back_out, back_dx = (
        lax.all_to_all(
            part_out.astype(jnp.bfloat16), "blk", split_axis=1, concat_axis=0, tiled=True
        ),
        lax.all_to_all(
            part_dx.astype(jnp.bfloat16), "blk", split_axis=1, concat_axis=0, tiled=True
        ),
    )
    row_index, is_valid = home_index(flat_ids, rank_in_group, capacity, copies)
    pair_out = collect(back_out, row_index, is_valid)
    token_dx = jnp.sum(
        collect(back_dx, row_index, is_valid).reshape(token_count, routed, model_width), axis=1
    )
    pair_out, token_dx = (
        lax.psum_scatter(
            pair_out.astype(jnp.bfloat16), "mp", scatter_dimension=1, tiled=True
        ).astype(jnp.float32),
        lax.psum_scatter(
            token_dx.astype(jnp.bfloat16), "mp", scatter_dimension=1, tiled=True
        ).astype(jnp.float32),
    )
    pair_out = pair_out.reshape(token_count, routed, -1)
    mixed = jnp.sum(probs.astype(jnp.float32)[:, :, None] * pair_out, axis=1).astype(jnp.bfloat16)
    probe_terms = jnp.sum(cotangent.astype(jnp.float32)[:, None, :] * pair_out, axis=2)
    grad_probs = lax.psum(probe_terms, "mp")
    return (mixed, token_dx.astype(jnp.bfloat16), grad_probs, grad_w_gate, grad_w_up, grad_w_down)


def solution(mesh):
    placed = (
        P("blk", "mp"),
        P("blk", None),
        P("blk", None),
        P("blk", "mp"),
        P(("blk", "mp"), None),
        P(("blk", "mp"), None),
        P(("blk", "mp"), None),
    )
    return jax.shard_map(
        body,
        mesh=mesh,
        in_specs=placed,
        out_specs=(
            P("blk", "mp"),
            P("blk", "mp"),
            P("blk", None),
            P(("blk", "mp"), None),
            P(("blk", "mp"), None),
            P(("blk", "mp"), None),
        ),
        check_vma=False,
    )
```

profile of v0, /device:TPU:32, one launch (start us, length us, event | category | flops | bytes accessed | tf_op | source)
XLA Modules:
  0.0 538.5 jit_solution(15826237463961847663)
XLA Ops:
  12.2 11.8 %all-to-all-start.2 = ((bf16[64,1,5]{2,1,0:T(2,128)(2,1)}), bf16[64,1,5]{2,1,0:T(2,128)(2,1)S(1)}, u32[]{:S(2)}, u32[]{:S(2)}) async-start(bf16[64,1,5]{2,1,0:T(2,128)(2,1)} %copy.27), calls=%async_computation.3 | async-start | bytes 65536 | tf_op jit(solution)/shard_map/all_to_all | solution.py:60
  24.0 14.9 %all-gather.3.cloned.1.call-done = bf16[128,4096]{1,0:T(8,128)(2,1)} async-done(((bf16[128,1024]{1,0:T(8,128)(2,1)}), bf16[128,4096]{1,0:T(8,128)(2,1)}) %all-gather.3.cloned.1.call-update) | async-done | bytes 1048592 | tf_op jit(solution)/shard_map/all_gather | solution.py:54
  42.6 4.7 reshape.249
  47.3 10.7 %all-to-all-start = ((bf16[64,1,5,4096]{3,2,1,0:T(8,128)(2,1)}), bf16[64,1,5,4096]{3,2,1,0:T(8,128)(2,1)}, u32[]{:S(2)}, u32[]{:S(2)}) async-start(bf16[64,1,5,4096]{3,2,1,0:T(8,128)(2,1)} %bitcast.61), calls=%async_computation | async-start | bytes 8388608 | tf_op jit(solution)/shard_map/all_to_all | solution.py:58
  58.7 28.6 %all-gather.5.cloned.1.call-done = bf16[128,4096]{1,0:T(8,128)(2,1)} async-done(((bf16[128,1024]{1,0:T(8,128)(2,1)}), bf16[128,4096]{1,0:T(8,128)(2,1)}) %all-gather.5.cloned.1.call-update) | async-done | bytes 1048592 | tf_op jit(solution)/shard_map/all_gather | solution.py:55
  91.0 4.7 reshape.252
  95.7 56.4 %all-to-all-done = bf16[64,1,5,4096]{3,2,1,0:T(8,128)(2,1)} async-done(((bf16[64,1,5,4096]{3,2,1,0:T(8,128)(2,1)}), bf16[64,1,5,4096]{3,2,1,0:T(8,128)(2,1)}, u32[]{:S(2)}, u32[]{:S(2)}) %all-to-all-start) | async-done | bytes 2621472 | tf_op jit(solution)/shard_map/all_to_all | solution.py:58
  152.0 8.1 %all-to-all-start.3 = ((bf16[64,1,5,4096]{3,2,1,0:T(8,128)(2,1)}), bf16[64,1,5,4096]{3,2,1,0:T(8,128)(2,1)}, u32[]{:S(2)}, u32[]{:S(2)}) async-start(bf16[64,1,5,4096]{3,2,1,0:T(8,128)(2,1)} %bitcast.62), calls=%async_computation.4 | async-start | bytes 8388608 | tf_op jit(solution)/shard_map/all_to_all | solution.py:59
  160.4 4.9 reshape.250
  168.9 85.2 %all-to-all-done.3 = bf16[64,1,5,4096]{3,2,1,0:T(8,128)(2,1)} async-done(((bf16[64,1,5,4096]{3,2,1,0:T(8,128)(2,1)}), bf16[64,1,5,4096]{3,2,1,0:T(8,128)(2,1)}, u32[]{:S(2)}, u32[]{:S(2)}) %all-to-all-start.3) | async-done | bytes 2621472 | tf_op jit(solution)/shard_map/all_to_all | solution.py:59
  254.2 5.3 reshape.255
  259.5 3.9 fusion.39
  267.6 10.1 %copy.44 = bf16[1,320,4096]{2,0,1:T(2,128)(2,1)} copy(bf16[1,320,4096]{2,1,0:T(8,128)(2,1)} %fusion.1) | data formatting | bytes 5242880 | tf_op jit(solution)/shard_map/convert_element_type | solution.py:105
  278.2 17.9 %reduce.9 = bf16[320,4096]{1,0:T(8,128)(2,1)} reduce(bf16[320,1,4096]{2,1,0:T(2,128)(2,1)} %bitcast.57, bf16[]{:T(256)} %broadcast.164), dimensions={1}, to_apply=%bitcast.54.reduce_sub_computation | reduce | bytes 5242882
  296.2 5.0 reshape.295
  301.2 7.7 %all-to-all-start.1 = ((bf16[64,2,10240]{2,1,0:T(2,128)(2,1)}), bf16[64,2,10240]{2,1,0:T(2,128)(2,1)}, u32[]{:S(2)}, u32[]{:S(2)}) async-start(bf16[64,2,10240]{2,1,0:T(2,128)(2,1)} %reshape.295), calls=%async_computation.1 | async-start | bytes 5242880 | tf_op jit(solution)/shard_map/all_to_all | solution.py:104
  313.1 10.0 %copy.43 = bf16[1,320,4096]{2,0,1:T(2,128)(2,1)} copy(bf16[1,320,4096]{2,1,0:T(8,128)(2,1)} %fusion.2) | data formatting | bytes 5242880 | tf_op jit(solution)/shard_map/convert_element_type | solution.py:108
  323.1 16.5 %reduce.8 = bf16[320,4096]{1,0:T(8,128)(2,1)S(1)} reduce(bf16[320,1,4096]{2,1,0:T(2,128)(2,1)} %bitcast.58, bf16[]{:T(256)} %broadcast.164), dimensions={1}, to_apply=%bitcast.53.reduce_sub_computation | reduce | bytes 5242882
  342.9 26.6 %all-to-all-done.1 = bf16[64,2,10240]{2,1,0:T(2,128)(2,1)} async-done(((bf16[64,2,10240]{2,1,0:T(2,128)(2,1)}), bf16[64,2,10240]{2,1,0:T(2,128)(2,1)}, u32[]{:S(2)}, u32[]{:S(2)}) %all-to-all-start.1) | async-done | bytes 2621472 | tf_op jit(solution)/shard_map/all_to_all | solution.py:104
  369.5 7.6 %all-to-all-start.4 = ((bf16[64,2,10240]{2,1,0:T(2,128)(2,1)}), bf16[64,2,10240]{2,1,0:T(2,128)(2,1)}, u32[]{:S(2)}, u32[]{:S(2)}) async-start(bf16[64,2,10240]{2,1,0:T(2,128)(2,1)} %reshape.293), calls=%async_computation.5 | async-start | bytes 5242880 | tf_op jit(solution)/shard_map/all_to_all | solution.py:107
  378.0 16.3 %reshape.296 = bf16[320,1,4096]{2,1,0:T(2,128)(2,1)} reshape(bf16[64,2,10240]{2,1,0:T(2,128)(2,1)} %all-to-all-done.1) | data formatting | bytes 5242880
  394.3 5.4 %copy.42 = bf16[1,320,4096]{2,1,0:T(8,128)(2,1)S(1)} copy(bf16[1,320,4096]{2,0,1:T(2,128)(2,1)} %bitcast.59) | data formatting | bytes 5242880
  402.9 4.4 reshape.279
  407.3 30.4 %all-to-all-done.4 = bf16[64,2,10240]{2,1,0:T(2,128)(2,1)} async-done(((bf16[64,2,10240]{2,1,0:T(2,128)(2,1)}), bf16[64,2,10240]{2,1,0:T(2,128)(2,1)}, u32[]{:S(2)}, u32[]{:S(2)}) %all-to-all-start.4) | async-done | bytes 2621472 | tf_op jit(solution)/shard_map/all_to_all | solution.py:107
  437.8 16.3 %reshape.294 = bf16[320,1,4096]{2,1,0:T(2,128)(2,1)} reshape(bf16[64,2,10240]{2,1,0:T(2,128)(2,1)} %all-to-all-done.4) | data formatting | bytes 5242880
  454.1 5.4 %copy.41 = bf16[1,320,4096]{2,1,0:T(8,128)(2,1)S(1)} copy(bf16[1,320,4096]{2,0,1:T(2,128)(2,1)} %bitcast.60) | data formatting | bytes 5242880
  462.6 4.4 reshape.283
  467.0 12.2 %fusion.4 = (bf16[128,4096]{1,0:T(8,128)(2,1)}, bf16[128,4096]{1,0:T(8,128)(2,1)}) fusion(bf16[128,2,4096]{2,1,0:T(2,128)(2,1)} %reshape.283, pred[128,2]{1,0:T(8,128)(4,1)S(1)} %copy.22, bf16[128,2,4096]{2,1,0:T(2,128)(2,1)} %reshape.279), kind=kLoop, calls=%fused_computation.18 | loop fusion | flops 3145728 | bytes 6291712 | tf_op jit(solution)/shard_map/reduce_sum | solution.py:19
  484.2 4.7 convolution_convert_fusion.3
  488.9 13.8 %reduce-scatter.3.cloned.1.call-done = bf16[128,1024]{1,0:T(8,128)(2,1)} async-done(((bf16[128,4096]{1,0:T(8,128)(2,1)}), bf16[128,1024]{1,0:T(8,128)(2,1)}) %reduce-scatter.3.cloned.1.call-update) | async-done | bytes 262160 | tf_op jit(solution)/shard_map/reduce_scatter | solution.py:117
  504.5 9.0 %psum.7 = f32[128,1]{0,1:T(1,128)} all-reduce(f32[128,1]{0,1:T(1,128)S(1)} %bitcast.65), channel_id=1, replica_groups=mesh['blk'=64,'mp'=4] {'mp'}, use_global_device_ids=true, to_apply=%region_7.9 | all-reduce | flops 128 | bytes 1024 | tf_op jit(solution)/shard_map/psum | solution.py:127
  513.5 18.2 %reduce-scatter.5.cloned.1.call-done = bf16[128,1024]{1,0:T(8,128)(2,1)} async-done(((bf16[128,4096]{1,0:T(8,128)(2,1)}), bf16[128,1024]{1,0:T(8,128)(2,1)}) %reduce-scatter.5.cloned.1.call-update) | async-done | bytes 262160 | tf_op jit(solution)/shard_map/reduce_scatter | solution.py:120
  (70 shorter events, 43.0 us)
Async XLA Ops:
  7.2 256.2 %copy-start = (bf16[192,4096]{1,0:T(8,128)(2,1)S(1)}, bf16[192,4096]{1,0:T(8,128)(2,1)}, u32[]{:S(2)}) copy-start(bf16[192,4096]{1,0:T(8,128)(2,1)} %param.14) | copy-start | bytes 4718596
  7.2 31.8 %all-gather.3.cloned.1.call-start = ((), (), s32[]{:S(2)}) async-start(), calls=%async_computation.7 | async-start | bytes 1310720 | tf_op jit(solution)/shard_map/all_gather | solution.py:54
  12.2 35.0 %all-to-all-start.2 = ((bf16[64,1,5]{2,1,0:T(2,128)(2,1)}), bf16[64,1,5]{2,1,0:T(2,128)(2,1)S(1)}, u32[]{:S(2)}, u32[]{:S(2)}) async-start(bf16[64,1,5]{2,1,0:T(2,128)(2,1)} %copy.27), calls=%async_computation.3 | async-start | bytes 65536 | tf_op jit(solution)/shard_map/all_to_all | solution.py:60
  47.3 104.8 %all-to-all-start = ((bf16[64,1,5,4096]{3,2,1,0:T(8,128)(2,1)}), bf16[64,1,5,4096]{3,2,1,0:T(8,128)(2,1)}, u32[]{:S(2)}, u32[]{:S(2)}) async-start(bf16[64,1,5,4096]{3,2,1,0:T(8,128)(2,1)} %bitcast.61), calls=%async_computation | async-start | bytes 8388608 | tf_op jit(solution)/shard_map/all_to_all | solution.py:58
  58.0 29.4 %all-gather.5.cloned.1.call-start = ((), (), s32[]{:S(2)}) async-start(), calls=%async_computation.9 | async-start | bytes 1310720 | tf_op jit(solution)/shard_map/all_gather | solution.py:55
  152.0 102.1 %all-to-all-start.3 = ((bf16[64,1,5,4096]{3,2,1,0:T(8,128)(2,1)}), bf16[64,1,5,4096]{3,2,1,0:T(8,128)(2,1)}, u32[]{:S(2)}, u32[]{:S(2)}) async-start(bf16[64,1,5,4096]{3,2,1,0:T(8,128)(2,1)} %bitcast.62), calls=%async_computation.4 | async-start | bytes 8388608 | tf_op jit(solution)/shard_map/all_to_all | solution.py:59
  160.4 4.9 copy-start.6
  168.9 90.5 %copy-start.5 = (bf16[192,4096]{1,0:T(8,128)(2,1)S(1)}, bf16[192,4096]{1,0:T(8,128)(2,1)}, u32[]{:S(2)}) copy-start(bf16[192,4096]{1,0:T(8,128)(2,1)} %param.15) | copy-start | bytes 4718596
  259.5 3.9 copy-start.2
  259.5 3.9 copy-start.12
  301.2 7.7 %copy-start.7 = (bf16[192,4096]{1,0:T(8,128)(2,1)S(1)}, bf16[192,4096]{1,0:T(8,128)(2,1)}, u32[]{:S(2)}) copy-start(bf16[192,4096]{1,0:T(8,128)(2,1)} %param.13) | copy-start | bytes 4718596
  301.2 68.4 %all-to-all-start.1 = ((bf16[64,2,10240]{2,1,0:T(2,128)(2,1)}), bf16[64,2,10240]{2,1,0:T(2,128)(2,1)}, u32[]{:S(2)}, u32[]{:S(2)}) async-start(bf16[64,2,10240]{2,1,0:T(2,128)(2,1)} %reshape.295), calls=%async_computation.1 | async-start | bytes 5242880 | tf_op jit(solution)/shard_map/all_to_all | solution.py:104
  342.9 34.6 %copy-start.10 = (s32[128,1]{0,1:T(1,128)S(1)}, s32[128,1]{0,1:T(1,128)}, u32[]{:S(2)}) copy-start(s32[128,1]{0,1:T(1,128)} %param.10) | copy-start | bytes 1540
  369.5 68.2 %all-to-all-start.4 = ((bf16[64,2,10240]{2,1,0:T(2,128)(2,1)}), bf16[64,2,10240]{2,1,0:T(2,128)(2,1)}, u32[]{:S(2)}, u32[]{:S(2)}) async-start(bf16[64,2,10240]{2,1,0:T(2,128)(2,1)} %reshape.293), calls=%async_computation.5 | async-start | bytes 5242880 | tf_op jit(solution)/shard_map/all_to_all | solution.py:107
  377.1 125.6 %reduce-scatter.3.cloned.1.call-start = ((), (), s32[]{:S(2)}) async-start(), calls=%async_computation.8 | async-start | bytes 1310720 | tf_op jit(solution)/shard_map/reduce_scatter | solution.py:117
  467.0 12.9 %copy-start.11 = (bf16[128,1]{0,1:T(2,128)(2,1)S(1)}, bf16[128,1]{0,1:T(2,128)(2,1)}, u32[]{:S(2)}) copy-start(bf16[128,1]{0,1:T(2,128)(2,1)} %param.11) | copy-start | bytes 772
  467.0 12.9 %copy-start.3 = (bf16[320,4096]{1,0:T(8,128)(2,1)S(1)}, bf16[320,4096]{1,0:T(8,128)(2,1)}, u32[]{:S(2)}) copy-start(bf16[320,4096]{1,0:T(8,128)(2,1)} %reshape.250) | copy-start | bytes 7864324
  467.0 12.9 %copy-start.9 = (bf16[320,192]{0,1:T(8,128)(2,1)S(1)}, bf16[320,192]{0,1:T(8,128)(2,1)}, u32[]{:S(2)}) copy-start(bf16[320,192]{0,1:T(8,128)(2,1)} %get-tuple-element.10) | copy-start | bytes 368644
  479.3 52.5 %reduce-scatter.5.cloned.1.call-start = ((), (), s32[]{:S(2)}) async-start(), calls=%async_computation.10 | async-start | bytes 1310720 | tf_op jit(solution)/shard_map/reduce_scatter | solution.py:120
  479.9 2.2 copy-start.4
  482.0 49.7 %copy-start.1 = (bf16[192,4096]{1,0:T(8,128)(2,1)S(1)}, bf16[192,4096]{1,0:T(8,128)(2,1)}, u32[]{:S(2)}) copy-start(bf16[192,4096]{1,0:T(8,128)(2,1)} %param.14) | copy-start | bytes 4718596
  484.2 18.5 %copy-start.8 = (bf16[128,1024]{1,0:T(8,128)(2,1)S(1)}, bf16[128,1024]{1,0:T(8,128)(2,1)}, u32[]{:S(2)}) copy-start(bf16[128,1024]{1,0:T(8,128)(2,1)} %param.12) | copy-start | bytes 786436
Sparse Core Ops, SparseCore 0:
  9.8 29.0 all-gather.2
  60.6 26.6 all-gather.4
  479.4 23.2 reduce-scatter.2
  505.9 25.8 reduce-scatter.4
where the time goes:
time: 546 us; the launch traced here: 538 us
  waiting for transfers between devices  276 us (51%)
  local copies, waits for them, and re-layouts  109 us (20%)
  other arithmetic  51.2 us (9%)
  starting transfers between devices  46.4 us (8%)
  matrix products  33 us (6%)
  between operations  14.2 us (3%)
  blocking collectives  9 us (2%)
    all_to_all x1, waiting for transfers between devices, body(): lax.all_to_all(grouped(grad_rows), 'blk', split_axis=0, concat_axis=2, ti...  85.2 us
    all_to_all x1, waiting for transfers between devices, body(): lax.all_to_all(grouped(features), 'blk', split_axis=0, concat_axis=2, til...  56.4 us
    unnamed x33, local copies, waits for them, and re-layouts  52.3 us
    unnamed x2, other arithmetic  34.4 us
    all_to_all x1, waiting for transfers between devices, body(): lax.all_to_all(part_dx.astype(jnp.bfloat16), 'blk', split_axis=1, concat_...  30.4 us
    all_gather x1, waiting for transfers between devices, body(): lax.all_gather(cotangent, 'mp', axis=1, tiled=True)  28.6 us
    all_to_all x1, waiting for transfers between devices, body(): lax.all_to_all(part_out.astype(jnp.bfloat16), 'blk', split_axis=1, concat...  26.6 us
    reduce_scatter x1, waiting for transfers between devices, body(): lax.psum_scatter(token_dx.astype(jnp.bfloat16), 'mp', scatter_dimension=1...  18.2 us
  transfers between devices with their start and end apart: 9, of which 8 were waited for; matrix products, arithmetic and copies ran while one was open for 19% of the time, Pallas kernels for 0%

commit v1 on v0

v1 whole, which is shorter than its diff:
```python
import functools

import jax
import jax.numpy as jnp
from jax import lax
from jax.experimental import pallas as pl
from jax.experimental.pallas import tpu as pltpu
from jax.sharding import Mesh, PartitionSpec as P

EXPERTS = 32
CAP = 5
LANES = 128
TILE = 16
F32 = jnp.float32
BF16 = jnp.bfloat16
VMEM_LIMIT = 48 * 1024 * 1024


def dot(a, b, contract=((1,), (0,))):
    return lax.dot_general(a, b, (contract, ((), ())), preferred_element_type=F32)


def kernel_call(body, out_shape, flops, moved, scalars=0):
    def call(*args):
        specs = [pl.BlockSpec(memory_space=pltpu.SMEM)] * scalars
        specs += [pl.BlockSpec(memory_space=pltpu.VMEM)] * (len(args) - scalars)
        return pl.pallas_call(
            body,
            out_shape=out_shape,
            in_specs=specs,
            out_specs=jax.tree.map(lambda _: pl.BlockSpec(memory_space=pltpu.VMEM), out_shape),
            compiler_params=pltpu.CompilerParams(vmem_limit_bytes=VMEM_LIMIT),
            cost_estimate=pl.CostEstimate(flops=flops, bytes_accessed=moved, transcendentals=0),
        )(*args)

    return call


def exchange_matrix():
    n = TILE * TILE
    out_row = lax.broadcasted_iota(jnp.int32, (n, n), 0)
    in_row = lax.broadcasted_iota(jnp.int32, (n, n), 1)
    return (in_row == (out_row % TILE) * TILE + out_row // TILE).astype(BF16)


def pack_rows(left, right, packed_ref):
    swap = exchange_matrix()
    for group in range(packed_ref.shape[0] // (TILE * TILE)):
        parts = [side(group * TILE, j * LANES) for side in (left, right) for j in range(8)]
        rows = dot(swap, jnp.concatenate(parts, axis=0)).astype(BF16)
        packed_ref[pl.ds(group * TILE * TILE, TILE * TILE), :] = rows


def unpack_rows(packed_ref, left_ref, right_ref):
    swap = exchange_matrix()
    for group in range(packed_ref.shape[0] // (TILE * TILE)):
        rows = dot(swap, packed_ref[pl.ds(group * TILE * TILE, TILE * TILE), :]).astype(BF16)
        for at, side in enumerate((left_ref, right_ref)):
            for j in range(8):
                q = at * 8 + j
                side[pl.ds(group * TILE, TILE), pl.ds(j * LANES, LANES)] = rows[
                    q * TILE : (q + 1) * TILE
                ]


def token_slots(ids_row):
    tokens = ids_row.shape[1]
    expert = lax.broadcasted_iota(jnp.int32, (EXPERTS, tokens), 0)
    onehot = (expert == ids_row).astype(F32)
    before = lax.broadcasted_iota(jnp.int32, (tokens, tokens), 0)
    token = lax.broadcasted_iota(jnp.int32, (tokens, tokens), 1)
    earlier = (before < token).astype(BF16)
    counts = dot(onehot.astype(BF16), earlier)
    rank = jnp.sum(counts * onehot, axis=0, keepdims=True)
    return ids_row * CAP + rank.astype(jnp.int32)


def placement(ids_row):
    tokens = ids_row.shape[1]
    slot = lax.broadcasted_iota(jnp.int32, (EXPERTS * CAP, tokens), 0)
    return (slot == token_slots(ids_row)).astype(BF16)


def send_kernel(ids_ref, probs_ref, hidden_ref, cotangent_ref, packed_ref, placed_x, placed_s):
    select = placement(ids_ref[...])
    placed_x[...] = dot(select, hidden_ref[...]).astype(BF16)
    scaled = (probs_ref[...].astype(F32) * cotangent_ref[...].astype(F32)).astype(BF16)
    placed_s[...] = dot(select, scaled).astype(BF16)

    def side(ref):
        return lambda row, column: ref[pl.ds(row, TILE), pl.ds(column, LANES)]

    pack_rows(side(placed_x), side(placed_s), packed_ref)


def send(ids_row, probs, hidden, cotangent):
    slots = EXPERTS * CAP
    width = hidden.shape[1]
    return pl.pallas_call(
        send_kernel,
        out_shape=jax.ShapeDtypeStruct((slots * TILE, LANES), BF16),
        scratch_shapes=[pltpu.VMEM((slots, width), BF16), pltpu.VMEM((slots, width), BF16)],
        compiler_params=pltpu.CompilerParams(vmem_limit_bytes=VMEM_LIMIT),
    )(ids_row, probs, hidden, cotangent)


def unpack_kernel(packed_ref, x_ref, s_ref):
    unpack_rows(packed_ref, x_ref, s_ref)


def unpack(packed):
    slots = packed.shape[0] // TILE
    out = jax.ShapeDtypeStruct((slots, 8 * LANES), BF16)
    return kernel_call(unpack_kernel, (out, out), 2 * slots * TILE * 256 * LANES, 4 * slots * 1024 * 4)(packed)


def columns(ref, mp, step, parts):
    width = ref.shape[1] // parts
    start = pl.multiple_of(lax.rem(mp + step, parts) * width, width)
    return pl.ds(start, width)


def both(own, other):
    return jnp.concatenate([own[...], other[...]], axis=0)


def forward_kernel(parts, mp_ref, *refs):
    own, other = refs[:parts], refs[parts : 2 * parts]
    wg, wu, wd = refs[2 * parts : 2 * parts + 3]
    gate_ref, up_ref, gated_ref = refs[2 * parts + 3 : 2 * parts + 6]
    out_own, out_other = refs[2 * parts + 6 : 3 * parts + 6], refs[3 * parts + 6 :]
    mp = mp_ref[0]
    half = own[0].shape[0]
    gate = jnp.zeros((2 * half, wg.shape[0]), F32)
    up = jnp.zeros((2 * half, wg.shape[0]), F32)
    for step in range(parts):
        at = columns(wg, mp, step, parts)
        x = both(own[step], other[step])
        gate = gate + dot(x, wg[:, at], ((1,), (1,)))
        up = up + dot(x, wu[:, at], ((1,), (1,)))
    gate_ref[...] = gate
    up_ref[...] = up
    gated = (gate * (1.0 / (1.0 + jnp.exp(-gate))) * up).astype(BF16)
    gated_ref[...] = gated
    for step in range(parts):
        out = dot(gated, wd[:, columns(wd, mp, step, parts)]).astype(BF16)
        out_own[step][...] = out[:half]
        out_other[step][...] = out[half:]


def backward_kernel(parts, mp_ref, *refs):
    own, other = refs[:parts], refs[parts : 2 * parts]
    wg, wu, wd, gate_ref, up_ref = refs[2 * parts : 2 * parts + 5]
    ggp_ref, gup_ref = refs[2 * parts + 5 : 2 * parts + 7]
    dx_own, dx_other = refs[2 * parts + 7 : 3 * parts + 7], refs[3 * parts + 7 :]
    mp = mp_ref[0]
    half = own[0].shape[0]
    grad = jnp.zeros(gate_ref.shape, F32)
    for step in range(parts):
        at = columns(wd, mp, step, parts)
        grad = grad + dot(both(own[step], other[step]), wd[:, at], ((1,), (1,)))
    gate = gate_ref[...]
    sigmoid = 1.0 / (1.0 + jnp.exp(-gate))
    ggp = (grad * up_ref[...] * sigmoid * (1.0 + gate * (1.0 - sigmoid))).astype(BF16)
    gup = (grad * (gate * sigmoid)).astype(BF16)
    ggp_ref[...] = ggp
    gup_ref[...] = gup
    for step in range(parts):
        at = columns(wg, mp, step, parts)
        dx = (dot(ggp, wg[:, at]) + dot(gup, wu[:, at])).astype(BF16)
        dx_own[step][...] = dx[:half]
        dx_other[step][...] = dx[half:]


def weights_kernel(parts, mp_ref, *refs):
    x_own, x_other = refs[:parts], refs[parts : 2 * parts]
    s_own, s_other = refs[2 * parts : 3 * parts], refs[3 * parts : 4 * parts]
    ggp_ref, gup_ref, gated_ref, gwg, gwu, gwd = refs[4 * parts :]
    mp = mp_ref[0]
    rows = ((0,), (0,))
    for step in range(parts):
        at = columns(gwg, mp, step, parts)
        x = both(x_own[step], x_other[step])
        gwg[:, at] = dot(ggp_ref[...], x, rows).astype(BF16)
        gwu[:, at] = dot(gup_ref[...], x, rows).astype(BF16)
        gwd[:, at] = dot(gated_ref[...], both(s_own[step], s_other[step]), rows).astype(BF16)


def return_kernel(parts, *refs):
    out, dx, packed_ref, sum_out, sum_dx = refs[:parts], refs[parts : 2 * parts], *refs[2 * parts :]
    for terms, total in ((out, sum_out), (dx, sum_dx)):
        value = terms[0][...].astype(F32)
        for term in terms[1:]:
            value = value + term[...].astype(F32)
        total[...] = value.astype(BF16)

    def side(ref):
        return lambda row, column: ref[pl.ds(row, TILE), pl.ds(column, LANES)]

    pack_rows(side(sum_out), side(sum_dx), packed_ref)


def pack_return(out, dx):
    slots, width = out[0].shape
    return pl.pallas_call(
        functools.partial(return_kernel, len(out)),
        out_shape=jax.ShapeDtypeStruct((slots * TILE, LANES), BF16),
        scratch_shapes=[pltpu.VMEM((slots, width), BF16), pltpu.VMEM((slots, width), BF16)],
        compiler_params=pltpu.CompilerParams(vmem_limit_bytes=VMEM_LIMIT),
    )(*out, *dx)


def home_kernel(ids_ref, probs_ref, cotangent_ref, packed_ref, mixed_ref, hidden_ref, terms_ref, out_ref, dx_ref):
    select = placement(ids_ref[...])
    unpack_rows(packed_ref, out_ref, dx_ref)
    rows = ((0,), (0,))
    out = dot(select, out_ref[...], rows)
    mixed_ref[...] = (probs_ref[...].astype(F32) * out).astype(BF16)
    hidden_ref[...] = dot(select, dx_ref[...], rows).astype(BF16)
    terms_ref[...] = jnp.sum(cotangent_ref[...].astype(F32) * out, axis=1, keepdims=True)


def home(ids_row, probs, cotangent, packed):
    slots = EXPERTS * CAP
    tokens, width = cotangent.shape
    wide = jax.ShapeDtypeStruct((tokens, width), BF16)
    return pl.pallas_call(
        home_kernel,
        out_shape=(wide, wide, jax.ShapeDtypeStruct((tokens, 1), F32)),
        scratch_shapes=[pltpu.VMEM((slots, width), BF16), pltpu.VMEM((slots, width), BF16)],
        compiler_params=pltpu.CompilerParams(vmem_limit_bytes=VMEM_LIMIT),
    )(ids_row, probs, cotangent, packed)


def shift(value, axis, step):
    count = lax.axis_size(axis)
    return lax.ppermute(value, axis, [(i, (i + step) % count) for i in range(count)])


def over_yz(packed):
    parts = lax.axis_size("y") * lax.axis_size("z")
    split = packed.reshape(parts, packed.shape[0] // parts, packed.shape[1])
    return lax.all_to_all(split, ("y", "z"), 0, 0, tiled=True).reshape(packed.shape)


def body(hidden_states, expert_ids, probs, cotangent, w_gate, w_up, w_down):
    parts = lax.axis_size("mp")
    mp = lax.axis_index("mp").astype(jnp.int32).reshape(1)
    tokens = hidden_states.shape[0]
    hidden_rows, model_width = w_gate.shape
    ids_row = expert_ids.reshape(1, tokens)
    packed = over_yz(send(ids_row, probs, hidden_states, cotangent))
    x, s = unpack(packed)

    def gathered(own):
        held = [None] * parts
        held[0] = own
        for step in (1, 3, 2):
            held[step] = shift(own, "mp", -step)
        return held, [shift(part, "core", 1) for part in held]

    x_own, x_other = gathered(x)
    s_own, s_other = gathered(s)
    slots, width = x.shape
    pair = 2 * slots
    act = jax.ShapeDtypeStruct((pair, hidden_rows), F32)
    act16 = jax.ShapeDtypeStruct((pair, hidden_rows), BF16)
    part = jax.ShapeDtypeStruct((slots, width), BF16)
    weight = jax.ShapeDtypeStruct(w_gate.shape, BF16)
    product = 2 * pair * hidden_rows * model_width
    moved = 2 * hidden_rows * model_width
    gate, up, gated, *out = kernel_call(
        functools.partial(forward_kernel, parts), (act, act, act16) + (part,) * (2 * parts), 3 * product, 6 * moved, 1
    )(mp, *x_own, *x_other, w_gate, w_up, w_down)
    ggp, gup, *dx = kernel_call(
        functools.partial(backward_kernel, parts), (act16, act16) + (part,) * (2 * parts), 3 * product, 6 * moved, 1
    )(mp, *s_own, *s_other, w_gate, w_up, w_down, gate, up)
    grads = kernel_call(
        functools.partial(weights_kernel, parts), (weight, weight, weight), 3 * product, 6 * moved, 1
    )(mp, *x_own, *x_other, *s_own, *s_other, ggp, gup, gated)

    def summed(terms):
        mine, others = terms[:parts], terms[parts:]
        total = []
        for step in range(parts):
            came = shift(others[step], "core", 1)
            total.append((mine[step].astype(F32) + came.astype(F32)).astype(BF16))
        return [total[0]] + [shift(total[step], "mp", step) for step in range(1, parts)]

    back = over_yz(pack_return(summed(out), summed(dx)))
    mixed, grad_hidden, terms = home(ids_row, probs, cotangent, back)
    grad_probs = lax.psum(terms, "mp")
    return (mixed, grad_hidden, grad_probs, *grads)


def solution(mesh):
    yz_core = mesh.devices.shape[0]
    cores = 2
    columns_count = EXPERTS
    rows_y = 4
    grid = Mesh(
        mesh.devices.reshape(rows_y, yz_core // (cores * rows_y), cores, mesh.devices.shape[1]),
        ("y", "z", "core", "mp"),
    )
    assert yz_core == columns_count * cores
    blk = ("y", "z", "core")
    wide, thin, weight = P(blk, "mp"), P(blk, None), P(blk + ("mp",), None)
    return jax.shard_map(
        body,
        mesh=grid,
        in_specs=(wide, thin, thin, wide, weight, weight, weight),
        out_specs=(wide, wide, thin, weight, weight, weight),
        check_vma=False,
    )
```

time: 546 us -> 172 us (0.32); the launches traced: 538 us -> 171 us
  waiting for transfers between devices: 276 us -> 51.3 us
  local copies, waits for them, and re-layouts: 109 us -> 18.8 us
  other arithmetic: 51.2 us -> 0.77 us
  blocking collectives: 9 us -> 49.2 us
  matrix products: 33 us -> 0 us
  Pallas kernels: 0 us -> 21.2 us
  starting transfers between devices: 46.4 us -> 28.9 us
  between operations: 14.2 us -> 0.92 us
    all_to_all x5 -> x1, waiting for transfers between devices: 199 us -> 6.4 us  [over_yz(): lax.all_to_all(split, ('y', 'z'), 0, 0, tiled=True).reshape(packed.shape)]
    ppermute x0 -> x28, waiting for transfers between devices: none -> 44.9 us  [shift(): lax.ppermute(value, axis, [(i, (i + step) % count) for i in range(count)])]
    all_gather x2 -> x0, waiting for transfers between devices: 43.6 us -> none  [the longest x1 28.6 us: body(): lax.all_gather(cotangent, 'mp', axis=1, tiled=True)]
    all_to_all x5 -> x1, starting transfers between devices: 45.8 us -> 6.85 us  [over_yz(): lax.all_to_all(split, ('y', 'z'), 0, 0, tiled=True).reshape(packed.shape)]
    unnamed x2 -> x0, other arithmetic: 34.4 us -> none
    unnamed x33 -> x56, local copies, waits for them, and re-layouts: 52.3 us -> 18.8 us
    dot_general x12 -> x0, matrix products: 33 us -> none  [the longest x2 7.25 us: grouped(): jnp.dot(select, per_pair, preferred_element_type=jnp.float32)]
    reduce_scatter x2 -> x0, waiting for transfers between devices: 32 us -> none  [the longest x1 18.2 us: body(): lax.psum_scatter(token_dx.astype(jnp.bfloat16), 'mp', scatter_dimension=1...]
  transfers between devices with their start and end apart: 9 -> 29, of which waited for: 8 -> 12; matrix products, arithmetic and copies ran while one was open for 19% -> 0% of each run, Pallas kernels for 0% -> 10%
where the time goes in v1:
time: 172 us; the launch traced here: 171 us
  waiting for transfers between devices  51.3 us (30%)
  blocking collectives  49.2 us (29%)
  starting transfers between devices  28.9 us (17%)
  Pallas kernels  21.2 us (12%)
  local copies, waits for them, and re-layouts  18.8 us (11%)
    ppermute x28, waiting for transfers between devices, shift(): lax.ppermute(value, axis, [(i, (i + step) % count) for i in range(count)])  44.9 us
    all_to_all x1, blocking collectives, over_yz(): lax.all_to_all(split, ('y', 'z'), 0, 0, tiled=True).reshape(packed.shape)  31.4 us
    ppermute x28, starting transfers between devices, shift(): lax.ppermute(value, axis, [(i, (i + step) % count) for i in range(count)])  22.1 us
    unnamed x56, local copies, waits for them, and re-layouts  18.8 us
    psum x1, blocking collectives, body(): grad_probs = lax.psum(terms, 'mp')  17.8 us
    pallas_call x4, Pallas kernels, call(): pl.pallas_call(body, out_shape=out_shape, in_specs=specs, out_specs=jax.t...  17.1 us
    all_to_all x1, starting transfers between devices, over_yz(): lax.all_to_all(split, ('y', 'z'), 0, 0, tiled=True).reshape(packed.shape)  6.85 us
    all_to_all x1, waiting for transfers between devices, over_yz(): lax.all_to_all(split, ('y', 'z'), 0, 0, tiled=True).reshape(packed.shape)  6.4 us
  transfers between devices with their start and end apart: 29, of which 12 were waited for; matrix products, arithmetic and copies ran while one was open for 0% of the time, Pallas kernels for 10%

profile of v1, /device:TPU:32, one launch (start us, length us, event | category | flops | bytes accessed | tf_op | source)
XLA Modules:
  0.0 171.1 jit_solution(10109257871053443533)
XLA Ops:
  1.4 1.0 copy-done.13
  2.4 0.9 copy-done.18
  4.9 31.4 %all_to_all.10 = bf16[32,80,128]{2,1,0:T(8,128)(2,1)S(1)} all-to-all(bf16[32,80,128]{2,1,0:T(8,128)(2,1)S(1)} %bitcast.8), channel_id=1, replica_groups=mesh['y'=4,'z'=8,'core'=2,'mp'=4] {'y','z'}, dimensions={0} | all-to-all | bytes 1310720 | tf_op jit(solution)/shard_map/all_to_all | solution.py:243
  36.8 2.8 %collective-permute-start = (bf16[160,1024]{1,0:T(8,128)(2,1)S(1)}, bf16[160,1024]{1,0:T(8,128)(2,1)S(1)}, u32[]{:S(2)}, u32[]{:S(2)}) collective-permute-start(bf16[160,1024]{1,0:T(8,128)(2,1)S(1)} %get-tuple-element.35.refs_0_), channel_id=1, source_target_pairs={{0,3},{1,0},{2,1},{3,2},{4,7},{5,4},{6,5},{7,6},{8,11},{9,8},{10,9... | collective-permute-start | bytes 983048 | tf_op jit(solution)/shard_map/ppermute | solution.py:237
  41.4 2.3 %collective-permute-start.14 = (bf16[160,1024]{1,0:T(8,128)(2,1)S(1)}, bf16[160,1024]{1,0:T(8,128)(2,1)S(1)}, u32[]{:S(2)}, u32[]{:S(2)}) collective-permute-start(bf16[160,1024]{1,0:T(8,128)(2,1)S(1)} %get-tuple-element.44.refs_0_.refs_8_), channel_id=1, source_target_pairs={{0,3},{1,0},{2,1},{3,2},{4,7},{5,4},{6,5},{7,6},{8,11},{9,8},{10,9... | collective-permute-start | bytes 983048 | tf_op jit(solution)/shard_map/ppermute | solution.py:237
  43.7 9.6 %collective-permute-done.refs_1_ = bf16[160,1024]{1,0:T(8,128)(2,1)S(1)} collective-permute-done((bf16[160,1024]{1,0:T(8,128)(2,1)S(1)}, bf16[160,1024]{1,0:T(8,128)(2,1)S(1)}, u32[]{:S(2)}, u32[]{:S(2)}) %collective-permute-start) | collective-permute-done | bytes 327712 | tf_op jit(solution)/shard_map/ppermute | solution.py:237
  53.3 5.1 %collective-permute-start.16 = (bf16[160,1024]{1,0:T(8,128)(2,1)S(1)}, bf16[160,1024]{1,0:T(8,128)(2,1)S(1)}, u32[]{:S(2)}, u32[]{:S(2)}) collective-permute-start(bf16[160,1024]{1,0:T(8,128)(2,1)S(1)} %get-tuple-element.44.refs_0_.refs_8_), channel_id=1, source_target_pairs={{0,1},{1,2},{2,3},{3,0},{4,5},{5,6},{6,7},{7,4},{8,9},{9,10},{10,1... | collective-permute-start | bytes 983048 | tf_op jit(solution)/shard_map/ppermute | solution.py:237
  58.4 1.2 collective-permute-done.2.refs_3_
  61.5 3.9 %collective-permute-done.14.refs_1_.refs_9_ = bf16[160,1024]{1,0:T(8,128)(2,1)S(1)} collective-permute-done((bf16[160,1024]{1,0:T(8,128)(2,1)S(1)}, bf16[160,1024]{1,0:T(8,128)(2,1)S(1)}, u32[]{:S(2)}, u32[]{:S(2)}) %collective-permute-start.14) | collective-permute-done | bytes 327712 | tf_op jit(solution)/shard_map/ppermute | solution.py:237
  65.9 3.2 %collective-permute-done.16.refs_3_.refs_11_ = bf16[160,1024]{1,0:T(8,128)(2,1)S(1)} collective-permute-done((bf16[160,1024]{1,0:T(8,128)(2,1)S(1)}, bf16[160,1024]{1,0:T(8,128)(2,1)S(1)}, u32[]{:S(2)}, u32[]{:S(2)}) %collective-permute-start.16) | collective-permute-done | bytes 327712 | tf_op jit(solution)/shard_map/ppermute | solution.py:237
  70.4 1.0 copy-done.5
  71.3 1.0 copy-done.8
  72.3 1.0 copy-done.11
  73.3 4.9 %shard_map.120 = (f32[320,192]{1,0:T(8,128)S(1)}, f32[320,192]{1,0:T(8,128)S(1)}, bf16[320,192]{1,0:T(8,128)(2,1)S(1)}, bf16[160,1024]{1,0:T(8,128)(2,1)S(1)}, b...) custom-call(s32[1]{0:T(128)} %bitcast.1.mp_ref, ...), custom_call_target="tpu_custom_call" | custom-call | flops 1509949440 | bytes 9437184 | tf_op jit(solution)/shard_map/pallas_call | solution.py:27
  80.7 6.1 %shard_map.121 = (bf16[320,192]{1,0:T(8,128)(2,1)S(1)}, bf16[320,192]{1,0:T(8,128)(2,1)S(1)}, bf16[160,1024]{1,0:T(8,128)(2,1)S(1)}, bf16[160,1024]{1,0:T(8,128)...) custom-call(s32[1]{0:T(128)} %bitcast.1.mp_ref, ...), custom_call_target="tpu_custom_call" | custom-call | flops 1509949440 | bytes 9437184 | tf_op jit(solution)/shard_map/pallas_call | solution.py:27
  89.5 2.2 %collective-permute-start.11 = (bf16[160,1024]{1,0:T(8,128)(2,1)S(1)}, bf16[160,1024]{1,0:T(8,128)(2,1)S(1)}, u32[]{:S(2)}, u32[]{:S(2)}) collective-permute-start(bf16[160,1024]{1,0:T(8,128)(2,1)S(1)} %add_convert_fusion.5), channel_id=1, source_target_pairs={{0,2},{1,3},{2,0},{3,1},{4,6},{5,7},{6,4},{7,5},{8,10},{9,11},{10,... | collective-permute-start | bytes 983048 | tf_op jit(solution)/shard_map/ppermute | solution.py:237
  91.8 1.1 collective-permute-start.13
  93.0 1.3 collective-permute-start.23
  94.3 1.8 %collective-permute-start.25 = (bf16[160,1024]{1,0:T(8,128)(2,1)S(1)}, bf16[160,1024]{1,0:T(8,128)(2,1)S(1)}, u32[]{:S(2)}, u32[]{:S(2)}) collective-permute-start(bf16[160,1024]{1,0:T(8,128)(2,1)S(1)} %add_convert_fusion.1), channel_id=1, source_target_pairs={{0,2},{1,3},{2,0},{3,1},{4,6},{5,7},{6,4},{7,5},{8,10},{9,11},{10,... | collective-permute-start | bytes 983048 | tf_op jit(solution)/shard_map/ppermute | solution.py:237
  96.2 11.7 %collective-permute-done.9.refs_1_ = bf16[160,1024]{1,0:T(8,128)(2,1)S(1)} collective-permute-done((bf16[160,1024]{1,0:T(8,128)(2,1)S(1)}, bf16[160,1024]{1,0:T(8,128)(2,1)S(1)}, u32[]{:S(2)}, u32[]{:S(2)}) %collective-permute-start.9) | collective-permute-done | bytes 327712 | tf_op jit(solution)/shard_map/ppermute | solution.py:237
  109.0 12.3 %collective-permute-done.23.refs_5_ = bf16[160,1024]{1,0:T(8,128)(2,1)S(1)} collective-permute-done((bf16[160,1024]{1,0:T(8,128)(2,1)S(1)}, bf16[160,1024]{1,0:T(8,128)(2,1)S(1)}, u32[]{:S(2)}, u32[]{:S(2)}) %collective-permute-start.23) | collective-permute-done | bytes 327712 | tf_op jit(solution)/shard_map/ppermute | solution.py:237
  122.2 1.6 shard_map.122
  123.8 6.9 %all-to-all-start.1 = ((bf16[32,80,128]{2,1,0:T(8,128)(2,1)}), bf16[32,80,128]{2,1,0:T(8,128)(2,1)S(1)}, u32[]{:S(2)}, u32[]{:S(2)}) async-start(bf16[32,80,128]{2,1,0:T(8,128)(2,1)} %bitcast.4), calls=%async_computation.1 | async-start | bytes 1310720 | tf_op jit(solution)/shard_map/all_to_all | solution.py:243
  130.7 1.0 copy-done.1
  131.7 1.0 copy-done.3
  132.6 1.0 copy-done.6
  133.6 1.0 copy-done.9
  134.6 1.0 copy-done.12
  138.3 5.7 %shard_map.124 = (bf16[192,4096]{1,0:T(8,128)(2,1)}, bf16[192,4096]{1,0:T(8,128)(2,1)}, bf16[192,4096]{1,0:T(8,128)(2,1)}) custom-call(s32[1]{0:T(128)} %bitcast.1.mp_ref, bf16[160,1024]{1,0:T(8,128)(2,1)S(1)} %copy-done.1, bf16[160,1024]{1,0:T(8,128)(2,1)S(1)} %copy-done.3, bf16[160,1024]{1,0:T(8,128)(2,1)S(1)} %copy-done.6, ...), custom_call_target="tpu_custom_call" | custom-call | flops 1509949440 | bytes 9437184 | tf_op jit(solution)/shard_map/pallas_call | solution.py:27
  144.0 6.4 %all-to-all-done.1 = bf16[32,80,128]{2,1,0:T(8,128)(2,1)S(1)} async-done(((bf16[32,80,128]{2,1,0:T(8,128)(2,1)}), bf16[32,80,128]{2,1,0:T(8,128)(2,1)S(1)}, u32[]{:S(2)}, u32[]{:S(2)}) %all-to-all-start.1) | async-done | bytes 655392 | tf_op jit(solution)/shard_map/all_to_all | solution.py:243
  151.2 1.5 shard_map.123
  152.7 17.8 %psum.7 = f32[128,1]{1,0:T(8,128)S(1)} all-reduce(f32[128,1]{1,0:T(8,128)S(1)} %get-tuple-element.57), channel_id=1, replica_groups=mesh['y'=4,'z'=8,'core'=2,'mp'=4] {'mp'}, use_global_device_ids=true, to_apply=%region_0.0 | all-reduce | flops 128 | bytes 1024 | tf_op jit(solution)/shard_map/psum | solution.py:292
  (99 shorter events, 19.8 us)
Async XLA Ops:
  1.4 34.9 %copy-start.16 = (bf16[128,1]{1,0:T(8,128)(2,1)}, bf16[128,1]{1,0:T(8,128)(2,1)S(1)}, u32[]{:S(2)}) copy-start(bf16[128,1]{1,0:T(8,128)(2,1)S(1)} %copy.14.probs_ref) | copy-start | bytes 772
  36.8 41.3 %copy-start = (bf16[160,1024]{1,0:T(8,128)(2,1)}, bf16[160,1024]{1,0:T(8,128)(2,1)S(1)}, u32[]{:S(2)}) copy-start(bf16[160,1024]{1,0:T(8,128)(2,1)S(1)} %get-tuple-element.35.refs_0_) | copy-start | bytes 983044
  36.8 16.4 %collective-permute-start = (bf16[160,1024]{1,0:T(8,128)(2,1)S(1)}, bf16[160,1024]{1,0:T(8,128)(2,1)S(1)}, u32[]{:S(2)}, u32[]{:S(2)}) collective-permute-start(bf16[160,1024]{1,0:T(8,128)(2,1)S(1)} %get-tuple-element.35.refs_0_), channel_id=1, source_target_pairs={{0,3},{1,0},{2,1},{3,2},{4,7},{5,4},{6,5},{7,6},{8,11},{9,8},{10,9... | collective-permute-start | bytes 983048 | tf_op jit(solution)/shard_map/ppermute | solution.py:237
  39.7 13.6 %collective-permute-start.1 = (bf16[160,1024]{1,0:T(8,128)(2,1)S(1)}, bf16[160,1024]{1,0:T(8,128)(2,1)S(1)}, u32[]{:S(2)}, u32[]{:S(2)}) collective-permute-start(bf16[160,1024]{1,0:T(8,128)(2,1)S(1)} %get-tuple-element.35.refs_0_), channel_id=1, source_target_pairs={{0,2},{1,3},{2,0},{3,1},{4,6},{5,7},{6,4},{7,5},{8,10},{9,11},{10,... | collective-permute-start | bytes 983048 | tf_op jit(solution)/shard_map/ppermute | solution.py:237
  40.5 19.0 %collective-permute-start.2 = (bf16[160,1024]{1,0:T(8,128)(2,1)S(1)}, bf16[160,1024]{1,0:T(8,128)(2,1)}, u32[]{:S(2)}, u32[]{:S(2)}) collective-permute-start(bf16[160,1024]{1,0:T(8,128)(2,1)S(1)} %get-tuple-element.35.refs_0_), channel_id=1, source_target_pairs={{0,1},{1,2},{2,3},{3,0},{4,5},{5,6},{6,7},{7,4},{8,9},{9,10},{10,1... | collective-permute-start | bytes 983048 | tf_op jit(solution)/shard_map/ppermute | solution.py:237
  41.4 18.2 %collective-permute-start.3 = (bf16[160,1024]{1,0:T(8,128)(2,1)S(1)}, bf16[160,1024]{1,0:T(8,128)(2,1)S(1)}, u32[]{:S(2)}, u32[]{:S(2)}) collective-permute-start(bf16[160,1024]{1,0:T(8,128)(2,1)S(1)} %get-tuple-element.35.refs_0_), channel_id=1, source_target_pairs={{0,4},{4,0},{1,5},{5,1},{2,6},{6,2},{3,7},{7,3},{8,12},{12,8},{9,1... | collective-permute-start | bytes 983048 | tf_op jit(solution)/shard_map/ppermute | solution.py:237
  41.4 24.0 %collective-permute-start.14 = (bf16[160,1024]{1,0:T(8,128)(2,1)S(1)}, bf16[160,1024]{1,0:T(8,128)(2,1)S(1)}, u32[]{:S(2)}, u32[]{:S(2)}) collective-permute-start(bf16[160,1024]{1,0:T(8,128)(2,1)S(1)} %get-tuple-element.44.refs_0_.refs_8_), channel_id=1, source_target_pairs={{0,3},{1,0},{2,1},{3,2},{4,7},{5,4},{6,5},{7,6},{8,11},{9,8},{10,9... | collective-permute-start | bytes 983048 | tf_op jit(solution)/shard_map/ppermute | solution.py:237
  53.3 24.9 %copy-start.2 = (bf16[160,1024]{1,0:T(8,128)(2,1)}, bf16[160,1024]{1,0:T(8,128)(2,1)S(1)}, u32[]{:S(2)}) copy-start(bf16[160,1024]{1,0:T(8,128)(2,1)S(1)} %collective-permute-done.refs_1_) | copy-start | bytes 983044
  53.3 12.4 %collective-permute-start.15 = (bf16[160,1024]{1,0:T(8,128)(2,1)S(1)}, bf16[160,1024]{1,0:T(8,128)(2,1)S(1)}, u32[]{:S(2)}, u32[]{:S(2)}) collective-permute-start(bf16[160,1024]{1,0:T(8,128)(2,1)S(1)} %get-tuple-element.44.refs_0_.refs_8_), channel_id=1, source_target_pairs={{0,2},{1,3},{2,0},{3,1},{4,6},{5,7},{6,4},{7,5},{8,10},{9,11},{10,... | collective-permute-start | bytes 983048 | tf_op jit(solution)/shard_map/ppermute | solution.py:237
  53.3 15.8 %collective-permute-start.16 = (bf16[160,1024]{1,0:T(8,128)(2,1)S(1)}, bf16[160,1024]{1,0:T(8,128)(2,1)S(1)}, u32[]{:S(2)}, u32[]{:S(2)}) collective-permute-start(bf16[160,1024]{1,0:T(8,128)(2,1)S(1)} %get-tuple-element.44.refs_0_.refs_8_), channel_id=1, source_target_pairs={{0,1},{1,2},{2,3},{3,0},{4,5},{5,6},{6,7},{7,4},{8,9},{9,10},{10,1... | collective-permute-start | bytes 983048 | tf_op jit(solution)/shard_map/ppermute | solution.py:237
  59.5 9.6 %collective-permute-start.4 = (bf16[160,1024]{1,0:T(8,128)(2,1)S(1)}, bf16[160,1024]{1,0:T(8,128)(2,1)S(1)}, u32[]{:S(2)}, u32[]{:S(2)}) collective-permute-start(bf16[160,1024]{1,0:T(8,128)(2,1)S(1)} %collective-permute-done.refs_1_), channel_id=1, source_target_pairs={{0,4},{4,0},{1,5},{5,1},{2,6},{6,2},{3,7},{7,3},{8,12},{12,8},{9,1... | collective-permute-start | bytes 983048 | tf_op jit(solution)/shard_map/ppermute | solution.py:237
  60.3 10.1 %collective-permute-start.5 = (bf16[160,1024]{1,0:T(8,128)(2,1)S(1)}, bf16[160,1024]{1,0:T(8,128)(2,1)}, u32[]{:S(2)}, u32[]{:S(2)}) collective-permute-start(bf16[160,1024]{1,0:T(8,128)(2,1)S(1)} %collective-permute-done.1.refs_2_), channel_id=1, source_target_pairs={{0,4},{4,0},{1,5},{5,1},{2,6},{6,2},{3,7},{7,3},{8,12},{12,8},{9,1... | collective-permute-start | bytes 983048 | tf_op jit(solution)/shard_map/ppermute | solution.py:237
  65.4 5.0 %collective-permute-start.6 = (bf16[160,1024]{1,0:T(8,128)(2,1)}, bf16[160,1024]{1,0:T(8,128)(2,1)}, u32[]{:S(2)}, u32[]{:S(2)}) collective-permute-start(bf16[160,1024]{1,0:T(8,128)(2,1)} %collective-permute-done.2.refs_3_), channel_id=1, source_target_pairs={{0,4},{4,0},{1,5},{5,1},{2,6},{6,2},{3,7},{7,3},{8,12},{12,8},{9,1... | collective-permute-start | bytes 983048 | tf_op jit(solution)/shard_map/ppermute | solution.py:237
  65.7 14.4 %collective-permute-start.17 = (bf16[160,1024]{1,0:T(8,128)(2,1)S(1)}, bf16[160,1024]{1,0:T(8,128)(2,1)S(1)}, u32[]{:S(2)}, u32[]{:S(2)}) collective-permute-start(bf16[160,1024]{1,0:T(8,128)(2,1)S(1)} %get-tuple-element.44.refs_0_.refs_8_), channel_id=1, source_target_pairs={{0,4},{4,0},{1,5},{5,1},{2,6},{6,2},{3,7},{7,3},{8,12},{12,8},{9,1... | collective-permute-start | bytes 983048 | tf_op jit(solution)/shard_map/ppermute | solution.py:237
  69.1 11.0 %collective-permute-start.18 = (bf16[160,1024]{1,0:T(8,128)(2,1)S(1)}, bf16[160,1024]{1,0:T(8,128)(2,1)S(1)}, u32[]{:S(2)}, u32[]{:S(2)}) collective-permute-start(bf16[160,1024]{1,0:T(8,128)(2,1)S(1)} %collective-permute-done.14.refs_1_.refs_9_), channel_id=1, source_target_pairs={{0,4},{4,0},{1,5},{5,1},{2,6},{6,2},{3,7},{7,3},{8,12},{12,8},{9,1... | collective-permute-start | bytes 983048 | tf_op jit(solution)/shard_map/ppermute | solution.py:237
  69.8 10.8 %collective-permute-start.19 = (bf16[160,1024]{1,0:T(8,128)(2,1)S(1)}, bf16[160,1024]{1,0:T(8,128)(2,1)S(1)}, u32[]{:S(2)}, u32[]{:S(2)}) collective-permute-start(bf16[160,1024]{1,0:T(8,128)(2,1)S(1)} %collective-permute-done.15.refs_2_.refs_10_), channel_id=1, source_target_pairs={{0,4},{4,0},{1,5},{5,1},{2,6},{6,2},{3,7},{7,3},{8,12},{12,8},{9,1... | collective-permute-start | bytes 983048 | tf_op jit(solution)/shard_map/ppermute | solution.py:237
  70.3 10.4 %collective-permute-start.20 = (bf16[160,1024]{1,0:T(8,128)(2,1)S(1)}, bf16[160,1024]{1,0:T(8,128)(2,1)S(1)}, u32[]{:S(2)}, u32[]{:S(2)}) collective-permute-start(bf16[160,1024]{1,0:T(8,128)(2,1)S(1)} %collective-permute-done.16.refs_3_.refs_11_), channel_id=1, source_target_pairs={{0,4},{4,0},{1,5},{5,1},{2,6},{6,2},{3,7},{7,3},{8,12},{12,8},{9,1... | collective-permute-start | bytes 983048 | tf_op jit(solution)/shard_map/ppermute | solution.py:237
  79.6 7.7 %collective-permute-start.8 = (bf16[160,1024]{1,0:T(8,128)(2,1)S(1)}, bf16[160,1024]{1,0:T(8,128)(2,1)S(1)}, u32[]{:S(2)}, u32[]{:S(2)}) collective-permute-start(bf16[160,1024]{1,0:T(8,128)(2,1)S(1)} %get-tuple-element.39), channel_id=1, source_target_pairs={{0,4},{4,0},{1,5},{5,1},{2,6},{6,2},{3,7},{7,3},{8,12},{12,8},{9,1... | collective-permute-start | bytes 983048 | tf_op jit(solution)/shard_map/ppermute | solution.py:237
  80.1 12.9 %collective-permute-start.7 = (bf16[160,1024]{1,0:T(8,128)(2,1)S(1)}, bf16[160,1024]{1,0:T(8,128)(2,1)S(1)}, u32[]{:S(2)}, u32[]{:S(2)}) collective-permute-start(bf16[160,1024]{1,0:T(8,128)(2,1)S(1)} %get-tuple-element.37), channel_id=1, source_target_pairs={{0,4},{4,0},{1,5},{5,1},{2,6},{6,2},{3,7},{7,3},{8,12},{12,8},{9,1... | collective-permute-start | bytes 983048 | tf_op jit(solution)/shard_map/ppermute | solution.py:237
  80.1 7.4 %collective-permute-start.10 = (bf16[160,1024]{1,0:T(8,128)(2,1)S(1)}, bf16[160,1024]{1,0:T(8,128)(2,1)S(1)}, u32[]{:S(2)}, u32[]{:S(2)}) collective-permute-start(bf16[160,1024]{1,0:T(8,128)(2,1)S(1)} %get-tuple-element.41), channel_id=1, source_target_pairs={{0,4},{4,0},{1,5},{5,1},{2,6},{6,2},{3,7},{7,3},{8,12},{12,8},{9,1... | collective-permute-start | bytes 983048 | tf_op jit(solution)/shard_map/ppermute | solution.py:237
  80.6 7.5 %collective-permute-start.12 = (bf16[160,1024]{1,0:T(8,128)(2,1)S(1)}, bf16[160,1024]{1,0:T(8,128)(2,1)S(1)}, u32[]{:S(2)}, u32[]{:S(2)}) collective-permute-start(bf16[160,1024]{1,0:T(8,128)(2,1)S(1)} %get-tuple-element.43), channel_id=1, source_target_pairs={{0,4},{4,0},{1,5},{5,1},{2,6},{6,2},{3,7},{7,3},{8,12},{12,8},{9,1... | collective-permute-start | bytes 983048 | tf_op jit(solution)/shard_map/ppermute | solution.py:237
  86.8 7.5 %collective-permute-start.21 = (bf16[160,1024]{1,0:T(8,128)(2,1)S(1)}, bf16[160,1024]{1,0:T(8,128)(2,1)S(1)}, u32[]{:S(2)}, u32[]{:S(2)}) collective-permute-start(bf16[160,1024]{1,0:T(8,128)(2,1)S(1)} %get-tuple-element.48), channel_id=1, source_target_pairs={{0,4},{4,0},{1,5},{5,1},{2,6},{6,2},{3,7},{7,3},{8,12},{12,8},{9,1... | collective-permute-start | bytes 983048 | tf_op jit(solution)/shard_map/ppermute | solution.py:237
  87.3 1.7 %collective-permute-start.22 = (bf16[160,1024]{1,0:T(8,128)(2,1)S(1)}, bf16[160,1024]{1,0:T(8,128)(2,1)S(1)}, u32[]{:S(2)}, u32[]{:S(2)}) collective-permute-start(bf16[160,1024]{1,0:T(8,128)(2,1)S(1)} %get-tuple-element.50), channel_id=1, source_target_pairs={{0,4},{4,0},{1,5},{5,1},{2,6},{6,2},{3,7},{7,3},{8,12},{12,8},{9,1... | collective-permute-start | bytes 983048 | tf_op jit(solution)/shard_map/ppermute | solution.py:237
  87.5 2.0 %collective-permute-start.24 = (bf16[160,1024]{1,0:T(8,128)(2,1)S(1)}, bf16[160,1024]{1,0:T(8,128)(2,1)S(1)}, u32[]{:S(2)}, u32[]{:S(2)}) collective-permute-start(bf16[160,1024]{1,0:T(8,128)(2,1)S(1)} %get-tuple-element.52), channel_id=1, source_target_pairs={{0,4},{4,0},{1,5},{5,1},{2,6},{6,2},{3,7},{7,3},{8,12},{12,8},{9,1... | collective-permute-start | bytes 983048 | tf_op jit(solution)/shard_map/ppermute | solution.py:237
  88.1 3.7 %collective-permute-start.26 = (bf16[160,1024]{1,0:T(8,128)(2,1)S(1)}, bf16[160,1024]{1,0:T(8,128)(2,1)S(1)}, u32[]{:S(2)}, u32[]{:S(2)}) collective-permute-start(bf16[160,1024]{1,0:T(8,128)(2,1)S(1)} %get-tuple-element.54), channel_id=1, source_target_pairs={{0,4},{4,0},{1,5},{5,1},{2,6},{6,2},{3,7},{7,3},{8,12},{12,8},{9,1... | collective-permute-start | bytes 983048 | tf_op jit(solution)/shard_map/ppermute | solution.py:237
  89.0 18.8 %collective-permute-start.9 = (bf16[160,1024]{1,0:T(8,128)(2,1)S(1)}, bf16[160,1024]{1,0:T(8,128)(2,1)S(1)}, u32[]{:S(2)}, u32[]{:S(2)}) collective-permute-start(bf16[160,1024]{1,0:T(8,128)(2,1)S(1)} %add_convert_fusion.6), channel_id=1, source_target_pairs={{0,1},{1,2},{2,3},{3,0},{4,5},{5,6},{6,7},{7,4},{8,9},{9,10},{10,1... | collective-permute-start | bytes 983048 | tf_op jit(solution)/shard_map/ppermute | solution.py:237
  89.5 18.5 %collective-permute-start.11 = (bf16[160,1024]{1,0:T(8,128)(2,1)S(1)}, bf16[160,1024]{1,0:T(8,128)(2,1)S(1)}, u32[]{:S(2)}, u32[]{:S(2)}) collective-permute-start(bf16[160,1024]{1,0:T(8,128)(2,1)S(1)} %add_convert_fusion.5), channel_id=1, source_target_pairs={{0,2},{1,3},{2,0},{3,1},{4,6},{5,7},{6,4},{7,5},{8,10},{9,11},{10,... | collective-permute-start | bytes 983048 | tf_op jit(solution)/shard_map/ppermute | solution.py:237
  91.8 17.2 %collective-permute-start.13 = (bf16[160,1024]{1,0:T(8,128)(2,1)S(1)}, bf16[160,1024]{1,0:T(8,128)(2,1)S(1)}, u32[]{:S(2)}, u32[]{:S(2)}) collective-permute-start(bf16[160,1024]{1,0:T(8,128)(2,1)S(1)} %add_convert_fusion.4), channel_id=1, source_target_pairs={{0,3},{1,0},{2,1},{3,2},{4,7},{5,4},{6,5},{7,6},{8,11},{9,8},{10,9... | collective-permute-start | bytes 983048 | tf_op jit(solution)/shard_map/ppermute | solution.py:237
  93.0 28.3 %collective-permute-start.23 = (bf16[160,1024]{1,0:T(8,128)(2,1)S(1)}, bf16[160,1024]{1,0:T(8,128)(2,1)S(1)}, u32[]{:S(2)}, u32[]{:S(2)}) collective-permute-start(bf16[160,1024]{1,0:T(8,128)(2,1)S(1)} %add_convert_fusion.2), channel_id=1, source_target_pairs={{0,1},{1,2},{2,3},{3,0},{4,5},{5,6},{6,7},{7,4},{8,9},{9,10},{10,1... | collective-permute-start | bytes 983048 | tf_op jit(solution)/shard_map/ppermute | solution.py:237
  94.3 27.0 %collective-permute-start.25 = (bf16[160,1024]{1,0:T(8,128)(2,1)S(1)}, bf16[160,1024]{1,0:T(8,128)(2,1)S(1)}, u32[]{:S(2)}, u32[]{:S(2)}) collective-permute-start(bf16[160,1024]{1,0:T(8,128)(2,1)S(1)} %add_convert_fusion.1), channel_id=1, source_target_pairs={{0,2},{1,3},{2,0},{3,1},{4,6},{5,7},{6,4},{7,5},{8,10},{9,11},{10,... | collective-permute-start | bytes 983048 | tf_op jit(solution)/shard_map/ppermute | solution.py:237
  107.8 14.4 %collective-permute-start.27 = (bf16[160,1024]{1,0:T(8,128)(2,1)S(1)}, bf16[160,1024]{1,0:T(8,128)(2,1)S(1)}, u32[]{:S(2)}, u32[]{:S(2)}) collective-permute-start(bf16[160,1024]{1,0:T(8,128)(2,1)S(1)} %add_convert_fusion), channel_id=1, source_target_pairs={{0,3},{1,0},{2,1},{3,2},{4,7},{5,4},{6,5},{7,6},{8,11},{9,8},{10,9... | collective-permute-start | bytes 983048 | tf_op jit(solution)/shard_map/ppermute | solution.py:237
  123.8 26.6 %all-to-all-start.1 = ((bf16[32,80,128]{2,1,0:T(8,128)(2,1)}), bf16[32,80,128]{2,1,0:T(8,128)(2,1)S(1)}, u32[]{:S(2)}, u32[]{:S(2)}) async-start(bf16[32,80,128]{2,1,0:T(8,128)(2,1)} %bitcast.4), calls=%async_computation.1 | async-start | bytes 1310720 | tf_op jit(solution)/shard_map/all_to_all | solution.py:243
  (24 other events, 46.4 us)

commit v2 on v1

v2 whole, which is shorter than its diff:
```python
import functools

import jax
import jax.numpy as jnp
from jax import lax
from jax.experimental import pallas as pl
from jax.experimental.pallas import tpu as pltpu
from jax.sharding import Mesh, PartitionSpec as P

EXPERTS = 32
CAP = 5
LANES = 128
TILE = 16
F32 = jnp.float32
BF16 = jnp.bfloat16
VMEM_LIMIT = 12 * 1024 * 1024
SEND_LIMIT = 56 * 1024 * 1024


def dot(a, b, contract=((1,), (0,))):
    return lax.dot_general(a, b, (contract, ((), ())), preferred_element_type=F32)


def kernel_call(body, out_shape, flops, moved):
    def call(*args):
        specs = [pl.BlockSpec(memory_space=pltpu.VMEM)] * len(args)
        return pl.pallas_call(
            body,
            name=getattr(body, "func", body).__name__,
            out_shape=out_shape,
            in_specs=specs,
            out_specs=jax.tree.map(lambda _: pl.BlockSpec(memory_space=pltpu.VMEM), out_shape),
            compiler_params=pltpu.CompilerParams(vmem_limit_bytes=VMEM_LIMIT),
            cost_estimate=pl.CostEstimate(flops=flops, bytes_accessed=moved, transcendentals=0),
        )(*args)

    return call


def exchange_matrix():
    n = TILE * TILE
    out_row = lax.broadcasted_iota(jnp.int32, (n, n), 0)
    in_row = lax.broadcasted_iota(jnp.int32, (n, n), 1)
    return (in_row == (out_row % TILE) * TILE + out_row // TILE).astype(BF16)


def pack_rows(left, right, packed_ref):
    swap = exchange_matrix()
    rows = TILE * TILE
    for group in range(packed_ref.shape[0] // rows):
        parts = [side[group * TILE : (group + 1) * TILE] for side in (left, right)]
        stacked = [part[:, j * LANES : (j + 1) * LANES] for part in parts for j in range(TILE // 2)]
        packed_ref[pl.ds(group * rows, rows), :] = dot(swap, jnp.concatenate(stacked, axis=0)).astype(BF16)


def unpack_rows(packed_ref, wide_refs):
    swap = exchange_matrix()
    rows = TILE * TILE
    for group in range(packed_ref.shape[0] // rows):
        value = dot(swap, packed_ref[pl.ds(group * rows, rows), :]).astype(BF16)
        for at, wide in wide_refs.items():
            for j in range(TILE // 2):
                q = (at * (TILE // 2) + j) * TILE
                wide[pl.ds(group * TILE, TILE), pl.ds(j * LANES, LANES)] = value[q : q + TILE]


def token_slots(ids_row):
    tokens = ids_row.shape[1]
    expert = lax.broadcasted_iota(jnp.int32, (EXPERTS, tokens), 0)
    onehot = (expert == ids_row).astype(F32)
    before = lax.broadcasted_iota(jnp.int32, (tokens, tokens), 0)
    token = lax.broadcasted_iota(jnp.int32, (tokens, tokens), 1)
    earlier = (before < token).astype(BF16)
    counts = dot(onehot.astype(BF16), earlier)
    rank = jnp.sum(counts * onehot, axis=0, keepdims=True)
    return ids_row * CAP + rank.astype(jnp.int32)


def placement(ids_row):
    tokens = ids_row.shape[1]
    slot = lax.broadcasted_iota(jnp.int32, (EXPERTS * CAP, tokens), 0)
    return (slot == token_slots(ids_row)).astype(BF16)


def column(row):
    return jnp.transpose(jnp.broadcast_to(row.astype(F32), (LANES, row.shape[1])))[:, :1]


def column(row):
    return jnp.transpose(jnp.broadcast_to(row.astype(F32), (LANES, row.shape[1])))[:, :1]


def send_kernel(ids_hbm, probs_hbm, hidden_hbm, cotangent_hbm, packed_ref, ids, probs, hidden, cotangent, sems):
    pairs = ((ids_hbm, ids), (probs_hbm, probs), (hidden_hbm, hidden), (cotangent_hbm, cotangent))
    copies = [pltpu.make_async_copy(*pair, sems.at[at]) for at, pair in enumerate(pairs)]
    for copy in copies:
        copy.start()
    copies[0].wait()
    select = placement(ids[...])
    copies[2].wait()
    left = dot(select, hidden[...]).astype(BF16)
    copies[1].wait()
    copies[3].wait()
    scaled = (column(probs[...]) * cotangent[...].astype(F32)).astype(BF16)
    pack_rows(left, dot(select, scaled).astype(BF16), packed_ref)


def send(*args):
    return pl.pallas_call(
        send_kernel,
        name="send",
        out_shape=jax.ShapeDtypeStruct((EXPERTS * CAP * TILE, LANES), BF16),
        in_specs=[pl.BlockSpec(memory_space=pltpu.HBM)] * len(args),
        out_specs=pl.BlockSpec(memory_space=pltpu.VMEM),
        scratch_shapes=[pltpu.VMEM(a.shape, a.dtype) for a in args] + [pltpu.SemaphoreType.DMA((len(args),))],
        compiler_params=pltpu.CompilerParams(vmem_limit_bytes=SEND_LIMIT),
    )(*args)


def unpack_kernel(packed_ref, x_ref, s_ref):
    unpack_rows(packed_ref, {0: x_ref, 1: s_ref})


def unpack(packed):
    out = jax.ShapeDtypeStruct((packed.shape[0] // TILE, TILE * LANES // 2), BF16)
    return kernel_call(unpack_kernel, (out, out), 4 * packed.size * LANES, 8 * packed.size)(packed)


def blocks(parts):
    mp, core = lax.axis_index("mp"), lax.axis_index("core")
    ahead = 1 + (parts - 2) * core
    return [lax.rem(mp + step, parts) for step in (0, parts - ahead, ahead, parts // 2)]


def columns(ref, block, parts):
    width = ref.shape[1] // parts
    return pl.ds(pl.multiple_of(block * width, width), width)


def held_shards(refs):
    return [jnp.concatenate([refs[at][...], refs[at + 1][...]], axis=0) for at in range(0, len(refs), 2)]


def write_shards(values, refs):
    for at, value in enumerate(values):
        half = value.shape[0] // 2
        refs[2 * at][...] = value[:half]
        refs[2 * at + 1][...] = value[half:]


def forward_kernel(parts, *refs):
    shards, (wg, wu, wd, gate_ref, up_ref, gated_ref), out = refs[:8], refs[8:14], refs[14:]
    places = blocks(parts)
    gate, up = 0.0, 0.0
    for block, x in zip(places, held_shards(shards)):
        at = columns(wg, block, parts)
        gate = gate + dot(x, wg[:, at], ((1,), (1,)))
        up = up + dot(x, wu[:, at], ((1,), (1,)))
    gate_ref[...] = gate
    up_ref[...] = up
    gated = (gate * (1.0 / (1.0 + jnp.exp(-gate))) * up).astype(BF16)
    gated_ref[...] = gated
    write_shards([dot(gated, wd[:, columns(wd, block, parts)]).astype(BF16) for block in places], out)


def backward_kernel(parts, *refs):
    shards, (wg, wu, wd, gate_ref, up_ref, ggp_ref, gup_ref), dx = refs[:8], refs[8:15], refs[15:]
    places = blocks(parts)
    grad = 0.0
    for block, s in zip(places, held_shards(shards)):
        grad = grad + dot(s, wd[:, columns(wd, block, parts)], ((1,), (1,)))
    gate = gate_ref[...]
    sigmoid = 1.0 / (1.0 + jnp.exp(-gate))
    ggp = (grad * up_ref[...] * sigmoid * (1.0 + gate * (1.0 - sigmoid))).astype(BF16)
    gup = (grad * (gate * sigmoid)).astype(BF16)
    ggp_ref[...] = ggp
    gup_ref[...] = gup
    values = []
    for block in places:
        at = columns(wg, block, parts)
        values.append((dot(ggp, wg[:, at]) + dot(gup, wu[:, at])).astype(BF16))
    write_shards(values, dx)


def weights_kernel(parts, *refs):
    x_shards, s_shards, (ggp_ref, gup_ref, gated_ref, gwg, gwu, gwd) = refs[:8], refs[8:16], refs[16:]
    rows = ((0,), (0,))
    for block, x, s in zip(blocks(parts), held_shards(x_shards), held_shards(s_shards)):
        at = columns(gwg, block, parts)
        gwg[:, at] = dot(ggp_ref[...], x, rows).astype(BF16)
        gwu[:, at] = dot(gup_ref[...], x, rows).astype(BF16)
        gwd[:, at] = dot(gated_ref[...], s, rows).astype(BF16)


def add(*terms):
    value = terms[0].astype(F32)
    for term in terms[1:]:
        value = value + term.astype(F32)
    return value.astype(BF16)


def return_kernel(*refs):
    sums = []
    for terms in (refs[:3], refs[3:6]):
        sums.append(add(*(term[...] for term in terms)))
    pack_rows(*sums, refs[6])


def pack_return(*terms):
    packed = jax.ShapeDtypeStruct((2 * terms[0].size // LANES, LANES), BF16)
    return kernel_call(return_kernel, packed, 4 * packed.size * LANES, 8 * packed.size)(*terms)


def home_terms_kernel(ids_ref, cotangent_ref, packed_ref, terms_ref, out_ref, wide):
    unpack_rows(packed_ref, {0: wide})
    out = dot(placement(ids_ref[...]), wide[...], ((0,), (0,)))
    out_ref[...] = out
    terms = jnp.sum(cotangent_ref[...].astype(F32) * out, axis=1, keepdims=True)
    terms_ref[...] = jnp.transpose(jnp.broadcast_to(terms, (terms.shape[0], LANES)))[:1]


def home_rest_kernel(ids_ref, probs_ref, out_ref, packed_ref, mixed_ref, hidden_ref, wide):
    mixed_ref[...] = (column(probs_ref[...]) * out_ref[...]).astype(BF16)
    unpack_rows(packed_ref, {1: wide})
    hidden_ref[...] = dot(placement(ids_ref[...]), wide[...], ((0,), (0,))).astype(BF16)


def home(body, name, out_shape, *args):
    packed = args[-1]
    return pl.pallas_call(
        body,
        name=name,
        out_shape=out_shape,
        in_specs=[pl.BlockSpec(memory_space=pltpu.VMEM)] * len(args),
        scratch_shapes=[pltpu.VMEM((packed.shape[0] // TILE, TILE * LANES // 2), BF16)],
        compiler_params=pltpu.CompilerParams(vmem_limit_bytes=VMEM_LIMIT),
    )(*args)


def shift(value, axis, step):
    count = lax.axis_size(axis)
    return lax.ppermute(value, axis, [(i, (i + step) % count) for i in range(count)])


def swap_cores(value):
    return shift(value, "core", 1)


def ring(value):
    count = lax.axis_size("mp")
    pairs = [(i, (i + 1) % count) for i in range(count)]
    pairs += [(count + i, count + (i - 1) % count) for i in range(count)]
    return lax.ppermute(value, ("core", "mp"), pairs)


def after(value, *first):
    return lax.optimization_barrier((value, *first))[0]


def summed(own, own_other, behind, behind_other, ahead, ahead_other, opposite, opposite_other):
    tail = ring(add(opposite, swap_cores(opposite_other)))
    came_other = ring(add(ahead_other, swap_cores(behind)))
    came = ring(add(ahead, swap_cores(behind_other), tail))
    return own, came, swap_cores(add(own_other, came_other))


def over_yz(packed):
    parts = lax.axis_size("y") * lax.axis_size("z")
    split = packed.reshape(parts, packed.shape[0] // parts, packed.shape[1])
    return lax.all_to_all(split, ("y", "z"), 0, 0, tiled=True).reshape(packed.shape)


def body(hidden_states, expert_ids, probs, cotangent, w_gate, w_up, w_down):
    parts = lax.axis_size("mp")
    tokens = hidden_states.shape[0]
    hidden_rows, model_width = w_gate.shape
    ids_row, probs_row = expert_ids.reshape(1, tokens), probs.reshape(1, tokens)
    x_own, s_own = unpack(over_yz(send(ids_row, probs_row, hidden_states, cotangent)))
    x_other, s_other = swap_cores(x_own), swap_cores(s_own)
    x_behind = ring(x_own)
    x_behind_other = ring(x_other)
    x_opposite = ring(x_behind)
    x_shards = (x_own, x_other, x_behind, x_behind_other)
    x_shards += (swap_cores(x_behind_other), swap_cores(x_behind), x_opposite, swap_cores(x_opposite))
    slots, width = x_own.shape
    pair = 2 * slots
    act = jax.ShapeDtypeStruct((pair, hidden_rows), F32)
    act16 = jax.ShapeDtypeStruct((pair, hidden_rows), BF16)
    sums = (jax.ShapeDtypeStruct((slots, width), BF16),) * (2 * parts)
    weight = jax.ShapeDtypeStruct(w_gate.shape, BF16)
    product = 2 * pair * hidden_rows * model_width
    moved = 2 * hidden_rows * model_width
    gate, up, gated, *out = kernel_call(
        functools.partial(forward_kernel, parts), (act, act, act16) + sums, 3 * product, 6 * moved
    )(*x_shards, w_gate, w_up, w_down)
    s_behind = ring(s_own)
    s_behind_other = ring(after(s_other, x_behind))
    s_opposite = ring(s_behind)
    s_shards = (s_own, s_other, s_behind, s_behind_other)
    s_shards += tuple(
        swap_cores(after(value, gate)) for value in (s_behind_other, s_behind, s_opposite)
    )
    s_shards = s_shards[:6] + (s_opposite, s_shards[6])
    ggp, gup, *dx = kernel_call(
        functools.partial(backward_kernel, parts), (act16, act16) + sums, 3 * product, 6 * moved
    )(*s_shards, w_gate, w_up, w_down, gate, up)
    out_sum = summed(*out)
    own, own_other, behind, behind_other, ahead, ahead_other, opposite, opposite_other = dx
    tail = ring(add(opposite, swap_cores(opposite_other)))
    came_other = ring(add(ahead_other, swap_cores(behind)))
    last = add(ahead, swap_cores(behind_other), tail)
    came = ring(last)
    grads = kernel_call(functools.partial(weights_kernel, parts), (weight, weight, weight), 3 * product, 6 * moved)(
        *x_shards, *s_shards, after(ggp, last), gup, gated
    )
    dx_sum = (own, after(came, grads[0]), swap_cores(add(own_other, came_other)))
    packed = over_yz(pack_return(*out_sum, *dx_sum))
    wide = jax.ShapeDtypeStruct(hidden_states.shape, BF16)
    row = jax.ShapeDtypeStruct((1, tokens), F32)
    placed = jax.ShapeDtypeStruct(hidden_states.shape, F32)
    terms, out_rows = home(home_terms_kernel, "home_terms", (row, placed), ids_row, cotangent, packed)
    one, two, three = (shift(terms, "mp", step) for step in range(1, parts))
    mixed, grad_hidden = home(home_rest_kernel, "home_rest", (wide, wide), ids_row, probs_row, out_rows, packed)
    grad_probs = ((terms + two) + (one + three)).reshape(tokens, 1)
    return (mixed, grad_hidden, grad_probs, *grads)


def solution(mesh):
    yz_core = mesh.devices.shape[0]
    cores = 2
    columns_count = EXPERTS
    rows_y = 4
    grid = Mesh(
        mesh.devices.reshape(rows_y, yz_core // (cores * rows_y), cores, mesh.devices.shape[1]),
        ("y", "z", "core", "mp"),
    )
    assert yz_core == columns_count * cores
    blk = ("y", "z", "core")
    wide, thin, weight = P(blk, "mp"), P(blk, None), P(blk + ("mp",), None)
    return jax.shard_map(
        body,
        mesh=grid,
        in_specs=(wide, thin, thin, wide, weight, weight, weight),
        out_specs=(wide, wide, thin, weight, weight, weight),
        check_vma=False,
    )
```

time: 172 us -> 133 us (0.77)
  local copies, waits for them, and re-layouts: 18.8 us -> 1.43 us
  starting transfers between devices: 28.9 us -> 14.3 us
  waiting for transfers between devices: 51.3 us -> 40.8 us
  blocking collectives: 49.2 us -> 57.3 us
  Pallas kernels: 21.2 us -> 17 us
    ppermute x28 -> x19, waiting for transfers between devices: 44.9 us -> 4.49 us  [shift(): lax.ppermute(value, axis, [(i, (i + step) % count) for i in range(count)])]
    ppermute x0 -> x12, waiting for transfers between devices: none -> 36.3 us  [ring(): return lax.ppermute(value, ('core', 'mp'), pairs)]
    all_to_all x1 -> x2, blocking collectives: 31.4 us -> 57.3 us  [over_yz(): lax.all_to_all(split, ('y', 'z'), 0, 0, tiled=True).reshape(packed.shape)]
    psum x1 -> x0, blocking collectives: 17.8 us -> none  [body(): grad_probs = lax.psum(terms, 'mp')]
    unnamed x56 -> x12, local copies, waits for them, and re-layouts: 18.8 us -> 1.43 us
    ppermute x28 -> x19, starting transfers between devices: 22.1 us -> 6.68 us  [shift(): lax.ppermute(value, axis, [(i, (i + step) % count) for i in range(count)])]
    ppermute x0 -> x12, starting transfers between devices: none -> 7.65 us  [ring(): return lax.ppermute(value, ('core', 'mp'), pairs)]
    all_to_all x1 -> x0, starting transfers between devices: 6.85 us -> none  [over_yz(): lax.all_to_all(split, ('y', 'z'), 0, 0, tiled=True).reshape(packed.shape)]
  transfers between devices with their start and end apart: 29 -> 31, of which waited for: 12 -> 15; matrix products, arithmetic and copies ran while one was open for 0% -> 1% of each run, Pallas kernels for 10% -> 9%
where the time goes in v2:
time: 133 us
  blocking collectives  57.3 us (43%)
  waiting for transfers between devices  40.8 us (31%)
  Pallas kernels  17 us (13%)
  starting transfers between devices  14.3 us (11%)
  local copies, waits for them, and re-layouts  1.43 us (1%)
  other arithmetic  1.42 us (1%)
    all_to_all x2, blocking collectives, over_yz(): lax.all_to_all(split, ('y', 'z'), 0, 0, tiled=True).reshape(packed.shape)  57.3 us
    ppermute x12, waiting for transfers between devices, ring(): return lax.ppermute(value, ('core', 'mp'), pairs)  36.3 us
    pallas_call x5, Pallas kernels, call(): pl.pallas_call(body, name=getattr(body, 'func', body).__name__, out_shape...  11.5 us
    ppermute x12, starting transfers between devices, ring(): return lax.ppermute(value, ('core', 'mp'), pairs)  7.65 us
    ppermute x19, starting transfers between devices, shift(): lax.ppermute(value, axis, [(i, (i + step) % count) for i in range(count)])  6.68 us
    ppermute x19, waiting for transfers between devices, shift(): lax.ppermute(value, axis, [(i, (i + step) % count) for i in range(count)])  4.49 us
    pallas_call x1, Pallas kernels, send(): pl.pallas_call(send_kernel, name='send', out_shape=jax.ShapeDtypeStruct((...  3.08 us
  transfers between devices with their start and end apart: 31, of which 15 were waited for; matrix products, arithmetic and copies ran while one was open for 1% of the time, Pallas kernels for 9%

profile of v2, /device:TPU:32, one launch (start us, length us, event | category | flops | bytes accessed | tf_op | source)
XLA Modules:
  0.0 133.2 jit_solution(8700580835588349839)
XLA Ops:
  0.7 3.1 %send.1 = bf16[2560,128]{1,0:T(8,128)(2,1)} custom-call(s32[1,128]{1,0:T(1,128)} %bitcast.12, bf16[1,128]{1,0:T(2,128)(2,1)} %bitcast.15, bf16[128,1024]{1,0:T(8,128)(2,1)} %hidden_hbm.1, bf16[128,1024]{1,0:T(8,128)(2,1)} %cotangent_ref.1), custom_call_target="tpu_custom_call" | custom-call | tf_op jit(solution)/shard_map/send/pallas_call | solution.py:109
  3.7 31.6 %all_to_all.10 = bf16[32,80,128]{2,1,0:T(8,128)(2,1)S(1)} all-to-all(bf16[32,80,128]{2,1,0:T(8,128)(2,1)} %bitcast.17), channel_id=1, replica_groups=mesh['y'=4,'z'=8,'core'=2,'mp'=4] {'y','z'}, dimensions={0} | all-to-all | bytes 1310720 | tf_op jit(solution)/shard_map/all_to_all | solution.py:270
  35.9 1.6 %collective-permute-start.1 = (bf16[160,1024]{1,0:T(8,128)(2,1)S(1)}, bf16[160,1024]{1,0:T(8,128)(2,1)S(1)}, u32[]{:S(2)}, u32[]{:S(2)}) collective-permute-start(bf16[160,1024]{1,0:T(8,128)(2,1)S(1)} %get-tuple-element.42.refs_0_), channel_id=1, source_target_pairs={{0,1},{1,2},{2,3},{3,0},{4,7},{5,4},{6,5},{7,6},{8,9},{9,10},{10,1... | collective-permute-start | bytes 983048 | tf_op jit(solution)/shard_map/ppermute | solution.py:253
  37.4 6.8 %collective-permute-done.1.refs_2_ = bf16[160,1024]{1,0:T(8,128)(2,1)S(1)} collective-permute-done((bf16[160,1024]{1,0:T(8,128)(2,1)S(1)}, bf16[160,1024]{1,0:T(8,128)(2,1)S(1)}, u32[]{:S(2)}, u32[]{:S(2)}) %collective-permute-start.1) | collective-permute-done | bytes 327712 | tf_op jit(solution)/shard_map/ppermute | solution.py:253
  44.5 1.5 %collective-permute-start.2 = (bf16[160,1024]{1,0:T(8,128)(2,1)S(1)}, bf16[160,1024]{1,0:T(8,128)(2,1)S(1)}, u32[]{:S(2)}, u32[]{:S(2)}) collective-permute-start(bf16[160,1024]{1,0:T(8,128)(2,1)S(1)} %collective-permute-done.refs_1_), channel_id=1, source_target_pairs={{0,1},{1,2},{2,3},{3,0},{4,7},{5,4},{6,5},{7,6},{8,9},{9,10},{10,1... | collective-permute-start | bytes 983048 | tf_op jit(solution)/shard_map/ppermute | solution.py:253
  46.0 1.2 collective-permute-start.15
  47.2 0.8 collective-permute-start.4
  48.0 4.5 %collective-permute-done.5.refs_6_ = bf16[160,1024]{1,0:T(8,128)(2,1)S(1)} collective-permute-done((bf16[160,1024]{1,0:T(8,128)(2,1)S(1)}, bf16[160,1024]{1,0:T(8,128)(2,1)S(1)}, u32[]{:S(2)}, u32[]{:S(2)}) %collective-permute-start.5) | collective-permute-done | bytes 327712 | tf_op jit(solution)/shard_map/ppermute | solution.py:253
  52.5 3.5 %collective-permute-done.2.refs_3_ = bf16[160,1024]{1,0:T(8,128)(2,1)S(1)} collective-permute-done((bf16[160,1024]{1,0:T(8,128)(2,1)S(1)}, bf16[160,1024]{1,0:T(8,128)(2,1)S(1)}, u32[]{:S(2)}, u32[]{:S(2)}) %collective-permute-start.2) | collective-permute-done | bytes 327712 | tf_op jit(solution)/shard_map/ppermute | solution.py:253
  56.0 3.5 %collective-permute-done.15.refs_2_.refs_10_ = bf16[160,1024]{1,0:T(8,128)(2,1)S(1)} collective-permute-done((bf16[160,1024]{1,0:T(8,128)(2,1)S(1)}, bf16[160,1024]{1,0:T(8,128)(2,1)S(1)}, u32[]{:S(2)}, u32[]{:S(2)}) %collective-permute-start.15) | collective-permute-done | bytes 327712 | tf_op jit(solution)/shard_map/ppermute | solution.py:253
  59.6 1.4 %copy-done.2 = bf16[192,4096]{1,0:T(8,128)(2,1)S(1)} copy-done((bf16[192,4096]{1,0:T(8,128)(2,1)S(1)}, bf16[192,4096]{1,0:T(8,128)(2,1)}, u32[]{:S(2)}) %copy-start.2) | copy-done | bytes 1572888
  61.0 2.3 %forward_kernel.1 = (f32[320,192]{1,0:T(8,128)S(1)}, f32[320,192]{1,0:T(8,128)S(1)}, bf16[320,192]{1,0:T(8,128)(2,1)S(1)}, bf16[160,1024]{1,0:T(8,128)(2,1)S(1)}...) custom-call(bf16[160,1024]{1,0:T(8,128)(2,1)S(1)} %get-tuple-element, ...), custom_call_target="tpu_custom_call" | custom-call | flops 1509949440 | bytes 9437184 | tf_op jit(solution)/shard_map/forward_kernel/pallas_call | solution.py:27
  63.4 4.4 %collective-permute-done.19.refs_6_.refs_14_ = bf16[160,1024]{1,0:T(8,128)(2,1)S(1)} collective-permute-done((bf16[160,1024]{1,0:T(8,128)(2,1)S(1)}, bf16[160,1024]{1,0:T(8,128)(2,1)S(1)}, u32[]{:S(2)}, u32[]{:S(2)}) %collective-permute-start.19) | collective-permute-done | bytes 327712 | tf_op jit(solution)/shard_map/ppermute | solution.py:253
  70.4 3.7 %backward_kernel.1 = (bf16[320,192]{1,0:T(8,128)(2,1)S(1)}, bf16[320,192]{1,0:T(8,128)(2,1)S(1)}, bf16[160,1024]{1,0:T(8,128)(2,1)S(1)}, bf16[160,1024]{1,0:T(8,...) custom-call(bf16[160,1024]{1,0:T(8,128)(2,1)S(1)} %get-tuple-element, ...), custom_call_target="tpu_custom_call" | custom-call | flops 1509949440 | bytes 9437184 | tf_op jit(solution)/shard_map/backward_kernel/pallas_call | solution.py:27
  74.4 0.9 collective-permute-start.12
  75.3 1.6 %collective-permute-start.21 = (bf16[160,1024]{1,0:T(8,128)(2,1)S(1)}, bf16[160,1024]{1,0:T(8,128)(2,1)S(1)}, u32[]{:S(2)}, u32[]{:S(2)}) collective-permute-start(bf16[160,1024]{1,0:T(8,128)(2,1)S(1)} %get-tuple-element.60), channel_id=1, source_target_pairs={{0,4},{4,0},{1,5},{5,1},{2,6},{6,2},{3,7},{7,3},{8,12},{12,8},{9,1... | collective-permute-start | bytes 983048 | tf_op jit(solution)/shard_map/ppermute | solution.py:242
  76.9 0.9 collective-permute-done.9
  78.1 0.9 collective-permute-start.23
  79.2 1.1 collective-permute-start.26
  80.3 2.5 %collective-permute-done.12 = bf16[160,1024]{1,0:T(8,128)(2,1)S(1)} collective-permute-done((bf16[160,1024]{1,0:T(8,128)(2,1)S(1)}, bf16[160,1024]{1,0:T(8,128)(2,1)S(1)}, u32[]{:S(2)}, u32[]{:S(2)}) %collective-permute-start.12) | collective-permute-done | bytes 327712 | tf_op jit(solution)/shard_map/ppermute | solution.py:253
  83.0 6.8 %collective-permute-done.23 = bf16[160,1024]{1,0:T(8,128)(2,1)S(1)} collective-permute-done((bf16[160,1024]{1,0:T(8,128)(2,1)S(1)}, bf16[160,1024]{1,0:T(8,128)(2,1)S(1)}, u32[]{:S(2)}, u32[]{:S(2)}) %collective-permute-start.23) | collective-permute-done | bytes 327712 | tf_op jit(solution)/shard_map/ppermute | solution.py:253
  90.1 3.3 %collective-permute-done.26 = bf16[160,1024]{1,0:T(8,128)(2,1)S(1)} collective-permute-done((bf16[160,1024]{1,0:T(8,128)(2,1)S(1)}, bf16[160,1024]{1,0:T(8,128)(2,1)S(1)}, u32[]{:S(2)}, u32[]{:S(2)}) %collective-permute-start.26) | collective-permute-done | bytes 327712 | tf_op jit(solution)/shard_map/ppermute | solution.py:253
  93.7 4.5 %weights_kernel.1 = (bf16[192,4096]{1,0:T(8,128)(2,1)}, bf16[192,4096]{1,0:T(8,128)(2,1)}, bf16[192,4096]{1,0:T(8,128)(2,1)}) custom-call(bf16[160,1024]{1,0:T(8,128)(2,1)S(1)} %get-tuple-element.42.refs_0_, bf16[160,1024]{1,0:T(8,128)(2,1)S(1)} %collective-permute-done.refs_1_, bf16[160,1024]{1,0:T(8,128)(2,1)S(1)} %collective-permute-done.1.refs_2_, ...), custom_call_target="tpu_custom_call" | custom-call | flops 1509949440 | bytes 9437184 | tf_op jit(solution)/shard_map/weights_kernel/pallas_call | solution.py:27
  98.4 0.6 return_kernel.1
  98.9 25.7 %all_to_all.11 = bf16[32,80,128]{2,1,0:T(8,128)(2,1)S(1)} all-to-all(bf16[32,80,128]{2,1,0:T(8,128)(2,1)S(1)} %bitcast.10), channel_id=1, replica_groups=mesh['y'=4,'z'=8,'core'=2,'mp'=4] {'y','z'}, dimensions={0} | all-to-all | bytes 1310720 | tf_op jit(solution)/shard_map/all_to_all | solution.py:270
  124.7 0.9 home_terms.1
  125.5 1.0 collective-permute-start.30
  126.5 1.1 collective-permute-start.29
  128.1 1.5 %home_rest.1 = (bf16[128,1024]{1,0:T(8,128)(2,1)}, bf16[128,1024]{1,0:T(8,128)(2,1)}) custom-call(s32[1,128]{1,0:T(1,128)S(1)} %bitcast.14, bf16[1,128]{1,0:T(2,128)(2,1)S(1)} %bitcast.16, f32[128,1024]{1,0:T(8,128)S(1)} %get-tuple-element.72.out_ref, bf16[2560,128]{1,0:T(8,128)(2,1)S(1)} %bitcast.9), custom_call_target="tpu_custom_call" | custom-call | tf_op jit(solution)/shard_map/home_rest/pallas_call | solution.py:230
  129.6 1.7 %collective-permute-done.29 = f32[1,128]{1,0:T(1,128)S(1)} collective-permute-done((f32[1,128]{1,0:T(1,128)S(1)}, f32[1,128]{1,0:T(1,128)S(1)}, u32[]{:S(2)}, u32[]{:S(2)}) %collective-permute-start.29) | collective-permute-done | bytes 544 | tf_op jit(solution)/shard_map/ppermute | solution.py:242
  131.3 1.4 %collective-permute-done.28 = f32[1,128]{1,0:T(1,128)S(1)} collective-permute-done((f32[1,128]{1,0:T(1,128)S(1)}, f32[1,128]{1,0:T(1,128)S(1)}, u32[]{:S(2)}, u32[]{:S(2)}) %collective-permute-start.28) | collective-permute-done | bytes 544 | tf_op jit(solution)/shard_map/ppermute | solution.py:242
  132.7 0.5 add_bitcast_fusion
  (61 shorter events, 5.7 us)
Async XLA Ops:
  0.6 58.9 %copy-start = (bf16[192,4096]{1,0:T(8,128)(2,1)S(1)}, bf16[192,4096]{1,0:T(8,128)(2,1)}, u32[]{:S(2)}) copy-start(bf16[192,4096]{1,0:T(8,128)(2,1)} %refs_8_.3) | copy-start | bytes 4718596
  35.9 8.4 %collective-permute-start.1 = (bf16[160,1024]{1,0:T(8,128)(2,1)S(1)}, bf16[160,1024]{1,0:T(8,128)(2,1)S(1)}, u32[]{:S(2)}, u32[]{:S(2)}) collective-permute-start(bf16[160,1024]{1,0:T(8,128)(2,1)S(1)} %get-tuple-element.42.refs_0_), channel_id=1, source_target_pairs={{0,1},{1,2},{2,3},{3,0},{4,7},{5,4},{6,5},{7,6},{8,9},{9,10},{10,1... | collective-permute-start | bytes 983048 | tf_op jit(solution)/shard_map/ppermute | solution.py:253
  37.4 7.1 %collective-permute-start = (bf16[160,1024]{1,0:T(8,128)(2,1)S(1)}, bf16[160,1024]{1,0:T(8,128)(2,1)S(1)}, u32[]{:S(2)}, u32[]{:S(2)}) collective-permute-start(bf16[160,1024]{1,0:T(8,128)(2,1)S(1)} %get-tuple-element.42.refs_0_), channel_id=1, source_target_pairs={{0,4},{4,0},{1,5},{5,1},{2,6},{6,2},{3,7},{7,3},{8,12},{12,8},{9,1... | collective-permute-start | bytes 983048 | tf_op jit(solution)/shard_map/ppermute | solution.py:242
  44.2 8.3 %collective-permute-start.5 = (bf16[160,1024]{1,0:T(8,128)(2,1)S(1)}, bf16[160,1024]{1,0:T(8,128)(2,1)S(1)}, u32[]{:S(2)}, u32[]{:S(2)}) collective-permute-start(bf16[160,1024]{1,0:T(8,128)(2,1)S(1)} %collective-permute-done.1.refs_2_), channel_id=1, source_target_pairs={{0,1},{1,2},{2,3},{3,0},{4,7},{5,4},{6,5},{7,6},{8,9},{9,10},{10,1... | collective-permute-start | bytes 983048 | tf_op jit(solution)/shard_map/ppermute | solution.py:253
  44.5 11.5 %collective-permute-start.2 = (bf16[160,1024]{1,0:T(8,128)(2,1)S(1)}, bf16[160,1024]{1,0:T(8,128)(2,1)S(1)}, u32[]{:S(2)}, u32[]{:S(2)}) collective-permute-start(bf16[160,1024]{1,0:T(8,128)(2,1)S(1)} %collective-permute-done.refs_1_), channel_id=1, source_target_pairs={{0,1},{1,2},{2,3},{3,0},{4,7},{5,4},{6,5},{7,6},{8,9},{9,10},{10,1... | collective-permute-start | bytes 983048 | tf_op jit(solution)/shard_map/ppermute | solution.py:253
  46.0 10.0 %collective-permute-start.14 = (bf16[160,1024]{1,0:T(8,128)(2,1)S(1)}, bf16[160,1024]{1,0:T(8,128)(2,1)S(1)}, u32[]{:S(2)}, u32[]{:S(2)}) collective-permute-start(bf16[160,1024]{1,0:T(8,128)(2,1)S(1)} %get-tuple-element.51.refs_0_.refs_8_), channel_id=1, source_target_pairs={{0,4},{4,0},{1,5},{5,1},{2,6},{6,2},{3,7},{7,3},{8,12},{12,8},{9,1... | collective-permute-start | bytes 983048 | tf_op jit(solution)/shard_map/ppermute | solution.py:242
  46.0 13.5 %collective-permute-start.15 = (bf16[160,1024]{1,0:T(8,128)(2,1)S(1)}, bf16[160,1024]{1,0:T(8,128)(2,1)S(1)}, u32[]{:S(2)}, u32[]{:S(2)}) collective-permute-start(bf16[160,1024]{1,0:T(8,128)(2,1)S(1)} %get-tuple-element.51.refs_0_.refs_8_), channel_id=1, source_target_pairs={{0,1},{1,2},{2,3},{3,0},{4,7},{5,4},{6,5},{7,6},{8,9},{9,10},{10,1... | collective-permute-start | bytes 983048 | tf_op jit(solution)/shard_map/ppermute | solution.py:253
  47.2 12.3 %collective-permute-start.4 = (bf16[160,1024]{1,0:T(8,128)(2,1)S(1)}, bf16[160,1024]{1,0:T(8,128)(2,1)S(1)}, u32[]{:S(2)}, u32[]{:S(2)}) collective-permute-start(bf16[160,1024]{1,0:T(8,128)(2,1)S(1)} %collective-permute-done.1.refs_2_), channel_id=1, source_target_pairs={{0,4},{4,0},{1,5},{5,1},{2,6},{6,2},{3,7},{7,3},{8,12},{12,8},{9,1... | collective-permute-start | bytes 983048 | tf_op jit(solution)/shard_map/ppermute | solution.py:242
  52.5 7.0 %collective-permute-start.6 = (bf16[160,1024]{1,0:T(8,128)(2,1)S(1)}, bf16[160,1024]{1,0:T(8,128)(2,1)S(1)}, u32[]{:S(2)}, u32[]{:S(2)}) collective-permute-start(bf16[160,1024]{1,0:T(8,128)(2,1)S(1)} %collective-permute-done.5.refs_6_), channel_id=1, source_target_pairs={{0,4},{4,0},{1,5},{5,1},{2,6},{6,2},{3,7},{7,3},{8,12},{12,8},{9,1... | collective-permute-start | bytes 983048 | tf_op jit(solution)/shard_map/ppermute | solution.py:242
  56.0 3.5 %collective-permute-start.3 = (bf16[160,1024]{1,0:T(8,128)(2,1)S(1)}, bf16[160,1024]{1,0:T(8,128)(2,1)S(1)}, u32[]{:S(2)}, u32[]{:S(2)}) collective-permute-start(bf16[160,1024]{1,0:T(8,128)(2,1)S(1)} %collective-permute-done.2.refs_3_), channel_id=1, source_target_pairs={{0,4},{4,0},{1,5},{5,1},{2,6},{6,2},{3,7},{7,3},{8,12},{12,8},{9,1... | collective-permute-start | bytes 983048 | tf_op jit(solution)/shard_map/ppermute | solution.py:242
  56.0 11.8 %collective-permute-start.16 = (bf16[160,1024]{1,0:T(8,128)(2,1)S(1)}, bf16[160,1024]{1,0:T(8,128)(2,1)S(1)}, u32[]{:S(2)}, u32[]{:S(2)}) collective-permute-start(bf16[160,1024]{1,0:T(8,128)(2,1)S(1)} %collective-permute-done.14.refs_1_.refs_9_), channel_id=1, source_target_pairs={{0,1},{1,2},{2,3},{3,0},{4,7},{5,4},{6,5},{7,6},{8,9},{9,10},{10,1... | collective-permute-start | bytes 983048 | tf_op jit(solution)/shard_map/ppermute | solution.py:253
  59.5 8.3 %collective-permute-start.19 = (bf16[160,1024]{1,0:T(8,128)(2,1)S(1)}, bf16[160,1024]{1,0:T(8,128)(2,1)S(1)}, u32[]{:S(2)}, u32[]{:S(2)}) collective-permute-start(bf16[160,1024]{1,0:T(8,128)(2,1)S(1)} %collective-permute-done.15.refs_2_.refs_10_), channel_id=1, source_target_pairs={{0,1},{1,2},{2,3},{3,0},{4,7},{5,4},{6,5},{7,6},{8,9},{9,10},{10,1... | collective-permute-start | bytes 983048 | tf_op jit(solution)/shard_map/ppermute | solution.py:253
  63.3 5.6 %collective-permute-start.8 = (bf16[160,1024]{1,0:T(8,128)(2,1)S(1)}, bf16[160,1024]{1,0:T(8,128)(2,1)S(1)}, u32[]{:S(2)}, u32[]{:S(2)}) collective-permute-start(bf16[160,1024]{1,0:T(8,128)(2,1)S(1)} %get-tuple-element.47), channel_id=1, source_target_pairs={{0,4},{4,0},{1,5},{5,1},{2,6},{6,2},{3,7},{7,3},{8,12},{12,8},{9,1... | collective-permute-start | bytes 983048 | tf_op jit(solution)/shard_map/ppermute | solution.py:242
  67.8 1.6 %collective-permute-start.17 = (bf16[160,1024]{1,0:T(8,128)(2,1)S(1)}, bf16[160,1024]{1,0:T(8,128)(2,1)S(1)}, u32[]{:S(2)}, u32[]{:S(2)}) collective-permute-start(bf16[160,1024]{1,0:T(8,128)(2,1)S(1)} %collective-permute-done.16.refs_3_.refs_11_), channel_id=1, source_target_pairs={{0,4},{4,0},{1,5},{5,1},{2,6},{6,2},{3,7},{7,3},{8,12},{12,8},{9,1... | collective-permute-start | bytes 983048 | tf_op jit(solution)/shard_map/ppermute | solution.py:242
  67.8 2.1 %collective-permute-start.18 = (bf16[160,1024]{1,0:T(8,128)(2,1)S(1)}, bf16[160,1024]{1,0:T(8,128)(2,1)S(1)}, u32[]{:S(2)}, u32[]{:S(2)}) collective-permute-start(bf16[160,1024]{1,0:T(8,128)(2,1)S(1)} %collective-permute-done.15.refs_2_.refs_10_), channel_id=1, source_target_pairs={{0,4},{4,0},{1,5},{5,1},{2,6},{6,2},{3,7},{7,3},{8,12},{12,8},{9,1... | collective-permute-start | bytes 983048 | tf_op jit(solution)/shard_map/ppermute | solution.py:242
  68.3 2.1 %collective-permute-start.20 = (bf16[160,1024]{1,0:T(8,128)(2,1)S(1)}, bf16[160,1024]{1,0:T(8,128)(2,1)S(1)}, u32[]{:S(2)}, u32[]{:S(2)}) collective-permute-start(bf16[160,1024]{1,0:T(8,128)(2,1)S(1)} %collective-permute-done.19.refs_6_.refs_14_), channel_id=1, source_target_pairs={{0,4},{4,0},{1,5},{5,1},{2,6},{6,2},{3,7},{7,3},{8,12},{12,8},{9,1... | collective-permute-start | bytes 983048 | tf_op jit(solution)/shard_map/ppermute | solution.py:242
  68.4 8.5 %collective-permute-start.7 = (bf16[160,1024]{1,0:T(8,128)(2,1)S(1)}, bf16[160,1024]{1,0:T(8,128)(2,1)S(1)}, u32[]{:S(2)}, u32[]{:S(2)}) collective-permute-start(bf16[160,1024]{1,0:T(8,128)(2,1)S(1)} %get-tuple-element.45), channel_id=1, source_target_pairs={{0,4},{4,0},{1,5},{5,1},{2,6},{6,2},{3,7},{7,3},{8,12},{12,8},{9,1... | collective-permute-start | bytes 983048 | tf_op jit(solution)/shard_map/ppermute | solution.py:242
  68.9 5.4 %collective-permute-start.11 = (bf16[160,1024]{1,0:T(8,128)(2,1)S(1)}, bf16[160,1024]{1,0:T(8,128)(2,1)S(1)}, u32[]{:S(2)}, u32[]{:S(2)}) collective-permute-start(bf16[160,1024]{1,0:T(8,128)(2,1)S(1)} %get-tuple-element.50), channel_id=1, source_target_pairs={{0,4},{4,0},{1,5},{5,1},{2,6},{6,2},{3,7},{7,3},{8,12},{12,8},{9,1... | collective-permute-start | bytes 983048 | tf_op jit(solution)/shard_map/ppermute | solution.py:242
  69.5 8.3 %collective-permute-start.9 = (bf16[160,1024]{1,0:T(8,128)(2,1)S(1)}, bf16[160,1024]{1,0:T(8,128)(2,1)S(1)}, u32[]{:S(2)}, u32[]{:S(2)}) collective-permute-start(bf16[160,1024]{1,0:T(8,128)(2,1)S(1)} %add_convert_fusion.7), channel_id=1, source_target_pairs={{0,1},{1,2},{2,3},{3,0},{4,7},{5,4},{6,5},{7,6},{8,9},{9,10},{10,1... | collective-permute-start | bytes 983048 | tf_op jit(solution)/shard_map/ppermute | solution.py:253
  74.1 3.9 %collective-permute-start.22 = (bf16[160,1024]{1,0:T(8,128)(2,1)S(1)}, bf16[160,1024]{1,0:T(8,128)(2,1)S(1)}, u32[]{:S(2)}, u32[]{:S(2)}) collective-permute-start(bf16[160,1024]{1,0:T(8,128)(2,1)S(1)} %get-tuple-element.62), channel_id=1, source_target_pairs={{0,4},{4,0},{1,5},{5,1},{2,6},{6,2},{3,7},{7,3},{8,12},{12,8},{9,1... | collective-permute-start | bytes 983048 | tf_op jit(solution)/shard_map/ppermute | solution.py:242
  74.4 8.4 %collective-permute-start.12 = (bf16[160,1024]{1,0:T(8,128)(2,1)S(1)}, bf16[160,1024]{1,0:T(8,128)(2,1)S(1)}, u32[]{:S(2)}, u32[]{:S(2)}) collective-permute-start(bf16[160,1024]{1,0:T(8,128)(2,1)S(1)} %add_convert_fusion.5), channel_id=1, source_target_pairs={{0,1},{1,2},{2,3},{3,0},{4,7},{5,4},{6,5},{7,6},{8,9},{9,10},{10,1... | collective-permute-start | bytes 983048 | tf_op jit(solution)/shard_map/ppermute | solution.py:253
  75.3 7.7 %collective-permute-start.21 = (bf16[160,1024]{1,0:T(8,128)(2,1)S(1)}, bf16[160,1024]{1,0:T(8,128)(2,1)S(1)}, u32[]{:S(2)}, u32[]{:S(2)}) collective-permute-start(bf16[160,1024]{1,0:T(8,128)(2,1)S(1)} %get-tuple-element.60), channel_id=1, source_target_pairs={{0,4},{4,0},{1,5},{5,1},{2,6},{6,2},{3,7},{7,3},{8,12},{12,8},{9,1... | collective-permute-start | bytes 983048 | tf_op jit(solution)/shard_map/ppermute | solution.py:242
  76.9 2.2 %collective-permute-start.25 = (bf16[160,1024]{1,0:T(8,128)(2,1)S(1)}, bf16[160,1024]{1,0:T(8,128)(2,1)S(1)}, u32[]{:S(2)}, u32[]{:S(2)}) collective-permute-start(bf16[160,1024]{1,0:T(8,128)(2,1)S(1)} %get-tuple-element.71), channel_id=1, source_target_pairs={{0,4},{4,0},{1,5},{5,1},{2,6},{6,2},{3,7},{7,3},{8,12},{12,8},{9,1... | collective-permute-start | bytes 983048 | tf_op jit(solution)/shard_map/ppermute | solution.py:242
  77.9 20.4 %collective-permute-start.10 = (bf16[160,1024]{1,0:T(8,128)(2,1)S(1)}, bf16[160,1024]{1,0:T(8,128)(2,1)S(1)}, u32[]{:S(2)}, u32[]{:S(2)}) collective-permute-start(bf16[160,1024]{1,0:T(8,128)(2,1)S(1)} %add_convert_fusion.6), channel_id=1, source_target_pairs={{0,1},{1,2},{2,3},{3,0},{4,7},{5,4},{6,5},{7,6},{8,9},{9,10},{10,1... | collective-permute-start | bytes 983048 | tf_op jit(solution)/shard_map/ppermute | solution.py:253
  78.1 11.7 %collective-permute-start.23 = (bf16[160,1024]{1,0:T(8,128)(2,1)S(1)}, bf16[160,1024]{1,0:T(8,128)(2,1)S(1)}, u32[]{:S(2)}, u32[]{:S(2)}) collective-permute-start(bf16[160,1024]{1,0:T(8,128)(2,1)S(1)} %add_convert_fusion.3), channel_id=1, source_target_pairs={{0,1},{1,2},{2,3},{3,0},{4,7},{5,4},{6,5},{7,6},{8,9},{9,10},{10,1... | collective-permute-start | bytes 983048 | tf_op jit(solution)/shard_map/ppermute | solution.py:253
  79.2 14.2 %collective-permute-start.26 = (bf16[160,1024]{1,0:T(8,128)(2,1)S(1)}, bf16[160,1024]{1,0:T(8,128)(2,1)S(1)}, u32[]{:S(2)}, u32[]{:S(2)}) collective-permute-start(bf16[160,1024]{1,0:T(8,128)(2,1)S(1)} %add_convert_fusion.1), channel_id=1, source_target_pairs={{0,1},{1,2},{2,3},{3,0},{4,7},{5,4},{6,5},{7,6},{8,9},{9,10},{10,1... | collective-permute-start | bytes 983048 | tf_op jit(solution)/shard_map/ppermute | solution.py:253
  82.9 15.5 %collective-permute-start.13 = (bf16[160,1024]{1,0:T(8,128)(2,1)S(1)}, bf16[160,1024]{1,0:T(8,128)(2,1)S(1)}, u32[]{:S(2)}, u32[]{:S(2)}) collective-permute-start(bf16[160,1024]{1,0:T(8,128)(2,1)S(1)} %add_convert_fusion.4), channel_id=1, source_target_pairs={{0,4},{4,0},{1,5},{5,1},{2,6},{6,2},{3,7},{7,3},{8,12},{12,8},{9,1... | collective-permute-start | bytes 983048 | tf_op jit(solution)/shard_map/ppermute | solution.py:242
  90.0 8.4 %collective-permute-start.24 = (bf16[160,1024]{1,0:T(8,128)(2,1)S(1)}, bf16[160,1024]{1,0:T(8,128)(2,1)S(1)}, u32[]{:S(2)}, u32[]{:S(2)}) collective-permute-start(bf16[160,1024]{1,0:T(8,128)(2,1)S(1)} %add_convert_fusion.2), channel_id=1, source_target_pairs={{0,1},{1,2},{2,3},{3,0},{4,7},{5,4},{6,5},{7,6},{8,9},{9,10},{10,1... | collective-permute-start | bytes 983048 | tf_op jit(solution)/shard_map/ppermute | solution.py:253
  93.4 4.9 %collective-permute-start.27 = (bf16[160,1024]{1,0:T(8,128)(2,1)S(1)}, bf16[160,1024]{1,0:T(8,128)(2,1)S(1)}, u32[]{:S(2)}, u32[]{:S(2)}) collective-permute-start(bf16[160,1024]{1,0:T(8,128)(2,1)S(1)} %add_convert_fusion), channel_id=1, source_target_pairs={{0,4},{4,0},{1,5},{5,1},{2,6},{6,2},{3,7},{7,3},{8,12},{12,8},{9,1... | collective-permute-start | bytes 983048 | tf_op jit(solution)/shard_map/ppermute | solution.py:242
  125.5 4.1 %collective-permute-start.30 = (f32[1,128]{1,0:T(1,128)S(1)}, f32[1,128]{1,0:T(1,128)S(1)}, u32[]{:S(2)}, u32[]{:S(2)}) collective-permute-start(f32[1,128]{1,0:T(1,128)S(1)} %get-tuple-element.75), channel_id=1, source_target_pairs={{0,3},{1,0},{2,1},{3,2},{4,7},{5,4},{6,5},{7,6},{8,11},{9,8},{10,9... | collective-permute-start | bytes 1544 | tf_op jit(solution)/shard_map/ppermute | solution.py:242
  126.5 4.8 %collective-permute-start.29 = (f32[1,128]{1,0:T(1,128)S(1)}, f32[1,128]{1,0:T(1,128)S(1)}, u32[]{:S(2)}, u32[]{:S(2)}) collective-permute-start(f32[1,128]{1,0:T(1,128)S(1)} %get-tuple-element.75), channel_id=1, source_target_pairs={{0,1},{1,2},{2,3},{3,0},{4,5},{5,6},{6,7},{7,4},{8,9},{9,10},{10,1... | collective-permute-start | bytes 1544 | tf_op jit(solution)/shard_map/ppermute | solution.py:242
  127.6 5.0 %collective-permute-start.28 = (f32[1,128]{1,0:T(1,128)S(1)}, f32[1,128]{1,0:T(1,128)S(1)}, u32[]{:S(2)}, u32[]{:S(2)}) collective-permute-start(f32[1,128]{1,0:T(1,128)S(1)} %get-tuple-element.75), channel_id=1, source_target_pairs={{0,2},{1,3},{2,0},{3,1},{4,6},{5,7},{6,4},{7,5},{8,10},{9,11},{10,... | collective-permute-start | bytes 1544 | tf_op jit(solution)/shard_map/ppermute | solution.py:242
  (5 other events, 142.1 us)

commit v3 on v2

--- a/solution.py
+++ b/solution.py
@@ -137,8 +137,8 @@
     return pl.ds(pl.multiple_of(block * width, width), width)
 
 
-def held_shards(refs):
-    return [jnp.concatenate([refs[at][...], refs[at + 1][...]], axis=0) for at in range(0, len(refs), 2)]
+def held(own, other):
+    return jnp.concatenate([own[...], other[...]], axis=0)
 
 
 def write_shards(values, refs):
@@ -148,14 +148,33 @@
         refs[2 * at + 1][...] = value[half:]
 
 
-def forward_kernel(parts, *refs):
-    shards, (wg, wu, wd, gate_ref, up_ref, gated_ref), out = refs[:8], refs[8:14], refs[14:]
-    places = blocks(parts)
+def first_x_kernel(parts, own, own_other, behind, behind_other, wg, wu, wd, gate_ref, up_ref):
     gate, up = 0.0, 0.0
-    for block, x in zip(places, held_shards(shards)):
+    for block, mine, other in zip(blocks(parts), (own, behind), (own_other, behind_other)):
         at = columns(wg, block, parts)
+        x = held(mine, other)
         gate = gate + dot(x, wg[:, at], ((1,), (1,)))
         up = up + dot(x, wu[:, at], ((1,), (1,)))
+    gate_ref[...] = gate
+    up_ref[...] = up
+
+
+def first_s_kernel(parts, own, own_other, behind, behind_other, wd, grad_ref):
+    grad = 0.0
+    for block, mine, other in zip(blocks(parts), (own, behind), (own_other, behind_other)):
+        grad = grad + dot(held(mine, other), wd[:, columns(wd, block, parts)], ((1,), (1,)))
+    grad_ref[...] = grad
+
+
+def forward_kernel(parts, *refs):
+    shards, (wg, wu, wd, gate_in, up_in, gate_ref, up_ref, gated_ref), out = refs[:4], refs[4:12], refs[12:]
+    places = blocks(parts)
+    gate, up = gate_in[...], up_in[...]
+    for at in range(2):
+        cut = columns(wg, places[2 + at], parts)
+        x = held(shards[2 * at], shards[2 * at + 1])
+        gate = gate + dot(x, wg[:, cut], ((1,), (1,)))
+        up = up + dot(x, wu[:, cut], ((1,), (1,)))
     gate_ref[...] = gate
     up_ref[...] = up
     gated = (gate * (1.0 / (1.0 + jnp.exp(-gate))) * up).astype(BF16)
@@ -164,11 +183,12 @@
 
 
 def backward_kernel(parts, *refs):
-    shards, (wg, wu, wd, gate_ref, up_ref, ggp_ref, gup_ref), dx = refs[:8], refs[8:15], refs[15:]
+    shards, (wg, wu, wd, gate_ref, up_ref, grad_in, ggp_ref, gup_ref), dx = refs[:4], refs[4:12], refs[12:]
     places = blocks(parts)
-    grad = 0.0
-    for block, s in zip(places, held_shards(shards)):
-        grad = grad + dot(s, wd[:, columns(wd, block, parts)], ((1,), (1,)))
+    grad = grad_in[...]
+    for at in range(2):
+        cut = columns(wd, places[2 + at], parts)
+        grad = grad + dot(held(shards[2 * at], shards[2 * at + 1]), wd[:, cut], ((1,), (1,)))
     gate = gate_ref[...]
     sigmoid = 1.0 / (1.0 + jnp.exp(-gate))
     ggp = (grad * up_ref[...] * sigmoid * (1.0 + gate * (1.0 - sigmoid))).astype(BF16)
@@ -185,8 +205,9 @@
 def weights_kernel(parts, *refs):
     x_shards, s_shards, (ggp_ref, gup_ref, gated_ref, gwg, gwu, gwd) = refs[:8], refs[8:16], refs[16:]
     rows = ((0,), (0,))
-    for block, x, s in zip(blocks(parts), held_shards(x_shards), held_shards(s_shards)):
+    for step, block in enumerate(blocks(parts)):
         at = columns(gwg, block, parts)
+        x, s = (held(side[2 * step], side[2 * step + 1]) for side in (x_shards, s_shards))
         gwg[:, at] = dot(ggp_ref[...], x, rows).astype(BF16)
         gwu[:, at] = dot(gup_ref[...], x, rows).astype(BF16)
         gwd[:, at] = dot(gated_ref[...], s, rows).astype(BF16)
@@ -257,11 +278,15 @@
     return lax.optimization_barrier((value, *first))[0]
 
 
-def summed(own, own_other, behind, behind_other, ahead, ahead_other, opposite, opposite_other):
-    tail = ring(add(opposite, swap_cores(opposite_other)))
-    came_other = ring(add(ahead_other, swap_cores(behind)))
-    came = ring(add(ahead, swap_cores(behind_other), tail))
-    return own, came, swap_cores(add(own_other, came_other))
+def ring_inputs(own, own_other, behind, behind_other, ahead, ahead_other, opposite, opposite_other):
+    return add(opposite, swap_cores(opposite_other)), add(ahead_other, swap_cores(behind))
+
+
+def summed(terms, tail, other):
+    own, own_other, _, behind_other, ahead, *_ = terms
+    came_other = ring(other)
+    last = add(ahead, swap_cores(behind_other), ring(tail))
+    return (own, ring(last), swap_cores(add(own_other, came_other))), last
 
 
 def over_yz(packed):
@@ -277,11 +302,10 @@
     ids_row, probs_row = expert_ids.reshape(1, tokens), probs.reshape(1, tokens)
     x_own, s_own = unpack(over_yz(send(ids_row, probs_row, hidden_states, cotangent)))
     x_other, s_other = swap_cores(x_own), swap_cores(s_own)
-    x_behind = ring(x_own)
-    x_behind_other = ring(x_other)
-    x_opposite = ring(x_behind)
-    x_shards = (x_own, x_other, x_behind, x_behind_other)
-    x_shards += (swap_cores(x_behind_other), swap_cores(x_behind), x_opposite, swap_cores(x_opposite))
+    x_behind, x_behind_other = ring(x_own), ring(x_other)
+    s_behind, s_behind_other = ring(s_own), ring(s_other)
+    x_opposite, s_opposite = ring(x_behind), ring(s_behind)
+    x_first, s_first = (x_own, x_other, x_behind, x_behind_other), (s_own, s_other, s_behind, s_behind_other)
     slots, width = x_own.shape
     pair = 2 * slots
     act = jax.ShapeDtypeStruct((pair, hidden_rows), F32)
@@ -290,30 +314,27 @@
     weight = jax.ShapeDtypeStruct(w_gate.shape, BF16)
     product = 2 * pair * hidden_rows * model_width
     moved = 2 * hidden_rows * model_width
+    weights = (w_gate, w_up, w_down)
+    waited = after(x_behind_other, s_behind)
+    gate, up = kernel_call(functools.partial(first_x_kernel, parts), (act, act), product, 3 * moved)(
+        *x_first[:3], waited, *weights
+    )
+    grad = kernel_call(functools.partial(first_s_kernel, parts), act, product // 2, moved)(*s_first, w_down)
+    x_rest = (swap_cores(x_behind_other), swap_cores(x_behind), x_opposite, swap_cores(after(x_opposite, gate, grad)))
+    s_rest = (swap_cores(s_behind_other), swap_cores(s_behind), s_opposite, swap_cores(after(s_opposite, grad)))
     gate, up, gated, *out = kernel_call(
-        functools.partial(forward_kernel, parts), (act, act, act16) + sums, 3 * product, 6 * moved
-    )(*x_shards, w_gate, w_up, w_down)
-    s_behind = ring(s_own)
-    s_behind_other = ring(after(s_other, x_behind))
-    s_opposite = ring(s_behind)
-    s_shards = (s_own, s_other, s_behind, s_behind_other)
-    s_shards += tuple(
-        swap_cores(after(value, gate)) for value in (s_behind_other, s_behind, s_opposite)
+        functools.partial(forward_kernel, parts), (act, act, act16) + sums, 2 * product, 5 * moved
+    )(*x_rest, *weights, gate, up)
+    out_tail, out_other = ring_inputs(*out)
+    ggp, gup, *dx = kernel_call(
+        functools.partial(backward_kernel, parts), (act16, act16) + sums, 5 * product // 2, 5 * moved
+    )(*s_rest, *weights, gate, up, grad)
+    out_sum, _ = summed(out, out_tail, out_other)
+    dx_sum, last = summed(dx, *ring_inputs(*dx))
+    grads = kernel_call(functools.partial(weights_kernel, parts), (weight, weight, weight), 3 * product, 6 * moved)(
+        *x_first, *x_rest, *s_first, *s_rest, after(ggp, last), gup, gated
     )
-    s_shards = s_shards[:6] + (s_opposite, s_shards[6])
-    ggp, gup, *dx = kernel_call(
-        functools.partial(backward_kernel, parts), (act16, act16) + sums, 3 * product, 6 * moved
-    )(*s_shards, w_gate, w_up, w_down, gate, up)
-    out_sum = summed(*out)
-    own, own_other, behind, behind_other, ahead, ahead_other, opposite, opposite_other = dx
-    tail = ring(add(opposite, swap_cores(opposite_other)))
-    came_other = ring(add(ahead_other, swap_cores(behind)))
-    last = add(ahead, swap_cores(behind_other), tail)
-    came = ring(last)
-    grads = kernel_call(functools.partial(weights_kernel, parts), (weight, weight, weight), 3 * product, 6 * moved)(
-        *x_shards, *s_shards, after(ggp, last), gup, gated
-    )
-    dx_sum = (own, after(came, grads[0]), swap_cores(add(own_other, came_other)))
+    dx_sum = (dx_sum[0], after(dx_sum[1], grads[0]), dx_sum[2])
     packed = over_yz(pack_return(*out_sum, *dx_sum))
     wide = jax.ShapeDtypeStruct(hidden_states.shape, BF16)
     row = jax.ShapeDtypeStruct((1, tokens), F32)

time: 133 us -> 129 us (0.970)
  waiting for transfers between devices: 40.8 us -> 33.7 us
  starting transfers between devices: 14.3 us -> 18.5 us
  blocking collectives: 57.3 us -> 55.2 us
    ppermute x12, waiting for transfers between devices: 36.3 us -> 31.1 us  [ring(): return lax.ppermute(value, ('core', 'mp'), pairs)]
    ppermute x12, starting transfers between devices: 7.65 us -> 9.98 us  [ring(): return lax.ppermute(value, ('core', 'mp'), pairs)]
    all_to_all x2, blocking collectives: 57.3 us -> 55.2 us  [over_yz(): lax.all_to_all(split, ('y', 'z'), 0, 0, tiled=True).reshape(packed.shape)]
    ppermute x19, waiting for transfers between devices: 4.49 us -> 2.63 us  [shift(): lax.ppermute(value, axis, [(i, (i + step) % count) for i in range(count)])]
    ppermute x19, starting transfers between devices: 6.68 us -> 8.49 us  [shift(): lax.ppermute(value, axis, [(i, (i + step) % count) for i in range(count)])]
    pallas_call x5 -> x7, Pallas kernels: 11.5 us -> 11.2 us  [call(): pl.pallas_call(body, name=getattr(body, 'func', body).__name__, out_shape...]
  transfers between devices with their start and end apart: 31 -> 31, of which waited for: 15 -> 14; matrix products, arithmetic and copies ran while one was open for 1% -> 1% of each run, Pallas kernels for 9% -> 9%
where the time goes in v3:
time: 129 us; the launch traced here: 128 us
  blocking collectives  55.2 us (43%)
  waiting for transfers between devices  33.7 us (26%)
  starting transfers between devices  18.5 us (14%)
  Pallas kernels  16.7 us (13%)
  local copies, waits for them, and re-layouts  1.44 us (1%)
  other arithmetic  1.41 us (1%)
    all_to_all x2, blocking collectives, over_yz(): lax.all_to_all(split, ('y', 'z'), 0, 0, tiled=True).reshape(packed.shape)  55.2 us
    ppermute x12, waiting for transfers between devices, ring(): return lax.ppermute(value, ('core', 'mp'), pairs)  31.1 us
    pallas_call x7, Pallas kernels, call(): pl.pallas_call(body, name=getattr(body, 'func', body).__name__, out_shape...  11.2 us
    ppermute x12, starting transfers between devices, ring(): return lax.ppermute(value, ('core', 'mp'), pairs)  9.98 us
    ppermute x19, starting transfers between devices, shift(): lax.ppermute(value, axis, [(i, (i + step) % count) for i in range(count)])  8.49 us
    pallas_call x1, Pallas kernels, send(): pl.pallas_call(send_kernel, name='send', out_shape=jax.ShapeDtypeStruct((...  3.08 us
    ppermute x19, waiting for transfers between devices, shift(): lax.ppermute(value, axis, [(i, (i + step) % count) for i in range(count)])  2.63 us
  transfers between devices with their start and end apart: 31, of which 14 were waited for; matrix products, arithmetic and copies ran while one was open for 1% of the time, Pallas kernels for 9%

profile of v3, /device:TPU:32, one launch (start us, length us, event | category | flops | bytes accessed | tf_op | source)
XLA Modules:
  0.0 127.9 jit_solution(11188835958683079325)
XLA Ops:
  0.7 3.1 %send.1 = bf16[2560,128]{1,0:T(8,128)(2,1)} custom-call(s32[1,128]{1,0:T(1,128)} %bitcast.12, bf16[1,128]{1,0:T(2,128)(2,1)} %bitcast.15, bf16[128,1024]{1,0:T(8,128)(2,1)} %hidden_hbm.1, bf16[128,1024]{1,0:T(8,128)(2,1)} %cotangent_ref.1), custom_call_target="tpu_custom_call" | custom-call | tf_op jit(solution)/shard_map/send/pallas_call | solution.py:109
  3.7 31.6 %all_to_all.10 = bf16[32,80,128]{2,1,0:T(8,128)(2,1)S(1)} all-to-all(bf16[32,80,128]{2,1,0:T(8,128)(2,1)} %bitcast.17), channel_id=1, replica_groups=mesh['y'=4,'z'=8,'core'=2,'mp'=4] {'y','z'}, dimensions={0} | all-to-all | bytes 1310720 | tf_op jit(solution)/shard_map/all_to_all | solution.py:295
  36.5 1.5 %collective-permute-start.3 = (bf16[160,1024]{1,0:T(8,128)(2,1)S(1)}, bf16[160,1024]{1,0:T(8,128)(2,1)S(1)}, u32[]{:S(2)}, u32[]{:S(2)}) collective-permute-start(bf16[160,1024]{1,0:T(8,128)(2,1)S(1)} %get-tuple-element.43.own.refs_0_), channel_id=1, source_target_pairs={{0,1},{1,2},{2,3},{3,0},{4,7},{5,4},{6,5},{7,6},{8,9},{9,10},{10,1... | collective-permute-start | bytes 983048 | tf_op jit(solution)/shard_map/ppermute | solution.py:274
  38.0 1.5 %collective-permute-start.6 = (bf16[160,1024]{1,0:T(8,128)(2,1)S(1)}, bf16[160,1024]{1,0:T(8,128)(2,1)S(1)}, u32[]{:S(2)}, u32[]{:S(2)}) collective-permute-start(bf16[160,1024]{1,0:T(8,128)(2,1)S(1)} %get-tuple-element.44.own.refs_8_), channel_id=1, source_target_pairs={{0,1},{1,2},{2,3},{3,0},{4,7},{5,4},{6,5},{7,6},{8,9},{9,10},{10,1... | collective-permute-start | bytes 983048 | tf_op jit(solution)/shard_map/ppermute | solution.py:274
  39.5 1.2 collective-permute-start.1
  41.1 3.6 %collective-permute-done.3.behind.refs_2_ = bf16[160,1024]{1,0:T(8,128)(2,1)S(1)} collective-permute-done((bf16[160,1024]{1,0:T(8,128)(2,1)S(1)}, bf16[160,1024]{1,0:T(8,128)(2,1)S(1)}, u32[]{:S(2)}, u32[]{:S(2)}) %collective-permute-start.3) | collective-permute-done | bytes 327712 | tf_op jit(solution)/shard_map/ppermute | solution.py:274
  45.0 1.1 collective-permute-start.4
  46.2 2.1 %collective-permute-done.6.behind.refs_10_ = bf16[160,1024]{1,0:T(8,128)(2,1)S(1)} collective-permute-done((bf16[160,1024]{1,0:T(8,128)(2,1)S(1)}, bf16[160,1024]{1,0:T(8,128)(2,1)S(1)}, u32[]{:S(2)}, u32[]{:S(2)}) %collective-permute-start.6) | collective-permute-done | bytes 327712 | tf_op jit(solution)/shard_map/ppermute | solution.py:274
  48.5 3.2 %collective-permute-done.1.behind_other.refs_3_ = bf16[160,1024]{1,0:T(8,128)(2,1)S(1)} collective-permute-done((bf16[160,1024]{1,0:T(8,128)(2,1)S(1)}, bf16[160,1024]{1,0:T(8,128)(2,1)S(1)}, u32[]{:S(2)}, u32[]{:S(2)}) %collective-permute-start.1) | collective-permute-done | bytes 327712 | tf_op jit(solution)/shard_map/ppermute | solution.py:274
  51.8 1.4 %copy-done.2 = bf16[192,4096]{1,0:T(8,128)(2,1)S(1)} copy-done((bf16[192,4096]{1,0:T(8,128)(2,1)S(1)}, bf16[192,4096]{1,0:T(8,128)(2,1)}, u32[]{:S(2)}) %copy-start.2) | copy-done | bytes 1572888
  53.2 0.9 first_x_kernel.1
  54.1 1.2 collective-permute-done.8.behind_other.refs_11_
  55.8 3.0 %collective-permute-done.5.refs_2_.refs_6_ = bf16[160,1024]{1,0:T(8,128)(2,1)S(1)} collective-permute-done((bf16[160,1024]{1,0:T(8,128)(2,1)S(1)}, bf16[160,1024]{1,0:T(8,128)(2,1)S(1)}, u32[]{:S(2)}, u32[]{:S(2)}) %collective-permute-start.5) | collective-permute-done | bytes 327712 | tf_op jit(solution)/shard_map/ppermute | solution.py:274
  59.3 3.0 %collective-permute-done.19.refs_2_.refs_14_ = bf16[160,1024]{1,0:T(8,128)(2,1)S(1)} collective-permute-done((bf16[160,1024]{1,0:T(8,128)(2,1)S(1)}, bf16[160,1024]{1,0:T(8,128)(2,1)S(1)}, u32[]{:S(2)}, u32[]{:S(2)}) %collective-permute-start.19) | collective-permute-done | bytes 327712 | tf_op jit(solution)/shard_map/ppermute | solution.py:274
  62.8 1.7 %forward_kernel.1 = (f32[320,192]{1,0:T(8,128)S(1)}, f32[320,192]{1,0:T(8,128)S(1)}, bf16[320,192]{1,0:T(8,128)(2,1)S(1)}, bf16[160,1024]{1,0:T(8,128)(2,1)S(1)}...) custom-call(bf16[160,1024]{1,0:T(8,128)(2,1)S(1)} %collective-permut, ...), custom_call_target="tpu_custom_call" | custom-call | flops 1006632960 | bytes 7864320 | tf_op jit(solution)/shard_map/forward_kernel/pallas_call | solution.py:27
  65.2 2.7 %backward_kernel.1 = (bf16[320,192]{1,0:T(8,128)(2,1)S(1)}, bf16[320,192]{1,0:T(8,128)(2,1)S(1)}, bf16[160,1024]{1,0:T(8,128)(2,1)S(1)}, bf16[160,1024]{1,0:T(8,...) custom-call(bf16[160,1024]{1,0:T(8,128)(2,1)S(1)} %collective-permut, ...), custom_call_target="tpu_custom_call" | custom-call | flops 1258291200 | bytes 7864320 | tf_op jit(solution)/shard_map/backward_kernel/pallas_call | solution.py:27
  69.5 0.6 collective-permute-done.22
  70.1 1.0 collective-permute-start.15
  71.2 1.3 collective-permute-start.23
  72.6 1.8 %collective-permute-start.26 = (bf16[160,1024]{1,0:T(8,128)(2,1)S(1)}, bf16[160,1024]{1,0:T(8,128)(2,1)S(1)}, u32[]{:S(2)}, u32[]{:S(2)}) collective-permute-start(bf16[160,1024]{1,0:T(8,128)(2,1)S(1)} %add_convert_fusion.1), channel_id=1, source_target_pairs={{0,1},{1,2},{2,3},{3,0},{4,7},{5,4},{6,5},{7,6},{8,9},{9,10},{10,1... | collective-permute-start | bytes 983048 | tf_op jit(solution)/shard_map/ppermute | solution.py:274
  74.3 3.1 %collective-permute-done.12 = bf16[160,1024]{1,0:T(8,128)(2,1)S(1)} collective-permute-done((bf16[160,1024]{1,0:T(8,128)(2,1)S(1)}, bf16[160,1024]{1,0:T(8,128)(2,1)S(1)}, u32[]{:S(2)}, u32[]{:S(2)}) %collective-permute-start.12) | collective-permute-done | bytes 327712 | tf_op jit(solution)/shard_map/ppermute | solution.py:274
  77.6 3.3 %collective-permute-done.15 = bf16[160,1024]{1,0:T(8,128)(2,1)S(1)} collective-permute-done((bf16[160,1024]{1,0:T(8,128)(2,1)S(1)}, bf16[160,1024]{1,0:T(8,128)(2,1)S(1)}, u32[]{:S(2)}, u32[]{:S(2)}) %collective-permute-start.15) | collective-permute-done | bytes 327712 | tf_op jit(solution)/shard_map/ppermute | solution.py:274
  81.1 3.3 %collective-permute-done.23 = bf16[160,1024]{1,0:T(8,128)(2,1)S(1)} collective-permute-done((bf16[160,1024]{1,0:T(8,128)(2,1)S(1)}, bf16[160,1024]{1,0:T(8,128)(2,1)S(1)}, u32[]{:S(2)}, u32[]{:S(2)}) %collective-permute-start.23) | collective-permute-done | bytes 327712 | tf_op jit(solution)/shard_map/ppermute | solution.py:274
  84.9 3.0 %collective-permute-done.26 = bf16[160,1024]{1,0:T(8,128)(2,1)S(1)} collective-permute-done((bf16[160,1024]{1,0:T(8,128)(2,1)S(1)}, bf16[160,1024]{1,0:T(8,128)(2,1)S(1)}, u32[]{:S(2)}, u32[]{:S(2)}) %collective-permute-start.26) | collective-permute-done | bytes 327712 | tf_op jit(solution)/shard_map/ppermute | solution.py:274
  88.1 4.5 %weights_kernel.1 = (bf16[192,4096]{1,0:T(8,128)(2,1)}, bf16[192,4096]{1,0:T(8,128)(2,1)}, bf16[192,4096]{1,0:T(8,128)(2,1)}) custom-call(bf16[160,1024]{1,0:T(8,128)(2,1)S(1)} %get-tuple-element.43.own.refs_0_, bf16[160,1024]{1,0:T(8,128)(2,1)S(1)} %collective-permute-done.own_other.refs_1_, bf16[160,1024]{1,0:T(8,128)(2,1)S(1)} %collective-permute-done.3.behind.refs_2_, ...), custom_call_target="tpu_custom_call" | custom-call | flops 1509949440 | bytes 9437184 | tf_op jit(solution)/shard_map/weights_kernel/pallas_call | solution.py:27
  92.6 2.3 %collective-permute-done.24.refs_4_ = bf16[160,1024]{1,0:T(8,128)(2,1)S(1)} collective-permute-done((bf16[160,1024]{1,0:T(8,128)(2,1)S(1)}, bf16[160,1024]{1,0:T(8,128)(2,1)S(1)}, u32[]{:S(2)}, u32[]{:S(2)}) %collective-permute-start.24) | collective-permute-done | bytes 327712 | tf_op jit(solution)/shard_map/ppermute | solution.py:274
  95.5 23.6 %all_to_all.11 = bf16[32,80,128]{2,1,0:T(8,128)(2,1)S(1)} all-to-all(bf16[32,80,128]{2,1,0:T(8,128)(2,1)S(1)} %bitcast.10), channel_id=1, replica_groups=mesh['y'=4,'z'=8,'core'=2,'mp'=4] {'y','z'}, dimensions={0} | all-to-all | bytes 1310720 | tf_op jit(solution)/shard_map/all_to_all | solution.py:295
  119.2 0.9 home_terms.1
  120.0 2.3 %collective-permute-start.30 = (f32[1,128]{1,0:T(1,128)S(1)}, f32[1,128]{1,0:T(1,128)S(1)}, u32[]{:S(2)}, u32[]{:S(2)}) collective-permute-start(f32[1,128]{1,0:T(1,128)S(1)} %get-tuple-element.77), channel_id=1, source_target_pairs={{0,3},{1,0},{2,1},{3,2},{4,7},{5,4},{6,5},{7,6},{8,11},{9,8},{10,9... | collective-permute-start | bytes 1544 | tf_op jit(solution)/shard_map/ppermute | solution.py:263
  122.3 1.6 %collective-permute-start.28 = (f32[1,128]{1,0:T(1,128)S(1)}, f32[1,128]{1,0:T(1,128)S(1)}, u32[]{:S(2)}, u32[]{:S(2)}) collective-permute-start(f32[1,128]{1,0:T(1,128)S(1)} %get-tuple-element.77), channel_id=1, source_target_pairs={{0,2},{1,3},{2,0},{3,1},{4,6},{5,7},{6,4},{7,5},{8,10},{9,11},{10,... | collective-permute-start | bytes 1544 | tf_op jit(solution)/shard_map/ppermute | solution.py:263
  123.9 1.5 %home_rest.1 = (bf16[128,1024]{1,0:T(8,128)(2,1)}, bf16[128,1024]{1,0:T(8,128)(2,1)}) custom-call(s32[1,128]{1,0:T(1,128)S(1)} %bitcast.14, bf16[1,128]{1,0:T(2,128)(2,1)S(1)} %bitcast.16, f32[128,1024]{1,0:T(8,128)S(1)} %get-tuple-element.74.out_ref, bf16[2560,128]{1,0:T(8,128)(2,1)S(1)} %bitcast.9), custom_call_target="tpu_custom_call" | custom-call | tf_op jit(solution)/shard_map/home_rest/pallas_call | solution.py:251
  125.4 1.7 %collective-permute-done.29 = f32[1,128]{1,0:T(1,128)S(1)} collective-permute-done((f32[1,128]{1,0:T(1,128)S(1)}, f32[1,128]{1,0:T(1,128)S(1)}, u32[]{:S(2)}, u32[]{:S(2)}) %collective-permute-start.29) | collective-permute-done | bytes 544 | tf_op jit(solution)/shard_map/ppermute | solution.py:263
  (65 shorter events, 8.7 us)
Async XLA Ops:
  0.6 51.1 %copy-start = (bf16[192,4096]{1,0:T(8,128)(2,1)S(1)}, bf16[192,4096]{1,0:T(8,128)(2,1)}, u32[]{:S(2)}) copy-start(bf16[192,4096]{1,0:T(8,128)(2,1)} %refs_6_.3) | copy-start | bytes 4718596
  35.9 3.6 %collective-permute-start = (bf16[160,1024]{1,0:T(8,128)(2,1)S(1)}, bf16[160,1024]{1,0:T(8,128)(2,1)S(1)}, u32[]{:S(2)}, u32[]{:S(2)}) collective-permute-start(bf16[160,1024]{1,0:T(8,128)(2,1)S(1)} %get-tuple-element.43.own.refs_0_), channel_id=1, source_target_pairs={{0,4},{4,0},{1,5},{5,1},{2,6},{6,2},{3,7},{7,3},{8,12},{12,8},{9,1... | collective-permute-start | bytes 983048 | tf_op jit(solution)/shard_map/ppermute | solution.py:263
  36.0 4.7 %collective-permute-start.7 = (bf16[160,1024]{1,0:T(8,128)(2,1)S(1)}, bf16[160,1024]{1,0:T(8,128)(2,1)S(1)}, u32[]{:S(2)}, u32[]{:S(2)}) collective-permute-start(bf16[160,1024]{1,0:T(8,128)(2,1)S(1)} %get-tuple-element.44.own.refs_8_), channel_id=1, source_target_pairs={{0,4},{4,0},{1,5},{5,1},{2,6},{6,2},{3,7},{7,3},{8,12},{12,8},{9,1... | collective-permute-start | bytes 983048 | tf_op jit(solution)/shard_map/ppermute | solution.py:263
  36.5 8.3 %collective-permute-start.3 = (bf16[160,1024]{1,0:T(8,128)(2,1)S(1)}, bf16[160,1024]{1,0:T(8,128)(2,1)S(1)}, u32[]{:S(2)}, u32[]{:S(2)}) collective-permute-start(bf16[160,1024]{1,0:T(8,128)(2,1)S(1)} %get-tuple-element.43.own.refs_0_), channel_id=1, source_target_pairs={{0,1},{1,2},{2,3},{3,0},{4,7},{5,4},{6,5},{7,6},{8,9},{9,10},{10,1... | collective-permute-start | bytes 983048 | tf_op jit(solution)/shard_map/ppermute | solution.py:274
  38.0 10.3 %collective-permute-start.6 = (bf16[160,1024]{1,0:T(8,128)(2,1)S(1)}, bf16[160,1024]{1,0:T(8,128)(2,1)S(1)}, u32[]{:S(2)}, u32[]{:S(2)}) collective-permute-start(bf16[160,1024]{1,0:T(8,128)(2,1)S(1)} %get-tuple-element.44.own.refs_8_), channel_id=1, source_target_pairs={{0,1},{1,2},{2,3},{3,0},{4,7},{5,4},{6,5},{7,6},{8,9},{9,10},{10,1... | collective-permute-start | bytes 983048 | tf_op jit(solution)/shard_map/ppermute | solution.py:274
  39.5 12.3 %collective-permute-start.1 = (bf16[160,1024]{1,0:T(8,128)(2,1)S(1)}, bf16[160,1024]{1,0:T(8,128)(2,1)S(1)}, u32[]{:S(2)}, u32[]{:S(2)}) collective-permute-start(bf16[160,1024]{1,0:T(8,128)(2,1)S(1)} %collective-permute-done.own_other.refs_1_), channel_id=1, source_target_pairs={{0,1},{1,2},{2,3},{3,0},{4,7},{5,4},{6,5},{7,6},{8,9},{9,10},{10,1... | collective-permute-start | bytes 983048 | tf_op jit(solution)/shard_map/ppermute | solution.py:274
  40.7 14.6 %collective-permute-start.8 = (bf16[160,1024]{1,0:T(8,128)(2,1)S(1)}, bf16[160,1024]{1,0:T(8,128)(2,1)S(1)}, u32[]{:S(2)}, u32[]{:S(2)}) collective-permute-start(bf16[160,1024]{1,0:T(8,128)(2,1)S(1)} %collective-permute-done.7.own_other.refs_9_), channel_id=1, source_target_pairs={{0,1},{1,2},{2,3},{3,0},{4,7},{5,4},{6,5},{7,6},{8,9},{9,10},{10,1... | collective-permute-start | bytes 983048 | tf_op jit(solution)/shard_map/ppermute | solution.py:274
  44.8 14.0 %collective-permute-start.5 = (bf16[160,1024]{1,0:T(8,128)(2,1)S(1)}, bf16[160,1024]{1,0:T(8,128)(2,1)S(1)}, u32[]{:S(2)}, u32[]{:S(2)}) collective-permute-start(bf16[160,1024]{1,0:T(8,128)(2,1)S(1)} %collective-permute-done.3.behind.refs_2_), channel_id=1, source_target_pairs={{0,1},{1,2},{2,3},{3,0},{4,7},{5,4},{6,5},{7,6},{8,9},{9,10},{10,1... | collective-permute-start | bytes 983048 | tf_op jit(solution)/shard_map/ppermute | solution.py:274
  45.0 17.3 %collective-permute-start.4 = (bf16[160,1024]{1,0:T(8,128)(2,1)S(1)}, bf16[160,1024]{1,0:T(8,128)(2,1)S(1)}, u32[]{:S(2)}, u32[]{:S(2)}) collective-permute-start(bf16[160,1024]{1,0:T(8,128)(2,1)S(1)} %collective-permute-done.3.behind.refs_2_), channel_id=1, source_target_pairs={{0,4},{4,0},{1,5},{5,1},{2,6},{6,2},{3,7},{7,3},{8,12},{12,8},{9,1... | collective-permute-start | bytes 983048 | tf_op jit(solution)/shard_map/ppermute | solution.py:263
  48.3 14.0 %collective-permute-start.19 = (bf16[160,1024]{1,0:T(8,128)(2,1)S(1)}, bf16[160,1024]{1,0:T(8,128)(2,1)S(1)}, u32[]{:S(2)}, u32[]{:S(2)}) collective-permute-start(bf16[160,1024]{1,0:T(8,128)(2,1)S(1)} %collective-permute-done.6.behind.refs_10_), channel_id=1, source_target_pairs={{0,1},{1,2},{2,3},{3,0},{4,7},{5,4},{6,5},{7,6},{8,9},{9,10},{10,1... | collective-permute-start | bytes 983048 | tf_op jit(solution)/shard_map/ppermute | solution.py:274
  58.8 4.0 %collective-permute-start.2 = (bf16[160,1024]{1,0:T(8,128)(2,1)S(1)}, bf16[160,1024]{1,0:T(8,128)(2,1)S(1)}, u32[]{:S(2)}, u32[]{:S(2)}) collective-permute-start(bf16[160,1024]{1,0:T(8,128)(2,1)S(1)} %collective-permute-done.1.behind_other.refs_3_), channel_id=1, source_target_pairs={{0,4},{4,0},{1,5},{5,1},{2,6},{6,2},{3,7},{7,3},{8,12},{12,8},{9,1... | collective-permute-start | bytes 983048 | tf_op jit(solution)/shard_map/ppermute | solution.py:263
  58.8 4.0 %collective-permute-start.9 = (bf16[160,1024]{1,0:T(8,128)(2,1)S(1)}, bf16[160,1024]{1,0:T(8,128)(2,1)S(1)}, u32[]{:S(2)}, u32[]{:S(2)}) collective-permute-start(bf16[160,1024]{1,0:T(8,128)(2,1)S(1)} %collective-permute-done.5.refs_2_.refs_6_), channel_id=1, source_target_pairs={{0,4},{4,0},{1,5},{5,1},{2,6},{6,2},{3,7},{7,3},{8,12},{12,8},{9,1... | collective-permute-start | bytes 983048 | tf_op jit(solution)/shard_map/ppermute | solution.py:263
  59.3 5.8 %collective-permute-start.18 = (bf16[160,1024]{1,0:T(8,128)(2,1)S(1)}, bf16[160,1024]{1,0:T(8,128)(2,1)S(1)}, u32[]{:S(2)}, u32[]{:S(2)}) collective-permute-start(bf16[160,1024]{1,0:T(8,128)(2,1)S(1)} %collective-permute-done.6.behind.refs_10_), channel_id=1, source_target_pairs={{0,4},{4,0},{1,5},{5,1},{2,6},{6,2},{3,7},{7,3},{8,12},{12,8},{9,1... | collective-permute-start | bytes 983048 | tf_op jit(solution)/shard_map/ppermute | solution.py:263
  62.3 2.9 %collective-permute-start.17 = (bf16[160,1024]{1,0:T(8,128)(2,1)S(1)}, bf16[160,1024]{1,0:T(8,128)(2,1)S(1)}, u32[]{:S(2)}, u32[]{:S(2)}) collective-permute-start(bf16[160,1024]{1,0:T(8,128)(2,1)S(1)} %collective-permute-done.8.behind_other.refs_11_), channel_id=1, source_target_pairs={{0,4},{4,0},{1,5},{5,1},{2,6},{6,2},{3,7},{7,3},{8,12},{12,8},{9,1... | collective-permute-start | bytes 983048 | tf_op jit(solution)/shard_map/ppermute | solution.py:263
  62.3 2.9 %collective-permute-start.20 = (bf16[160,1024]{1,0:T(8,128)(2,1)S(1)}, bf16[160,1024]{1,0:T(8,128)(2,1)S(1)}, u32[]{:S(2)}, u32[]{:S(2)}) collective-permute-start(bf16[160,1024]{1,0:T(8,128)(2,1)S(1)} %collective-permute-done.19.refs_2_.refs_14_), channel_id=1, source_target_pairs={{0,4},{4,0},{1,5},{5,1},{2,6},{6,2},{3,7},{7,3},{8,12},{12,8},{9,1... | collective-permute-start | bytes 983048 | tf_op jit(solution)/shard_map/ppermute | solution.py:263
  64.5 4.0 %collective-permute-start.11 = (bf16[160,1024]{1,0:T(8,128)(2,1)S(1)}, bf16[160,1024]{1,0:T(8,128)(2,1)S(1)}, u32[]{:S(2)}, u32[]{:S(2)}) collective-permute-start(bf16[160,1024]{1,0:T(8,128)(2,1)S(1)} %get-tuple-element.53), channel_id=1, source_target_pairs={{0,4},{4,0},{1,5},{5,1},{2,6},{6,2},{3,7},{7,3},{8,12},{12,8},{9,1... | collective-permute-start | bytes 983048 | tf_op jit(solution)/shard_map/ppermute | solution.py:263
  64.6 7.9 %collective-permute-start.10 = (bf16[160,1024]{1,0:T(8,128)(2,1)S(1)}, bf16[160,1024]{1,0:T(8,128)(2,1)S(1)}, u32[]{:S(2)}, u32[]{:S(2)}) collective-permute-start(bf16[160,1024]{1,0:T(8,128)(2,1)S(1)} %get-tuple-element.51), channel_id=1, source_target_pairs={{0,4},{4,0},{1,5},{5,1},{2,6},{6,2},{3,7},{7,3},{8,12},{12,8},{9,1... | collective-permute-start | bytes 983048 | tf_op jit(solution)/shard_map/ppermute | solution.py:263
  65.1 3.9 %collective-permute-start.14 = (bf16[160,1024]{1,0:T(8,128)(2,1)S(1)}, bf16[160,1024]{1,0:T(8,128)(2,1)S(1)}, u32[]{:S(2)}, u32[]{:S(2)}) collective-permute-start(bf16[160,1024]{1,0:T(8,128)(2,1)S(1)} %get-tuple-element.56), channel_id=1, source_target_pairs={{0,4},{4,0},{1,5},{5,1},{2,6},{6,2},{3,7},{7,3},{8,12},{12,8},{9,1... | collective-permute-start | bytes 983048 | tf_op jit(solution)/shard_map/ppermute | solution.py:263
  67.9 13.2 %collective-permute-start.21 = (bf16[160,1024]{1,0:T(8,128)(2,1)S(1)}, bf16[160,1024]{1,0:T(8,128)(2,1)S(1)}, u32[]{:S(2)}, u32[]{:S(2)}) collective-permute-start(bf16[160,1024]{1,0:T(8,128)(2,1)S(1)} %get-tuple-element.62), channel_id=1, source_target_pairs={{0,4},{4,0},{1,5},{5,1},{2,6},{6,2},{3,7},{7,3},{8,12},{12,8},{9,1... | collective-permute-start | bytes 983048 | tf_op jit(solution)/shard_map/ppermute | solution.py:263
  68.4 1.7 %collective-permute-start.22 = (bf16[160,1024]{1,0:T(8,128)(2,1)S(1)}, bf16[160,1024]{1,0:T(8,128)(2,1)S(1)}, u32[]{:S(2)}, u32[]{:S(2)}) collective-permute-start(bf16[160,1024]{1,0:T(8,128)(2,1)S(1)} %get-tuple-element.64), channel_id=1, source_target_pairs={{0,4},{4,0},{1,5},{5,1},{2,6},{6,2},{3,7},{7,3},{8,12},{12,8},{9,1... | collective-permute-start | bytes 983048 | tf_op jit(solution)/shard_map/ppermute | solution.py:263
  68.5 2.7 %collective-permute-start.25 = (bf16[160,1024]{1,0:T(8,128)(2,1)S(1)}, bf16[160,1024]{1,0:T(8,128)(2,1)S(1)}, u32[]{:S(2)}, u32[]{:S(2)}) collective-permute-start(bf16[160,1024]{1,0:T(8,128)(2,1)S(1)} %get-tuple-element.73), channel_id=1, source_target_pairs={{0,4},{4,0},{1,5},{5,1},{2,6},{6,2},{3,7},{7,3},{8,12},{12,8},{9,1... | collective-permute-start | bytes 983048 | tf_op jit(solution)/shard_map/ppermute | solution.py:263
  69.0 8.4 %collective-permute-start.12 = (bf16[160,1024]{1,0:T(8,128)(2,1)S(1)}, bf16[160,1024]{1,0:T(8,128)(2,1)S(1)}, u32[]{:S(2)}, u32[]{:S(2)}) collective-permute-start(bf16[160,1024]{1,0:T(8,128)(2,1)S(1)} %add_convert_fusion.7), channel_id=1, source_target_pairs={{0,1},{1,2},{2,3},{3,0},{4,7},{5,4},{6,5},{7,6},{8,9},{9,10},{10,1... | collective-permute-start | bytes 983048 | tf_op jit(solution)/shard_map/ppermute | solution.py:274
  70.1 10.8 %collective-permute-start.15 = (bf16[160,1024]{1,0:T(8,128)(2,1)S(1)}, bf16[160,1024]{1,0:T(8,128)(2,1)S(1)}, u32[]{:S(2)}, u32[]{:S(2)}) collective-permute-start(bf16[160,1024]{1,0:T(8,128)(2,1)S(1)} %add_convert_fusion.5), channel_id=1, source_target_pairs={{0,1},{1,2},{2,3},{3,0},{4,7},{5,4},{6,5},{7,6},{8,9},{9,10},{10,1... | collective-permute-start | bytes 983048 | tf_op jit(solution)/shard_map/ppermute | solution.py:274
  71.2 13.2 %collective-permute-start.23 = (bf16[160,1024]{1,0:T(8,128)(2,1)S(1)}, bf16[160,1024]{1,0:T(8,128)(2,1)S(1)}, u32[]{:S(2)}, u32[]{:S(2)}) collective-permute-start(bf16[160,1024]{1,0:T(8,128)(2,1)S(1)} %add_convert_fusion.3), channel_id=1, source_target_pairs={{0,1},{1,2},{2,3},{3,0},{4,7},{5,4},{6,5},{7,6},{8,9},{9,10},{10,1... | collective-permute-start | bytes 983048 | tf_op jit(solution)/shard_map/ppermute | solution.py:274
  72.6 15.3 %collective-permute-start.26 = (bf16[160,1024]{1,0:T(8,128)(2,1)S(1)}, bf16[160,1024]{1,0:T(8,128)(2,1)S(1)}, u32[]{:S(2)}, u32[]{:S(2)}) collective-permute-start(bf16[160,1024]{1,0:T(8,128)(2,1)S(1)} %add_convert_fusion.1), channel_id=1, source_target_pairs={{0,1},{1,2},{2,3},{3,0},{4,7},{5,4},{6,5},{7,6},{8,9},{9,10},{10,1... | collective-permute-start | bytes 983048 | tf_op jit(solution)/shard_map/ppermute | solution.py:274
  77.5 17.4 %collective-permute-start.13 = (bf16[160,1024]{1,0:T(8,128)(2,1)S(1)}, bf16[160,1024]{1,0:T(8,128)(2,1)S(1)}, u32[]{:S(2)}, u32[]{:S(2)}) collective-permute-start(bf16[160,1024]{1,0:T(8,128)(2,1)S(1)} %add_convert_fusion.6), channel_id=1, source_target_pairs={{0,1},{1,2},{2,3},{3,0},{4,7},{5,4},{6,5},{7,6},{8,9},{9,10},{10,1... | collective-permute-start | bytes 983048 | tf_op jit(solution)/shard_map/ppermute | solution.py:274
  81.0 13.9 %collective-permute-start.16 = (bf16[160,1024]{1,0:T(8,128)(2,1)S(1)}, bf16[160,1024]{1,0:T(8,128)(2,1)S(1)}, u32[]{:S(2)}, u32[]{:S(2)}) collective-permute-start(bf16[160,1024]{1,0:T(8,128)(2,1)S(1)} %add_convert_fusion.4), channel_id=1, source_target_pairs={{0,4},{4,0},{1,5},{5,1},{2,6},{6,2},{3,7},{7,3},{8,12},{12,8},{9,1... | collective-permute-start | bytes 983048 | tf_op jit(solution)/shard_map/ppermute | solution.py:263
  84.6 10.4 %collective-permute-start.24 = (bf16[160,1024]{1,0:T(8,128)(2,1)S(1)}, bf16[160,1024]{1,0:T(8,128)(2,1)S(1)}, u32[]{:S(2)}, u32[]{:S(2)}) collective-permute-start(bf16[160,1024]{1,0:T(8,128)(2,1)S(1)} %add_convert_fusion.2), channel_id=1, source_target_pairs={{0,1},{1,2},{2,3},{3,0},{4,7},{5,4},{6,5},{7,6},{8,9},{9,10},{10,1... | collective-permute-start | bytes 983048 | tf_op jit(solution)/shard_map/ppermute | solution.py:274
  88.0 6.9 %collective-permute-start.27 = (bf16[160,1024]{1,0:T(8,128)(2,1)S(1)}, bf16[160,1024]{1,0:T(8,128)(2,1)S(1)}, u32[]{:S(2)}, u32[]{:S(2)}) collective-permute-start(bf16[160,1024]{1,0:T(8,128)(2,1)S(1)} %add_convert_fusion), channel_id=1, source_target_pairs={{0,4},{4,0},{1,5},{5,1},{2,6},{6,2},{3,7},{7,3},{8,12},{12,8},{9,1... | collective-permute-start | bytes 983048 | tf_op jit(solution)/shard_map/ppermute | solution.py:263
  120.0 5.4 %collective-permute-start.30 = (f32[1,128]{1,0:T(1,128)S(1)}, f32[1,128]{1,0:T(1,128)S(1)}, u32[]{:S(2)}, u32[]{:S(2)}) collective-permute-start(f32[1,128]{1,0:T(1,128)S(1)} %get-tuple-element.77), channel_id=1, source_target_pairs={{0,3},{1,0},{2,1},{3,2},{4,7},{5,4},{6,5},{7,6},{8,11},{9,8},{10,9... | collective-permute-start | bytes 1544 | tf_op jit(solution)/shard_map/ppermute | solution.py:263
  122.3 4.8 %collective-permute-start.29 = (f32[1,128]{1,0:T(1,128)S(1)}, f32[1,128]{1,0:T(1,128)S(1)}, u32[]{:S(2)}, u32[]{:S(2)}) collective-permute-start(f32[1,128]{1,0:T(1,128)S(1)} %get-tuple-element.77), channel_id=1, source_target_pairs={{0,1},{1,2},{2,3},{3,0},{4,5},{5,6},{6,7},{7,4},{8,9},{9,10},{10,1... | collective-permute-start | bytes 1544 | tf_op jit(solution)/shard_map/ppermute | solution.py:263
  122.3 5.0 %collective-permute-start.28 = (f32[1,128]{1,0:T(1,128)S(1)}, f32[1,128]{1,0:T(1,128)S(1)}, u32[]{:S(2)}, u32[]{:S(2)}) collective-permute-start(f32[1,128]{1,0:T(1,128)S(1)} %get-tuple-element.77), channel_id=1, source_target_pairs={{0,2},{1,3},{2,0},{3,1},{4,6},{5,7},{6,4},{7,5},{8,10},{9,11},{10,... | collective-permute-start | bytes 1544 | tf_op jit(solution)/shard_map/ppermute | solution.py:263
  (6 other events, 138.1 us)

commit v4 on v3

--- a/solution.py
+++ b/solution.py
@@ -9,6 +9,7 @@
 
 EXPERTS = 32
 CAP = 5
+ROOM = CAP + 1
 LANES = 128
 TILE = 16
 F32 = jnp.float32
@@ -64,7 +65,7 @@
                 wide[pl.ds(group * TILE, TILE), pl.ds(j * LANES, LANES)] = value[q : q + TILE]
 
 
-def token_slots(ids_row):
+def token_ranks(ids_row):
     tokens = ids_row.shape[1]
     expert = lax.broadcasted_iota(jnp.int32, (EXPERTS, tokens), 0)
     onehot = (expert == ids_row).astype(F32)
@@ -72,14 +73,12 @@
     token = lax.broadcasted_iota(jnp.int32, (tokens, tokens), 1)
     earlier = (before < token).astype(BF16)
     counts = dot(onehot.astype(BF16), earlier)
-    rank = jnp.sum(counts * onehot, axis=0, keepdims=True)
-    return ids_row * CAP + rank.astype(jnp.int32)
-
-
-def placement(ids_row):
-    tokens = ids_row.shape[1]
-    slot = lax.broadcasted_iota(jnp.int32, (EXPERTS * CAP, tokens), 0)
-    return (slot == token_slots(ids_row)).astype(BF16)
+    return jnp.sum(counts * onehot, axis=0, keepdims=True).astype(jnp.int32)
+
+
+def placement(ids_row, ranks, room):
+    slot = lax.broadcasted_iota(jnp.int32, (EXPERTS * room, ids_row.shape[1]), 0)
+    return (slot == ids_row * room + ranks).astype(BF16)
 
 
 def column(row):
@@ -96,7 +95,7 @@
     for copy in copies:
         copy.start()
     copies[0].wait()
-    select = placement(ids[...])
+    select = placement(ids[...], token_ranks(ids[...]), CAP)
     copies[2].wait()
     left = dot(select, hidden[...]).astype(BF16)
     copies[1].wait()
@@ -183,12 +182,14 @@
 
 
 def backward_kernel(parts, *refs):
-    shards, (wg, wu, wd, gate_ref, up_ref, grad_in, ggp_ref, gup_ref), dx = refs[:4], refs[4:12], refs[12:]
+    shards, (wg, wu, wd, gate_ref, up_ref, gated_ref, grad_in, ggp_ref, gup_ref), dx = refs[:4], refs[4:13], refs[13:]
     places = blocks(parts)
     grad = grad_in[...]
     for at in range(2):
         cut = columns(wd, places[2 + at], parts)
         grad = grad + dot(held(shards[2 * at], shards[2 * at + 1]), wd[:, cut], ((1,), (1,)))
+    terms = jnp.sum(grad * gated_ref[...].astype(F32), axis=1, keepdims=True)
+    terms = jnp.broadcast_to(terms, (terms.shape[0], LANES)).astype(BF16)
     gate = gate_ref[...]
     sigmoid = 1.0 / (1.0 + jnp.exp(-gate))
     ggp = (grad * up_ref[...] * sigmoid * (1.0 + gate * (1.0 - sigmoid))).astype(BF16)
@@ -198,7 +199,8 @@
     values = []
     for block in places:
         at = columns(wg, block, parts)
-        values.append((dot(ggp, wg[:, at]) + dot(gup, wu[:, at])).astype(BF16))
+        value = (dot(ggp, wg[:, at]) + dot(gup, wu[:, at])).astype(BF16)
+        values.append(jnp.concatenate([value, terms], axis=1))
     write_shards(values, dx)
 
 
@@ -220,42 +222,58 @@
     return value.astype(BF16)
 
 
+def slot_parts(shape, axis, room):
+    slot = lax.broadcasted_iota(jnp.int32, shape, axis)
+    expert = jnp.floor((slot.astype(F32) + 0.5) * (1.0 / room)).astype(jnp.int32)
+    return expert, slot - expert * room
+
+
 def return_kernel(*refs):
-    sums = []
-    for terms in (refs[:3], refs[3:6]):
-        sums.append(add(*(term[...] for term in terms)))
-    pack_rows(*sums, refs[6])
-
-
-def pack_return(*terms):
-    packed = jax.ShapeDtypeStruct((2 * terms[0].size // LANES, LANES), BF16)
-    return kernel_call(return_kernel, packed, 4 * packed.size * LANES, 8 * packed.size)(*terms)
-
-
-def home_terms_kernel(ids_ref, cotangent_ref, packed_ref, terms_ref, out_ref, wide):
-    unpack_rows(packed_ref, {0: wide})
-    out = dot(placement(ids_ref[...]), wide[...], ((0,), (0,)))
-    out_ref[...] = out
-    terms = jnp.sum(cotangent_ref[...].astype(F32) * out, axis=1, keepdims=True)
-    terms_ref[...] = jnp.transpose(jnp.broadcast_to(terms, (terms.shape[0], LANES)))[:1]
-
-
-def home_rest_kernel(ids_ref, probs_ref, out_ref, packed_ref, mixed_ref, hidden_ref, wide):
-    mixed_ref[...] = (column(probs_ref[...]) * out_ref[...]).astype(BF16)
-    unpack_rows(packed_ref, {1: wide})
-    hidden_ref[...] = dot(placement(ids_ref[...]), wide[...], ((0,), (0,))).astype(BF16)
-
-
-def home(body, name, out_shape, *args):
-    packed = args[-1]
+    out, dx, packed_ref = refs[:3], refs[3:6], refs[6]
+    width = out[0].shape[1]
+    slots, wide = EXPERTS * CAP, EXPERTS * ROOM
+    row_expert, row_place = slot_parts((wide, slots), 0, ROOM)
+    expert, place = slot_parts((wide, slots), 1, CAP)
+    same = row_expert == expert
+    spread = (same & (row_place == place)).astype(BF16)
+    last = (same & (row_place == CAP)).astype(BF16)
+    _, lane_place = slot_parts((slots, LANES), 0, CAP)
+    lane = lax.broadcasted_iota(jnp.int32, (slots, LANES), 1)
+    sums = add(*(term[...] for term in dx))
+    terms = jnp.where(lane_place == lane, sums[:, width:].astype(F32), 0.0).astype(BF16)
+    left = dot(spread, add(*(term[...] for term in out)))
+    left = jnp.concatenate([left[:, :LANES] + dot(last, terms), left[:, LANES:]], axis=1)
+    pack_rows(left.astype(BF16), dot(spread, sums[:, :width]).astype(BF16), packed_ref)
+
+
+def home_kernel(ids_ref, probs_ref, packed_ref, mixed_ref, hidden_ref, grad_ref, out_wide, dx_wide):
+    ids = ids_ref[...]
+    ranks = token_ranks(ids)
+    select = placement(ids, ranks, ROOM)
+    unpack_rows(packed_ref, {0: out_wide, 1: dx_wide})
+    rows = ((0,), (0,))
+    probs = column(probs_ref[...])
+    mixed_ref[...] = (probs * dot(select, out_wide[...], rows)).astype(BF16)
+    hidden_ref[...] = dot(select, dx_wide[...], rows).astype(BF16)
+    last = placement(ids, jnp.full_like(ranks, CAP), ROOM)
+    parts = dot(last, out_wide[:, :LANES], rows)
+    lane = lax.broadcasted_iota(jnp.int32, (ids.shape[1], LANES), 1)
+    terms = jnp.where(lane == column(ranks).astype(jnp.int32), parts, 0.0)
+    grad = jnp.sum(terms, axis=1, keepdims=True) / probs
+    grad_ref[...] = jnp.transpose(jnp.broadcast_to(grad, (grad.shape[0], LANES)))[:1]
+
+
+def home(ids_row, probs_row, packed):
+    slots, width, tokens = packed.shape[0] // TILE, TILE * LANES // 2, ids_row.shape[1]
+    wide = jax.ShapeDtypeStruct((tokens, width), BF16)
     return pl.pallas_call(
-        body,
-        name=name,
-        out_shape=out_shape,
-        in_specs=[pl.BlockSpec(memory_space=pltpu.VMEM)] * len(args),
-        scratch_shapes=[pltpu.VMEM((packed.shape[0] // TILE, TILE * LANES // 2), BF16)],
+        home_kernel,
+        name="home",
+        out_shape=(wide, wide, jax.ShapeDtypeStruct((1, tokens), F32)),
+        in_specs=[pl.BlockSpec(memory_space=pltpu.VMEM)] * 3,
+        scratch_shapes=[pltpu.VMEM((slots, width), BF16)] * 2,
         compiler_params=pltpu.CompilerParams(vmem_limit_bytes=VMEM_LIMIT),
-    )(*args)
+    )(ids_row, probs_row, packed)
 
 
 def shift(value, axis, step):
@@ -326,23 +344,20 @@
         functools.partial(forward_kernel, parts), (act, act, act16) + sums, 2 * product, 5 * moved
     )(*x_rest, *weights, gate, up)
     out_tail, out_other = ring_inputs(*out)
+    wider = (jax.ShapeDtypeStruct((slots, width + LANES), BF16),) * (2 * parts)
     ggp, gup, *dx = kernel_call(
-        functools.partial(backward_kernel, parts), (act16, act16) + sums, 5 * product // 2, 5 * moved
-    )(*s_rest, *weights, gate, up, grad)
+        functools.partial(backward_kernel, parts), (act16, act16) + wider, 5 * product // 2, 5 * moved
+    )(*s_rest, *weights, gate, up, gated, grad)
     out_sum, _ = summed(out, out_tail, out_other)
     dx_sum, last = summed(dx, *ring_inputs(*dx))
     grads = kernel_call(functools.partial(weights_kernel, parts), (weight, weight, weight), 3 * product, 6 * moved)(
         *x_first, *x_rest, *s_first, *s_rest, after(ggp, last), gup, gated
     )
     dx_sum = (dx_sum[0], after(dx_sum[1], grads[0]), dx_sum[2])
-    packed = over_yz(pack_return(*out_sum, *dx_sum))
-    wide = jax.ShapeDtypeStruct(hidden_states.shape, BF16)
-    row = jax.ShapeDtypeStruct((1, tokens), F32)
-    placed = jax.ShapeDtypeStruct(hidden_states.shape, F32)
-    terms, out_rows = home(home_terms_kernel, "home_terms", (row, placed), ids_row, cotangent, packed)
-    one, two, three = (shift(terms, "mp", step) for step in range(1, parts))
-    mixed, grad_hidden = home(home_rest_kernel, "home_rest", (wide, wide), ids_row, probs_row, out_rows, packed)
-    grad_probs = ((terms + two) + (one + three)).reshape(tokens, 1)
+    packed = jax.ShapeDtypeStruct((EXPERTS * ROOM * TILE, LANES), BF16)
+    packed = kernel_call(return_kernel, packed, 4 * packed.size * LANES, 8 * packed.size)(*out_sum, *dx_sum)
+    mixed, grad_hidden, grad_row = home(ids_row, probs_row, over_yz(packed))
+    grad_probs = grad_row.reshape(tokens, 1)
     return (mixed, grad_hidden, grad_probs, *grads)
 
 

time: 129 us -> 126 us (0.977)
  starting transfers between devices: 18.5 us -> 15 us
  blocking collectives: 55.2 us -> 58 us
    ppermute x19 -> x16, starting transfers between devices: 8.49 us -> 5.34 us  [shift(): lax.ppermute(value, axis, [(i, (i + step) % count) for i in range(count)])]
    all_to_all x2, blocking collectives: 55.2 us -> 58 us  [over_yz(): lax.all_to_all(split, ('y', 'z'), 0, 0, tiled=True).reshape(packed.shape)]
    ppermute x19 -> x16, waiting for transfers between devices: 2.63 us -> 0.78 us  [shift(): lax.ppermute(value, axis, [(i, (i + step) % count) for i in range(count)])]
  transfers between devices with their start and end apart: 31 -> 28, of which waited for: 14 -> 11; matrix products, arithmetic and copies ran while one was open for 1% -> 1% of each run, Pallas kernels for 9% -> 8%
where the time goes in v4:
time: 126 us; the launch traced here: 125 us
  blocking collectives  58 us (46%)
  waiting for transfers between devices  32.7 us (26%)
  Pallas kernels  16.6 us (13%)
  starting transfers between devices  15 us (12%)
  local copies, waits for them, and re-layouts  1.44 us (1%)
    all_to_all x2, blocking collectives, over_yz(): lax.all_to_all(split, ('y', 'z'), 0, 0, tiled=True).reshape(packed.shape)  58 us
    ppermute x12, waiting for transfers between devices, ring(): return lax.ppermute(value, ('core', 'mp'), pairs)  32 us
    pallas_call x7, Pallas kernels, call(): pl.pallas_call(body, name=getattr(body, 'func', body).__name__, out_shape...  11.8 us
    ppermute x12, starting transfers between devices, ring(): return lax.ppermute(value, ('core', 'mp'), pairs)  9.64 us
    ppermute x16, starting transfers between devices, shift(): lax.ppermute(value, axis, [(i, (i + step) % count) for i in range(count)])  5.34 us
    pallas_call x1, Pallas kernels, send(): pl.pallas_call(send_kernel, name='send', out_shape=jax.ShapeDtypeStruct((...  3.08 us
  transfers between devices with their start and end apart: 28, of which 11 were waited for; matrix products, arithmetic and copies ran while one was open for 1% of the time, Pallas kernels for 8%

profile of v4, /device:TPU:32, one launch (start us, length us, event | category | flops | bytes accessed | tf_op | source)
XLA Modules:
  0.0 125.4 jit_solution(9328391448470186442)
XLA Ops:
  0.7 3.1 %send.1 = bf16[2560,128]{1,0:T(8,128)(2,1)} custom-call(s32[1,128]{1,0:T(1,128)} %bitcast.10, bf16[1,128]{1,0:T(2,128)(2,1)} %bitcast.12, bf16[128,1024]{1,0:T(8,128)(2,1)} %hidden_hbm.1, bf16[128,1024]{1,0:T(8,128)(2,1)} %cotangent_hbm.1), custom_call_target="tpu_custom_call" | custom-call | tf_op jit(solution)/shard_map/send/pallas_call | solution.py:108
  3.7 31.6 %all_to_all.10 = bf16[32,80,128]{2,1,0:T(8,128)(2,1)S(1)} all-to-all(bf16[32,80,128]{2,1,0:T(8,128)(2,1)} %bitcast.14), channel_id=1, replica_groups=mesh['y'=4,'z'=8,'core'=2,'mp'=4] {'y','z'}, dimensions={0} | all-to-all | bytes 1310720 | tf_op jit(solution)/shard_map/all_to_all | solution.py:313
  36.5 1.5 %collective-permute-start.3 = (bf16[160,1024]{1,0:T(8,128)(2,1)S(1)}, bf16[160,1024]{1,0:T(8,128)(2,1)S(1)}, u32[]{:S(2)}, u32[]{:S(2)}) collective-permute-start(bf16[160,1024]{1,0:T(8,128)(2,1)S(1)} %get-tuple-element.42.own.refs_0_), channel_id=1, source_target_pairs={{0,1},{1,2},{2,3},{3,0},{4,7},{5,4},{6,5},{7,6},{8,9},{9,10},{10,1... | collective-permute-start | bytes 983048 | tf_op jit(solution)/shard_map/ppermute | solution.py:292
  38.0 1.5 %collective-permute-start.6 = (bf16[160,1024]{1,0:T(8,128)(2,1)S(1)}, bf16[160,1024]{1,0:T(8,128)(2,1)S(1)}, u32[]{:S(2)}, u32[]{:S(2)}) collective-permute-start(bf16[160,1024]{1,0:T(8,128)(2,1)S(1)} %get-tuple-element.43.own.refs_8_), channel_id=1, source_target_pairs={{0,1},{1,2},{2,3},{3,0},{4,7},{5,4},{6,5},{7,6},{8,9},{9,10},{10,1... | collective-permute-start | bytes 983048 | tf_op jit(solution)/shard_map/ppermute | solution.py:292
  39.5 1.2 collective-permute-start.1
  41.1 3.6 %collective-permute-done.3.behind.refs_2_ = bf16[160,1024]{1,0:T(8,128)(2,1)S(1)} collective-permute-done((bf16[160,1024]{1,0:T(8,128)(2,1)S(1)}, bf16[160,1024]{1,0:T(8,128)(2,1)S(1)}, u32[]{:S(2)}, u32[]{:S(2)}) %collective-permute-start.3) | collective-permute-done | bytes 327712 | tf_op jit(solution)/shard_map/ppermute | solution.py:292
  45.0 1.1 collective-permute-start.4
  46.2 2.1 %collective-permute-done.6.behind.refs_10_ = bf16[160,1024]{1,0:T(8,128)(2,1)S(1)} collective-permute-done((bf16[160,1024]{1,0:T(8,128)(2,1)S(1)}, bf16[160,1024]{1,0:T(8,128)(2,1)S(1)}, u32[]{:S(2)}, u32[]{:S(2)}) %collective-permute-start.6) | collective-permute-done | bytes 327712 | tf_op jit(solution)/shard_map/ppermute | solution.py:292
  48.5 3.2 %collective-permute-done.1.behind_other.refs_3_ = bf16[160,1024]{1,0:T(8,128)(2,1)S(1)} collective-permute-done((bf16[160,1024]{1,0:T(8,128)(2,1)S(1)}, bf16[160,1024]{1,0:T(8,128)(2,1)S(1)}, u32[]{:S(2)}, u32[]{:S(2)}) %collective-permute-start.1) | collective-permute-done | bytes 327712 | tf_op jit(solution)/shard_map/ppermute | solution.py:292
  51.8 1.4 %copy-done.2 = bf16[192,4096]{1,0:T(8,128)(2,1)S(1)} copy-done((bf16[192,4096]{1,0:T(8,128)(2,1)S(1)}, bf16[192,4096]{1,0:T(8,128)(2,1)}, u32[]{:S(2)}) %copy-start.2) | copy-done | bytes 1572888
  53.2 0.9 first_x_kernel.1
  54.1 1.2 collective-permute-done.8.behind_other.refs_11_
  55.3 0.5 first_s_kernel.1.refs_10_
  55.8 3.0 %collective-permute-done.5.refs_2_.refs_6_ = bf16[160,1024]{1,0:T(8,128)(2,1)S(1)} collective-permute-done((bf16[160,1024]{1,0:T(8,128)(2,1)S(1)}, bf16[160,1024]{1,0:T(8,128)(2,1)S(1)}, u32[]{:S(2)}, u32[]{:S(2)}) %collective-permute-start.5) | collective-permute-done | bytes 327712 | tf_op jit(solution)/shard_map/ppermute | solution.py:292
  58.8 0.5 collective-permute-start.9
  59.3 3.0 %collective-permute-done.19.refs_2_.refs_14_ = bf16[160,1024]{1,0:T(8,128)(2,1)S(1)} collective-permute-done((bf16[160,1024]{1,0:T(8,128)(2,1)S(1)}, bf16[160,1024]{1,0:T(8,128)(2,1)S(1)}, u32[]{:S(2)}, u32[]{:S(2)}) %collective-permute-start.19) | collective-permute-done | bytes 327712 | tf_op jit(solution)/shard_map/ppermute | solution.py:292
  62.3 0.5 collective-permute-start.20
  62.8 1.7 %forward_kernel.1 = (f32[320,192]{1,0:T(8,128)S(1)}, f32[320,192]{1,0:T(8,128)S(1)}, bf16[320,192]{1,0:T(8,128)(2,1)S(1)}, bf16[160,1024]{1,0:T(8,128)(2,1)S(1)}...) custom-call(bf16[160,1024]{1,0:T(8,128)(2,1)S(1)} %collective-permut, ...), custom_call_target="tpu_custom_call" | custom-call | flops 1006632960 | bytes 7864320 | tf_op jit(solution)/shard_map/forward_kernel/pallas_call | solution.py:28
  65.2 2.7 %backward_kernel.1 = (bf16[320,192]{1,0:T(8,128)(2,1)S(1)}, bf16[320,192]{1,0:T(8,128)(2,1)S(1)}, bf16[160,1152]{1,0:T(8,128)(2,1)S(1)}, bf16[160,1152]{1,0:T(8,...) custom-call(bf16[160,1024]{1,0:T(8,128)(2,1)S(1)} %collective-permut, ...), custom_call_target="tpu_custom_call" | custom-call | flops 1258291200 | bytes 7864320 | tf_op jit(solution)/shard_map/backward_kernel/pallas_call | solution.py:28
  69.5 0.7 collective-permute-done.22
  70.3 0.8 collective-permute-start.15
  71.2 1.3 %collective-permute-start.23 = (bf16[160,1152]{1,0:T(8,128)(2,1)S(1)}, bf16[160,1152]{1,0:T(8,128)(2,1)S(1)}, u32[]{:S(2)}, u32[]{:S(2)}) collective-permute-start(bf16[160,1152]{1,0:T(8,128)(2,1)S(1)} %add_convert_fusion.3), channel_id=1, source_target_pairs={{0,1},{1,2},{2,3},{3,0},{4,7},{5,4},{6,5},{7,6},{8,9},{9,10},{10,1... | collective-permute-start | bytes 1105928 | tf_op jit(solution)/shard_map/ppermute | solution.py:292
  72.6 1.8 %collective-permute-start.26 = (bf16[160,1152]{1,0:T(8,128)(2,1)S(1)}, bf16[160,1152]{1,0:T(8,128)(2,1)S(1)}, u32[]{:S(2)}, u32[]{:S(2)}) collective-permute-start(bf16[160,1152]{1,0:T(8,128)(2,1)S(1)} %add_convert_fusion.1), channel_id=1, source_target_pairs={{0,1},{1,2},{2,3},{3,0},{4,7},{5,4},{6,5},{7,6},{8,9},{9,10},{10,1... | collective-permute-start | bytes 1105928 | tf_op jit(solution)/shard_map/ppermute | solution.py:292
  74.3 3.1 %collective-permute-done.12 = bf16[160,1024]{1,0:T(8,128)(2,1)S(1)} collective-permute-done((bf16[160,1024]{1,0:T(8,128)(2,1)S(1)}, bf16[160,1024]{1,0:T(8,128)(2,1)S(1)}, u32[]{:S(2)}, u32[]{:S(2)}) %collective-permute-start.12) | collective-permute-done | bytes 327712 | tf_op jit(solution)/shard_map/ppermute | solution.py:292
  77.7 7.2 %collective-permute-done.23 = bf16[160,1152]{1,0:T(8,128)(2,1)S(1)} collective-permute-done((bf16[160,1152]{1,0:T(8,128)(2,1)S(1)}, bf16[160,1152]{1,0:T(8,128)(2,1)S(1)}, u32[]{:S(2)}, u32[]{:S(2)}) %collective-permute-start.23) | collective-permute-done | bytes 368672 | tf_op jit(solution)/shard_map/ppermute | solution.py:292
  85.1 3.7 %collective-permute-done.26 = bf16[160,1152]{1,0:T(8,128)(2,1)S(1)} collective-permute-done((bf16[160,1152]{1,0:T(8,128)(2,1)S(1)}, bf16[160,1152]{1,0:T(8,128)(2,1)S(1)}, u32[]{:S(2)}, u32[]{:S(2)}) %collective-permute-start.26) | collective-permute-done | bytes 368672 | tf_op jit(solution)/shard_map/ppermute | solution.py:292
  89.4 0.6 collective-permute-start.16
  89.9 4.5 %weights_kernel.1 = (bf16[192,4096]{1,0:T(8,128)(2,1)}, bf16[192,4096]{1,0:T(8,128)(2,1)}, bf16[192,4096]{1,0:T(8,128)(2,1)}) custom-call(bf16[160,1024]{1,0:T(8,128)(2,1)S(1)} %get-tuple-element.42.own.refs_0_, bf16[160,1024]{1,0:T(8,128)(2,1)S(1)} %collective-permute-done.own_other.refs_1_, bf16[160,1024]{1,0:T(8,128)(2,1)S(1)} %collective-permute-done.3.behind.refs_2_, ...), custom_call_target="tpu_custom_call" | custom-call | flops 1509949440 | bytes 9437184 | tf_op jit(solution)/shard_map/weights_kernel/pallas_call | solution.py:28
  94.4 1.9 %collective-permute-done.24.refs_4_ = bf16[160,1152]{1,0:T(8,128)(2,1)S(1)} collective-permute-done((bf16[160,1152]{1,0:T(8,128)(2,1)S(1)}, bf16[160,1152]{1,0:T(8,128)(2,1)S(1)}, u32[]{:S(2)}, u32[]{:S(2)}) %collective-permute-start.24) | collective-permute-done | bytes 368672 | tf_op jit(solution)/shard_map/ppermute | solution.py:292
  96.3 1.1 return_kernel.1
  97.4 26.3 %all_to_all.11 = bf16[32,96,128]{2,1,0:T(8,128)(2,1)S(1)} all-to-all(bf16[32,96,128]{2,1,0:T(8,128)(2,1)S(1)} %bitcast.8), channel_id=1, replica_groups=mesh['y'=4,'z'=8,'core'=2,'mp'=4] {'y','z'}, dimensions={0} | all-to-all | bytes 1572864 | tf_op jit(solution)/shard_map/all_to_all | solution.py:313
  123.7 1.7 %home.1 = (bf16[128,1024]{1,0:T(8,128)(2,1)}, bf16[128,1024]{1,0:T(8,128)(2,1)}, f32[1,128]{1,0:T(1,128)}) custom-call(s32[1,128]{1,0:T(1,128)S(1)} %bitcast.11, bf16[1,128]{1,0:T(2,128)(2,1)S(1)} %bitcast.13, bf16[3072,128]{1,0:T(8,128)(2,1)S(1)} %bitcast.7), custom_call_target="tpu_custom_call" | custom-call | tf_op jit(solution)/shard_map/home/pallas_call | solution.py:269
  (55 shorter events, 5.6 us)
Async XLA Ops:
  0.6 51.1 %copy-start = (bf16[192,4096]{1,0:T(8,128)(2,1)S(1)}, bf16[192,4096]{1,0:T(8,128)(2,1)}, u32[]{:S(2)}) copy-start(bf16[192,4096]{1,0:T(8,128)(2,1)} %refs_6_.3) | copy-start | bytes 4718596
  0.6 51.1 %copy-start.1 = (bf16[192,4096]{1,0:T(8,128)(2,1)S(1)}, bf16[192,4096]{1,0:T(8,128)(2,1)}, u32[]{:S(2)}) copy-start(bf16[192,4096]{1,0:T(8,128)(2,1)} %refs_4_.3) | copy-start | bytes 4718596
  35.9 3.6 %collective-permute-start = (bf16[160,1024]{1,0:T(8,128)(2,1)S(1)}, bf16[160,1024]{1,0:T(8,128)(2,1)S(1)}, u32[]{:S(2)}, u32[]{:S(2)}) collective-permute-start(bf16[160,1024]{1,0:T(8,128)(2,1)S(1)} %get-tuple-element.42.own.refs_0_), channel_id=1, source_target_pairs={{0,4},{4,0},{1,5},{5,1},{2,6},{6,2},{3,7},{7,3},{8,12},{12,8},{9,1... | collective-permute-start | bytes 983048 | tf_op jit(solution)/shard_map/ppermute | solution.py:281
  36.0 4.7 %collective-permute-start.7 = (bf16[160,1024]{1,0:T(8,128)(2,1)S(1)}, bf16[160,1024]{1,0:T(8,128)(2,1)S(1)}, u32[]{:S(2)}, u32[]{:S(2)}) collective-permute-start(bf16[160,1024]{1,0:T(8,128)(2,1)S(1)} %get-tuple-element.43.own.refs_8_), channel_id=1, source_target_pairs={{0,4},{4,0},{1,5},{5,1},{2,6},{6,2},{3,7},{7,3},{8,12},{12,8},{9,1... | collective-permute-start | bytes 983048 | tf_op jit(solution)/shard_map/ppermute | solution.py:281
  36.5 8.3 %collective-permute-start.3 = (bf16[160,1024]{1,0:T(8,128)(2,1)S(1)}, bf16[160,1024]{1,0:T(8,128)(2,1)S(1)}, u32[]{:S(2)}, u32[]{:S(2)}) collective-permute-start(bf16[160,1024]{1,0:T(8,128)(2,1)S(1)} %get-tuple-element.42.own.refs_0_), channel_id=1, source_target_pairs={{0,1},{1,2},{2,3},{3,0},{4,7},{5,4},{6,5},{7,6},{8,9},{9,10},{10,1... | collective-permute-start | bytes 983048 | tf_op jit(solution)/shard_map/ppermute | solution.py:292
  38.0 10.3 %collective-permute-start.6 = (bf16[160,1024]{1,0:T(8,128)(2,1)S(1)}, bf16[160,1024]{1,0:T(8,128)(2,1)S(1)}, u32[]{:S(2)}, u32[]{:S(2)}) collective-permute-start(bf16[160,1024]{1,0:T(8,128)(2,1)S(1)} %get-tuple-element.43.own.refs_8_), channel_id=1, source_target_pairs={{0,1},{1,2},{2,3},{3,0},{4,7},{5,4},{6,5},{7,6},{8,9},{9,10},{10,1... | collective-permute-start | bytes 983048 | tf_op jit(solution)/shard_map/ppermute | solution.py:292
  39.5 12.3 %collective-permute-start.1 = (bf16[160,1024]{1,0:T(8,128)(2,1)S(1)}, bf16[160,1024]{1,0:T(8,128)(2,1)S(1)}, u32[]{:S(2)}, u32[]{:S(2)}) collective-permute-start(bf16[160,1024]{1,0:T(8,128)(2,1)S(1)} %collective-permute-done.own_other.refs_1_), channel_id=1, source_target_pairs={{0,1},{1,2},{2,3},{3,0},{4,7},{5,4},{6,5},{7,6},{8,9},{9,10},{10,1... | collective-permute-start | bytes 983048 | tf_op jit(solution)/shard_map/ppermute | solution.py:292
  40.7 14.6 %collective-permute-start.8 = (bf16[160,1024]{1,0:T(8,128)(2,1)S(1)}, bf16[160,1024]{1,0:T(8,128)(2,1)S(1)}, u32[]{:S(2)}, u32[]{:S(2)}) collective-permute-start(bf16[160,1024]{1,0:T(8,128)(2,1)S(1)} %collective-permute-done.7.own_other.refs_9_), channel_id=1, source_target_pairs={{0,1},{1,2},{2,3},{3,0},{4,7},{5,4},{6,5},{7,6},{8,9},{9,10},{10,1... | collective-permute-start | bytes 983048 | tf_op jit(solution)/shard_map/ppermute | solution.py:292
  44.8 14.0 %collective-permute-start.5 = (bf16[160,1024]{1,0:T(8,128)(2,1)S(1)}, bf16[160,1024]{1,0:T(8,128)(2,1)S(1)}, u32[]{:S(2)}, u32[]{:S(2)}) collective-permute-start(bf16[160,1024]{1,0:T(8,128)(2,1)S(1)} %collective-permute-done.3.behind.refs_2_), channel_id=1, source_target_pairs={{0,1},{1,2},{2,3},{3,0},{4,7},{5,4},{6,5},{7,6},{8,9},{9,10},{10,1... | collective-permute-start | bytes 983048 | tf_op jit(solution)/shard_map/ppermute | solution.py:292
  45.0 17.3 %collective-permute-start.4 = (bf16[160,1024]{1,0:T(8,128)(2,1)S(1)}, bf16[160,1024]{1,0:T(8,128)(2,1)S(1)}, u32[]{:S(2)}, u32[]{:S(2)}) collective-permute-start(bf16[160,1024]{1,0:T(8,128)(2,1)S(1)} %collective-permute-done.3.behind.refs_2_), channel_id=1, source_target_pairs={{0,4},{4,0},{1,5},{5,1},{2,6},{6,2},{3,7},{7,3},{8,12},{12,8},{9,1... | collective-permute-start | bytes 983048 | tf_op jit(solution)/shard_map/ppermute | solution.py:281
  48.3 14.0 %collective-permute-start.19 = (bf16[160,1024]{1,0:T(8,128)(2,1)S(1)}, bf16[160,1024]{1,0:T(8,128)(2,1)S(1)}, u32[]{:S(2)}, u32[]{:S(2)}) collective-permute-start(bf16[160,1024]{1,0:T(8,128)(2,1)S(1)} %collective-permute-done.6.behind.refs_10_), channel_id=1, source_target_pairs={{0,1},{1,2},{2,3},{3,0},{4,7},{5,4},{6,5},{7,6},{8,9},{9,10},{10,1... | collective-permute-start | bytes 983048 | tf_op jit(solution)/shard_map/ppermute | solution.py:292
  58.8 4.0 %collective-permute-start.2 = (bf16[160,1024]{1,0:T(8,128)(2,1)S(1)}, bf16[160,1024]{1,0:T(8,128)(2,1)S(1)}, u32[]{:S(2)}, u32[]{:S(2)}) collective-permute-start(bf16[160,1024]{1,0:T(8,128)(2,1)S(1)} %collective-permute-done.1.behind_other.refs_3_), channel_id=1, source_target_pairs={{0,4},{4,0},{1,5},{5,1},{2,6},{6,2},{3,7},{7,3},{8,12},{12,8},{9,1... | collective-permute-start | bytes 983048 | tf_op jit(solution)/shard_map/ppermute | solution.py:281
  58.8 4.0 %collective-permute-start.9 = (bf16[160,1024]{1,0:T(8,128)(2,1)S(1)}, bf16[160,1024]{1,0:T(8,128)(2,1)S(1)}, u32[]{:S(2)}, u32[]{:S(2)}) collective-permute-start(bf16[160,1024]{1,0:T(8,128)(2,1)S(1)} %collective-permute-done.5.refs_2_.refs_6_), channel_id=1, source_target_pairs={{0,4},{4,0},{1,5},{5,1},{2,6},{6,2},{3,7},{7,3},{8,12},{12,8},{9,1... | collective-permute-start | bytes 983048 | tf_op jit(solution)/shard_map/ppermute | solution.py:281
  59.3 5.8 %collective-permute-start.18 = (bf16[160,1024]{1,0:T(8,128)(2,1)S(1)}, bf16[160,1024]{1,0:T(8,128)(2,1)S(1)}, u32[]{:S(2)}, u32[]{:S(2)}) collective-permute-start(bf16[160,1024]{1,0:T(8,128)(2,1)S(1)} %collective-permute-done.6.behind.refs_10_), channel_id=1, source_target_pairs={{0,4},{4,0},{1,5},{5,1},{2,6},{6,2},{3,7},{7,3},{8,12},{12,8},{9,1... | collective-permute-start | bytes 983048 | tf_op jit(solution)/shard_map/ppermute | solution.py:281
  62.3 2.9 %collective-permute-start.17 = (bf16[160,1024]{1,0:T(8,128)(2,1)S(1)}, bf16[160,1024]{1,0:T(8,128)(2,1)S(1)}, u32[]{:S(2)}, u32[]{:S(2)}) collective-permute-start(bf16[160,1024]{1,0:T(8,128)(2,1)S(1)} %collective-permute-done.8.behind_other.refs_11_), channel_id=1, source_target_pairs={{0,4},{4,0},{1,5},{5,1},{2,6},{6,2},{3,7},{7,3},{8,12},{12,8},{9,1... | collective-permute-start | bytes 983048 | tf_op jit(solution)/shard_map/ppermute | solution.py:281
  62.3 2.9 %collective-permute-start.20 = (bf16[160,1024]{1,0:T(8,128)(2,1)S(1)}, bf16[160,1024]{1,0:T(8,128)(2,1)S(1)}, u32[]{:S(2)}, u32[]{:S(2)}) collective-permute-start(bf16[160,1024]{1,0:T(8,128)(2,1)S(1)} %collective-permute-done.19.refs_2_.refs_14_), channel_id=1, source_target_pairs={{0,4},{4,0},{1,5},{5,1},{2,6},{6,2},{3,7},{7,3},{8,12},{12,8},{9,1... | collective-permute-start | bytes 983048 | tf_op jit(solution)/shard_map/ppermute | solution.py:281
  64.5 4.0 %collective-permute-start.11 = (bf16[160,1024]{1,0:T(8,128)(2,1)S(1)}, bf16[160,1024]{1,0:T(8,128)(2,1)S(1)}, u32[]{:S(2)}, u32[]{:S(2)}) collective-permute-start(bf16[160,1024]{1,0:T(8,128)(2,1)S(1)} %get-tuple-element.52), channel_id=1, source_target_pairs={{0,4},{4,0},{1,5},{5,1},{2,6},{6,2},{3,7},{7,3},{8,12},{12,8},{9,1... | collective-permute-start | bytes 983048 | tf_op jit(solution)/shard_map/ppermute | solution.py:281
  64.6 8.0 %collective-permute-start.10 = (bf16[160,1024]{1,0:T(8,128)(2,1)S(1)}, bf16[160,1024]{1,0:T(8,128)(2,1)S(1)}, u32[]{:S(2)}, u32[]{:S(2)}) collective-permute-start(bf16[160,1024]{1,0:T(8,128)(2,1)S(1)} %get-tuple-element.50), channel_id=1, source_target_pairs={{0,4},{4,0},{1,5},{5,1},{2,6},{6,2},{3,7},{7,3},{8,12},{12,8},{9,1... | collective-permute-start | bytes 983048 | tf_op jit(solution)/shard_map/ppermute | solution.py:281
  65.1 3.9 %collective-permute-start.14 = (bf16[160,1024]{1,0:T(8,128)(2,1)S(1)}, bf16[160,1024]{1,0:T(8,128)(2,1)S(1)}, u32[]{:S(2)}, u32[]{:S(2)}) collective-permute-start(bf16[160,1024]{1,0:T(8,128)(2,1)S(1)} %get-tuple-element.55), channel_id=1, source_target_pairs={{0,4},{4,0},{1,5},{5,1},{2,6},{6,2},{3,7},{7,3},{8,12},{12,8},{9,1... | collective-permute-start | bytes 983048 | tf_op jit(solution)/shard_map/ppermute | solution.py:281
  67.9 9.7 %collective-permute-start.21 = (bf16[160,1152]{1,0:T(8,128)(2,1)S(1)}, bf16[160,1152]{1,0:T(8,128)(2,1)S(1)}, u32[]{:S(2)}, u32[]{:S(2)}) collective-permute-start(bf16[160,1152]{1,0:T(8,128)(2,1)S(1)} %get-tuple-element.62), channel_id=1, source_target_pairs={{0,4},{4,0},{1,5},{5,1},{2,6},{6,2},{3,7},{7,3},{8,12},{12,8},{9,1... | collective-permute-start | bytes 1105928 | tf_op jit(solution)/shard_map/ppermute | solution.py:281
  68.4 1.8 %collective-permute-start.22 = (bf16[160,1152]{1,0:T(8,128)(2,1)S(1)}, bf16[160,1152]{1,0:T(8,128)(2,1)S(1)}, u32[]{:S(2)}, u32[]{:S(2)}) collective-permute-start(bf16[160,1152]{1,0:T(8,128)(2,1)S(1)} %get-tuple-element.64), channel_id=1, source_target_pairs={{0,4},{4,0},{1,5},{5,1},{2,6},{6,2},{3,7},{7,3},{8,12},{12,8},{9,1... | collective-permute-start | bytes 1105928 | tf_op jit(solution)/shard_map/ppermute | solution.py:281
  68.5 2.7 %collective-permute-start.25 = (bf16[160,1152]{1,0:T(8,128)(2,1)S(1)}, bf16[160,1152]{1,0:T(8,128)(2,1)S(1)}, u32[]{:S(2)}, u32[]{:S(2)}) collective-permute-start(bf16[160,1152]{1,0:T(8,128)(2,1)S(1)} %get-tuple-element.72), channel_id=1, source_target_pairs={{0,4},{4,0},{1,5},{5,1},{2,6},{6,2},{3,7},{7,3},{8,12},{12,8},{9,1... | collective-permute-start | bytes 1105928 | tf_op jit(solution)/shard_map/ppermute | solution.py:281
  69.1 8.4 %collective-permute-start.12 = (bf16[160,1024]{1,0:T(8,128)(2,1)S(1)}, bf16[160,1024]{1,0:T(8,128)(2,1)S(1)}, u32[]{:S(2)}, u32[]{:S(2)}) collective-permute-start(bf16[160,1024]{1,0:T(8,128)(2,1)S(1)} %add_convert_fusion.7), channel_id=1, source_target_pairs={{0,1},{1,2},{2,3},{3,0},{4,7},{5,4},{6,5},{7,6},{8,9},{9,10},{10,1... | collective-permute-start | bytes 983048 | tf_op jit(solution)/shard_map/ppermute | solution.py:292
  70.3 19.0 %collective-permute-start.15 = (bf16[160,1024]{1,0:T(8,128)(2,1)S(1)}, bf16[160,1024]{1,0:T(8,128)(2,1)S(1)}, u32[]{:S(2)}, u32[]{:S(2)}) collective-permute-start(bf16[160,1024]{1,0:T(8,128)(2,1)S(1)} %add_convert_fusion.5), channel_id=1, source_target_pairs={{0,1},{1,2},{2,3},{3,0},{4,7},{5,4},{6,5},{7,6},{8,9},{9,10},{10,1... | collective-permute-start | bytes 983048 | tf_op jit(solution)/shard_map/ppermute | solution.py:292
  71.2 13.7 %collective-permute-start.23 = (bf16[160,1152]{1,0:T(8,128)(2,1)S(1)}, bf16[160,1152]{1,0:T(8,128)(2,1)S(1)}, u32[]{:S(2)}, u32[]{:S(2)}) collective-permute-start(bf16[160,1152]{1,0:T(8,128)(2,1)S(1)} %add_convert_fusion.3), channel_id=1, source_target_pairs={{0,1},{1,2},{2,3},{3,0},{4,7},{5,4},{6,5},{7,6},{8,9},{9,10},{10,1... | collective-permute-start | bytes 1105928 | tf_op jit(solution)/shard_map/ppermute | solution.py:292
  72.6 16.2 %collective-permute-start.26 = (bf16[160,1152]{1,0:T(8,128)(2,1)S(1)}, bf16[160,1152]{1,0:T(8,128)(2,1)S(1)}, u32[]{:S(2)}, u32[]{:S(2)}) collective-permute-start(bf16[160,1152]{1,0:T(8,128)(2,1)S(1)} %add_convert_fusion.1), channel_id=1, source_target_pairs={{0,1},{1,2},{2,3},{3,0},{4,7},{5,4},{6,5},{7,6},{8,9},{9,10},{10,1... | collective-permute-start | bytes 1105928 | tf_op jit(solution)/shard_map/ppermute | solution.py:292
  77.6 18.7 %collective-permute-start.13 = (bf16[160,1024]{1,0:T(8,128)(2,1)S(1)}, bf16[160,1024]{1,0:T(8,128)(2,1)S(1)}, u32[]{:S(2)}, u32[]{:S(2)}) collective-permute-start(bf16[160,1024]{1,0:T(8,128)(2,1)S(1)} %add_convert_fusion.6), channel_id=1, source_target_pairs={{0,1},{1,2},{2,3},{3,0},{4,7},{5,4},{6,5},{7,6},{8,9},{9,10},{10,1... | collective-permute-start | bytes 983048 | tf_op jit(solution)/shard_map/ppermute | solution.py:292
  85.0 11.3 %collective-permute-start.24 = (bf16[160,1152]{1,0:T(8,128)(2,1)S(1)}, bf16[160,1152]{1,0:T(8,128)(2,1)S(1)}, u32[]{:S(2)}, u32[]{:S(2)}) collective-permute-start(bf16[160,1152]{1,0:T(8,128)(2,1)S(1)} %add_convert_fusion.2), channel_id=1, source_target_pairs={{0,1},{1,2},{2,3},{3,0},{4,7},{5,4},{6,5},{7,6},{8,9},{9,10},{10,1... | collective-permute-start | bytes 1105928 | tf_op jit(solution)/shard_map/ppermute | solution.py:292
  88.9 7.4 %collective-permute-start.27 = (bf16[160,1152]{1,0:T(8,128)(2,1)S(1)}, bf16[160,1152]{1,0:T(8,128)(2,1)S(1)}, u32[]{:S(2)}, u32[]{:S(2)}) collective-permute-start(bf16[160,1152]{1,0:T(8,128)(2,1)S(1)} %add_convert_fusion), channel_id=1, source_target_pairs={{0,4},{4,0},{1,5},{5,1},{2,6},{6,2},{3,7},{7,3},{8,12},{12,8},{9,1... | collective-permute-start | bytes 1105928 | tf_op jit(solution)/shard_map/ppermute | solution.py:281
  89.4 6.9 %collective-permute-start.16 = (bf16[160,1024]{1,0:T(8,128)(2,1)S(1)}, bf16[160,1024]{1,0:T(8,128)(2,1)S(1)}, u32[]{:S(2)}, u32[]{:S(2)}) collective-permute-start(bf16[160,1024]{1,0:T(8,128)(2,1)S(1)} %add_convert_fusion.4), channel_id=1, source_target_pairs={{0,4},{4,0},{1,5},{5,1},{2,6},{6,2},{3,7},{7,3},{8,12},{12,8},{9,1... | collective-permute-start | bytes 983048 | tf_op jit(solution)/shard_map/ppermute | solution.py:281
  96.3 27.4 %copy-start.4 = (s32[128,1]{0,1:T(1,128)S(1)}, s32[128,1]{0,1:T(1,128)}, u32[]{:S(2)}) copy-start(s32[128,1]{0,1:T(1,128)} %param.8) | copy-start | bytes 1540
  96.3 27.4 %copy-start.5 = (bf16[128,1]{0,1:T(2,128)(2,1)S(1)}, bf16[128,1]{0,1:T(2,128)(2,1)}, u32[]{:S(2)}) copy-start(bf16[128,1]{0,1:T(2,128)(2,1)} %param.9) | copy-start | bytes 772
  (2 other events, 10.2 us)

commit v5 on v4

--- a/solution.py
+++ b/solution.py
@@ -45,8 +45,8 @@
     return (in_row == (out_row % TILE) * TILE + out_row // TILE).astype(BF16)
 
 
-def pack_rows(left, right, packed_ref):
-    swap = exchange_matrix()
+def pack_rows(left, right, packed_ref, swap=None):
+    swap = exchange_matrix() if swap is None else swap
     rows = TILE * TILE
     for group in range(packed_ref.shape[0] // rows):
         parts = [side[group * TILE : (group + 1) * TILE] for side in (left, right)]
@@ -94,6 +94,7 @@
     copies = [pltpu.make_async_copy(*pair, sems.at[at]) for at, pair in enumerate(pairs)]
     for copy in copies:
         copy.start()
+    swap = exchange_matrix()
     copies[0].wait()
     select = placement(ids[...], token_ranks(ids[...]), CAP)
     copies[2].wait()
@@ -101,7 +102,7 @@
     copies[1].wait()
     copies[3].wait()
     scaled = (column(probs[...]) * cotangent[...].astype(F32)).astype(BF16)
-    pack_rows(left, dot(select, scaled).astype(BF16), packed_ref)
+    pack_rows(left, dot(select, scaled).astype(BF16), packed_ref, swap)
 
 
 def send(*args):
@@ -338,7 +339,7 @@
         *x_first[:3], waited, *weights
     )
     grad = kernel_call(functools.partial(first_s_kernel, parts), act, product // 2, moved)(*s_first, w_down)
-    x_rest = (swap_cores(x_behind_other), swap_cores(x_behind), x_opposite, swap_cores(after(x_opposite, gate, grad)))
+    x_rest = (swap_cores(x_behind_other), swap_cores(x_behind), x_opposite, swap_cores(after(x_opposite, gate)))
     s_rest = (swap_cores(s_behind_other), swap_cores(s_behind), s_opposite, swap_cores(after(s_opposite, grad)))
     gate, up, gated, *out = kernel_call(
         functools.partial(forward_kernel, parts), (act, act, act16) + sums, 2 * product, 5 * moved

time: 126 us -> 125 us (level)
    ppermute x12, starting transfers between devices: 9.64 us -> 7.87 us  [ring(): return lax.ppermute(value, ('core', 'mp'), pairs)]
where the time goes in v5:
time: 125 us
  blocking collectives  57.9 us (46%)
  waiting for transfers between devices  32.9 us (26%)
  Pallas kernels  16.6 us (13%)
  starting transfers between devices  14.4 us (12%)
  local copies, waits for them, and re-layouts  1.43 us (1%)
    all_to_all x2, blocking collectives, over_yz(): lax.all_to_all(split, ('y', 'z'), 0, 0, tiled=True).reshape(packed.shape)  57.9 us
    ppermute x12, waiting for transfers between devices, ring(): return lax.ppermute(value, ('core', 'mp'), pairs)  32.1 us
    pallas_call x7, Pallas kernels, call(): pl.pallas_call(body, name=getattr(body, 'func', body).__name__, out_shape...  11.8 us
    ppermute x12, starting transfers between devices, ring(): return lax.ppermute(value, ('core', 'mp'), pairs)  7.87 us
    ppermute x16, starting transfers between devices, shift(): lax.ppermute(value, axis, [(i, (i + step) % count) for i in range(count)])  6.56 us
    pallas_call x1, Pallas kernels, send(): pl.pallas_call(send_kernel, name='send', out_shape=jax.ShapeDtypeStruct((...  3.08 us
  transfers between devices with their start and end apart: 28, of which 11 were waited for; matrix products, arithmetic and copies ran while one was open for 1% of the time, Pallas kernels for 8%

profile of v5, /device:TPU:32, one launch (start us, length us, event | category | flops | bytes accessed | tf_op | source)
XLA Modules:
  0.0 125.0 jit_solution(12490616204875855945)
XLA Ops:
  0.7 3.1 %send.1 = bf16[2560,128]{1,0:T(8,128)(2,1)} custom-call(s32[1,128]{1,0:T(1,128)} %bitcast.10, bf16[1,128]{1,0:T(2,128)(2,1)} %bitcast.12, bf16[128,1024]{1,0:T(8,128)(2,1)} %hidden_hbm.1, bf16[128,1024]{1,0:T(8,128)(2,1)} %cotangent_hbm.1), custom_call_target="tpu_custom_call" | custom-call | tf_op jit(solution)/shard_map/send/pallas_call | solution.py:109
  3.7 31.6 %all_to_all.10 = bf16[32,80,128]{2,1,0:T(8,128)(2,1)S(1)} all-to-all(bf16[32,80,128]{2,1,0:T(8,128)(2,1)} %bitcast.14), channel_id=1, replica_groups=mesh['y'=4,'z'=8,'core'=2,'mp'=4] {'y','z'}, dimensions={0} | all-to-all | bytes 1310720 | tf_op jit(solution)/shard_map/all_to_all | solution.py:314
  36.0 1.6 %collective-permute-start.3 = (bf16[160,1024]{1,0:T(8,128)(2,1)S(1)}, bf16[160,1024]{1,0:T(8,128)(2,1)S(1)}, u32[]{:S(2)}, u32[]{:S(2)}) collective-permute-start(bf16[160,1024]{1,0:T(8,128)(2,1)S(1)} %get-tuple-element.42.own.refs_0_), channel_id=1, source_target_pairs={{0,1},{1,2},{2,3},{3,0},{4,7},{5,4},{6,5},{7,6},{8,9},{9,10},{10,1... | collective-permute-start | bytes 983048 | tf_op jit(solution)/shard_map/ppermute | solution.py:293
  37.5 1.4 %collective-permute-start.15 = (bf16[160,1024]{1,0:T(8,128)(2,1)S(1)}, bf16[160,1024]{1,0:T(8,128)(2,1)S(1)}, u32[]{:S(2)}, u32[]{:S(2)}) collective-permute-start(bf16[160,1024]{1,0:T(8,128)(2,1)S(1)} %get-tuple-element.43.own.refs_8_), channel_id=1, source_target_pairs={{0,4},{4,0},{1,5},{5,1},{2,6},{6,2},{3,7},{7,3},{8,12},{12,8},{9,1... | collective-permute-start | bytes 983048 | tf_op jit(solution)/shard_map/ppermute | solution.py:282
  39.0 1.2 collective-permute-start.1
  40.2 4.1 %collective-permute-done.3.behind.refs_2_ = bf16[160,1024]{1,0:T(8,128)(2,1)S(1)} collective-permute-done((bf16[160,1024]{1,0:T(8,128)(2,1)S(1)}, bf16[160,1024]{1,0:T(8,128)(2,1)S(1)}, u32[]{:S(2)}, u32[]{:S(2)}) %collective-permute-start.3) | collective-permute-done | bytes 327712 | tf_op jit(solution)/shard_map/ppermute | solution.py:293
  44.6 1.5 %collective-permute-start.4 = (bf16[160,1024]{1,0:T(8,128)(2,1)S(1)}, bf16[160,1024]{1,0:T(8,128)(2,1)S(1)}, u32[]{:S(2)}, u32[]{:S(2)}) collective-permute-start(bf16[160,1024]{1,0:T(8,128)(2,1)S(1)} %collective-permute-done.3.behind.refs_2_), channel_id=1, source_target_pairs={{0,4},{4,0},{1,5},{5,1},{2,6},{6,2},{3,7},{7,3},{8,12},{12,8},{9,1... | collective-permute-start | bytes 983048 | tf_op jit(solution)/shard_map/ppermute | solution.py:282
  46.1 1.7 %collective-permute-done.6.behind.refs_10_ = bf16[160,1024]{1,0:T(8,128)(2,1)S(1)} collective-permute-done((bf16[160,1024]{1,0:T(8,128)(2,1)S(1)}, bf16[160,1024]{1,0:T(8,128)(2,1)S(1)}, u32[]{:S(2)}, u32[]{:S(2)}) %collective-permute-start.6) | collective-permute-done | bytes 327712 | tf_op jit(solution)/shard_map/ppermute | solution.py:293
  48.1 3.2 %collective-permute-done.1.behind_other.refs_3_ = bf16[160,1024]{1,0:T(8,128)(2,1)S(1)} collective-permute-done((bf16[160,1024]{1,0:T(8,128)(2,1)S(1)}, bf16[160,1024]{1,0:T(8,128)(2,1)S(1)}, u32[]{:S(2)}, u32[]{:S(2)}) %collective-permute-start.1) | collective-permute-done | bytes 327712 | tf_op jit(solution)/shard_map/ppermute | solution.py:293
  51.4 1.4 %copy-done.2 = bf16[192,4096]{1,0:T(8,128)(2,1)S(1)} copy-done((bf16[192,4096]{1,0:T(8,128)(2,1)S(1)}, bf16[192,4096]{1,0:T(8,128)(2,1)}, u32[]{:S(2)}) %copy-start.2) | copy-done | bytes 1572888
  52.8 0.9 first_x_kernel.1
  53.6 1.2 collective-permute-done.5.refs_2_.refs_6_
  54.9 0.5 collective-permute-start.7
  55.4 3.0 %collective-permute-done.16.behind_other.refs_11_ = bf16[160,1024]{1,0:T(8,128)(2,1)S(1)} collective-permute-done((bf16[160,1024]{1,0:T(8,128)(2,1)S(1)}, bf16[160,1024]{1,0:T(8,128)(2,1)S(1)}, u32[]{:S(2)}, u32[]{:S(2)}) %collective-permute-start.16) | collective-permute-done | bytes 327712 | tf_op jit(solution)/shard_map/ppermute | solution.py:293
  58.4 0.5 first_s_kernel.1.refs_10_
  58.9 3.0 %collective-permute-done.19.refs_2_.refs_14_ = bf16[160,1024]{1,0:T(8,128)(2,1)S(1)} collective-permute-done((bf16[160,1024]{1,0:T(8,128)(2,1)S(1)}, bf16[160,1024]{1,0:T(8,128)(2,1)S(1)}, u32[]{:S(2)}, u32[]{:S(2)}) %collective-permute-start.19) | collective-permute-done | bytes 327712 | tf_op jit(solution)/shard_map/ppermute | solution.py:293
  61.9 0.5 collective-permute-start.20
  62.4 1.7 %forward_kernel.1 = (f32[320,192]{1,0:T(8,128)S(1)}, f32[320,192]{1,0:T(8,128)S(1)}, bf16[320,192]{1,0:T(8,128)(2,1)S(1)}, bf16[160,1024]{1,0:T(8,128)(2,1)S(1)}...) custom-call(bf16[160,1024]{1,0:T(8,128)(2,1)S(1)} %collective-permut, ...), custom_call_target="tpu_custom_call" | custom-call | flops 1006632960 | bytes 7864320 | tf_op jit(solution)/shard_map/forward_kernel/pallas_call | solution.py:28
  64.8 2.7 %backward_kernel.1 = (bf16[320,192]{1,0:T(8,128)(2,1)S(1)}, bf16[320,192]{1,0:T(8,128)(2,1)S(1)}, bf16[160,1152]{1,0:T(8,128)(2,1)S(1)}, bf16[160,1152]{1,0:T(8,...) custom-call(bf16[160,1024]{1,0:T(8,128)(2,1)S(1)} %collective-permut, ...), custom_call_target="tpu_custom_call" | custom-call | flops 1258291200 | bytes 7864320 | tf_op jit(solution)/shard_map/backward_kernel/pallas_call | solution.py:28
  69.1 0.7 collective-permute-done.22
  69.8 0.8 collective-permute-start.13
  70.8 1.3 %collective-permute-start.23 = (bf16[160,1152]{1,0:T(8,128)(2,1)S(1)}, bf16[160,1152]{1,0:T(8,128)(2,1)S(1)}, u32[]{:S(2)}, u32[]{:S(2)}) collective-permute-start(bf16[160,1152]{1,0:T(8,128)(2,1)S(1)} %add_convert_fusion.3), channel_id=1, source_target_pairs={{0,1},{1,2},{2,3},{3,0},{4,7},{5,4},{6,5},{7,6},{8,9},{9,10},{10,1... | collective-permute-start | bytes 1105928 | tf_op jit(solution)/shard_map/ppermute | solution.py:293
  72.2 1.7 %collective-permute-start.26 = (bf16[160,1152]{1,0:T(8,128)(2,1)S(1)}, bf16[160,1152]{1,0:T(8,128)(2,1)S(1)}, u32[]{:S(2)}, u32[]{:S(2)}) collective-permute-start(bf16[160,1152]{1,0:T(8,128)(2,1)S(1)} %add_convert_fusion.1), channel_id=1, source_target_pairs={{0,1},{1,2},{2,3},{3,0},{4,7},{5,4},{6,5},{7,6},{8,9},{9,10},{10,1... | collective-permute-start | bytes 1105928 | tf_op jit(solution)/shard_map/ppermute | solution.py:293
  73.9 3.1 %collective-permute-done.10 = bf16[160,1024]{1,0:T(8,128)(2,1)S(1)} collective-permute-done((bf16[160,1024]{1,0:T(8,128)(2,1)S(1)}, bf16[160,1024]{1,0:T(8,128)(2,1)S(1)}, u32[]{:S(2)}, u32[]{:S(2)}) %collective-permute-start.10) | collective-permute-done | bytes 327712 | tf_op jit(solution)/shard_map/ppermute | solution.py:293
  77.3 7.2 %collective-permute-done.23 = bf16[160,1152]{1,0:T(8,128)(2,1)S(1)} collective-permute-done((bf16[160,1152]{1,0:T(8,128)(2,1)S(1)}, bf16[160,1152]{1,0:T(8,128)(2,1)S(1)}, u32[]{:S(2)}, u32[]{:S(2)}) %collective-permute-start.23) | collective-permute-done | bytes 368672 | tf_op jit(solution)/shard_map/ppermute | solution.py:293
  84.7 3.7 %collective-permute-done.26 = bf16[160,1152]{1,0:T(8,128)(2,1)S(1)} collective-permute-done((bf16[160,1152]{1,0:T(8,128)(2,1)S(1)}, bf16[160,1152]{1,0:T(8,128)(2,1)S(1)}, u32[]{:S(2)}, u32[]{:S(2)}) %collective-permute-start.26) | collective-permute-done | bytes 368672 | tf_op jit(solution)/shard_map/ppermute | solution.py:293
  88.9 0.6 collective-permute-start.14
  89.5 4.5 %weights_kernel.1 = (bf16[192,4096]{1,0:T(8,128)(2,1)}, bf16[192,4096]{1,0:T(8,128)(2,1)}, bf16[192,4096]{1,0:T(8,128)(2,1)}) custom-call(bf16[160,1024]{1,0:T(8,128)(2,1)S(1)} %get-tuple-element.42.own.refs_0_, bf16[160,1024]{1,0:T(8,128)(2,1)S(1)} %collective-permute-done.own_other.refs_1_, bf16[160,1024]{1,0:T(8,128)(2,1)S(1)} %collective-permute-done.3.behind.refs_2_, ...), custom_call_target="tpu_custom_call" | custom-call | flops 1509949440 | bytes 9437184 | tf_op jit(solution)/shard_map/weights_kernel/pallas_call | solution.py:28
  94.0 1.9 %collective-permute-done.24.refs_4_ = bf16[160,1152]{1,0:T(8,128)(2,1)S(1)} collective-permute-done((bf16[160,1152]{1,0:T(8,128)(2,1)S(1)}, bf16[160,1152]{1,0:T(8,128)(2,1)S(1)}, u32[]{:S(2)}, u32[]{:S(2)}) %collective-permute-start.24) | collective-permute-done | bytes 368672 | tf_op jit(solution)/shard_map/ppermute | solution.py:293
  95.9 1.1 return_kernel.1
  97.0 26.3 %all_to_all.11 = bf16[32,96,128]{2,1,0:T(8,128)(2,1)S(1)} all-to-all(bf16[32,96,128]{2,1,0:T(8,128)(2,1)S(1)} %bitcast.8), channel_id=1, replica_groups=mesh['y'=4,'z'=8,'core'=2,'mp'=4] {'y','z'}, dimensions={0} | all-to-all | bytes 1572864 | tf_op jit(solution)/shard_map/all_to_all | solution.py:314
  123.3 1.7 %home.1 = (bf16[128,1024]{1,0:T(8,128)(2,1)}, bf16[128,1024]{1,0:T(8,128)(2,1)}, f32[1,128]{1,0:T(1,128)}) custom-call(s32[1,128]{1,0:T(1,128)S(1)} %bitcast.11, bf16[1,128]{1,0:T(2,128)(2,1)S(1)} %bitcast.13, bf16[3072,128]{1,0:T(8,128)(2,1)S(1)} %bitcast.7), custom_call_target="tpu_custom_call" | custom-call | tf_op jit(solution)/shard_map/home/pallas_call | solution.py:270
  (55 shorter events, 4.8 us)
Async XLA Ops:
  0.6 50.7 %copy-start = (bf16[192,4096]{1,0:T(8,128)(2,1)S(1)}, bf16[192,4096]{1,0:T(8,128)(2,1)}, u32[]{:S(2)}) copy-start(bf16[192,4096]{1,0:T(8,128)(2,1)} %refs_6_.3) | copy-start | bytes 4718596
  0.6 50.7 %copy-start.1 = (bf16[192,4096]{1,0:T(8,128)(2,1)S(1)}, bf16[192,4096]{1,0:T(8,128)(2,1)}, u32[]{:S(2)}) copy-start(bf16[192,4096]{1,0:T(8,128)(2,1)} %refs_4_.3) | copy-start | bytes 4718596
  35.9 3.2 %collective-permute-start = (bf16[160,1024]{1,0:T(8,128)(2,1)S(1)}, bf16[160,1024]{1,0:T(8,128)(2,1)S(1)}, u32[]{:S(2)}, u32[]{:S(2)}) collective-permute-start(bf16[160,1024]{1,0:T(8,128)(2,1)S(1)} %get-tuple-element.42.own.refs_0_), channel_id=1, source_target_pairs={{0,4},{4,0},{1,5},{5,1},{2,6},{6,2},{3,7},{7,3},{8,12},{12,8},{9,1... | collective-permute-start | bytes 983048 | tf_op jit(solution)/shard_map/ppermute | solution.py:282
  36.0 8.4 %collective-permute-start.3 = (bf16[160,1024]{1,0:T(8,128)(2,1)S(1)}, bf16[160,1024]{1,0:T(8,128)(2,1)S(1)}, u32[]{:S(2)}, u32[]{:S(2)}) collective-permute-start(bf16[160,1024]{1,0:T(8,128)(2,1)S(1)} %get-tuple-element.42.own.refs_0_), channel_id=1, source_target_pairs={{0,1},{1,2},{2,3},{3,0},{4,7},{5,4},{6,5},{7,6},{8,9},{9,10},{10,1... | collective-permute-start | bytes 983048 | tf_op jit(solution)/shard_map/ppermute | solution.py:293
  37.5 8.5 %collective-permute-start.15 = (bf16[160,1024]{1,0:T(8,128)(2,1)S(1)}, bf16[160,1024]{1,0:T(8,128)(2,1)S(1)}, u32[]{:S(2)}, u32[]{:S(2)}) collective-permute-start(bf16[160,1024]{1,0:T(8,128)(2,1)S(1)} %get-tuple-element.43.own.refs_8_), channel_id=1, source_target_pairs={{0,4},{4,0},{1,5},{5,1},{2,6},{6,2},{3,7},{7,3},{8,12},{12,8},{9,1... | collective-permute-start | bytes 983048 | tf_op jit(solution)/shard_map/ppermute | solution.py:282
  38.9 8.9 %collective-permute-start.6 = (bf16[160,1024]{1,0:T(8,128)(2,1)S(1)}, bf16[160,1024]{1,0:T(8,128)(2,1)S(1)}, u32[]{:S(2)}, u32[]{:S(2)}) collective-permute-start(bf16[160,1024]{1,0:T(8,128)(2,1)S(1)} %get-tuple-element.43.own.refs_8_), channel_id=1, source_target_pairs={{0,1},{1,2},{2,3},{3,0},{4,7},{5,4},{6,5},{7,6},{8,9},{9,10},{10,1... | collective-permute-start | bytes 983048 | tf_op jit(solution)/shard_map/ppermute | solution.py:293
  39.0 12.3 %collective-permute-start.1 = (bf16[160,1024]{1,0:T(8,128)(2,1)S(1)}, bf16[160,1024]{1,0:T(8,128)(2,1)S(1)}, u32[]{:S(2)}, u32[]{:S(2)}) collective-permute-start(bf16[160,1024]{1,0:T(8,128)(2,1)S(1)} %collective-permute-done.own_other.refs_1_), channel_id=1, source_target_pairs={{0,1},{1,2},{2,3},{3,0},{4,7},{5,4},{6,5},{7,6},{8,9},{9,10},{10,1... | collective-permute-start | bytes 983048 | tf_op jit(solution)/shard_map/ppermute | solution.py:293
  44.3 10.5 %collective-permute-start.5 = (bf16[160,1024]{1,0:T(8,128)(2,1)S(1)}, bf16[160,1024]{1,0:T(8,128)(2,1)S(1)}, u32[]{:S(2)}, u32[]{:S(2)}) collective-permute-start(bf16[160,1024]{1,0:T(8,128)(2,1)S(1)} %collective-permute-done.3.behind.refs_2_), channel_id=1, source_target_pairs={{0,1},{1,2},{2,3},{3,0},{4,7},{5,4},{6,5},{7,6},{8,9},{9,10},{10,1... | collective-permute-start | bytes 983048 | tf_op jit(solution)/shard_map/ppermute | solution.py:293
  44.6 17.3 %collective-permute-start.4 = (bf16[160,1024]{1,0:T(8,128)(2,1)S(1)}, bf16[160,1024]{1,0:T(8,128)(2,1)S(1)}, u32[]{:S(2)}, u32[]{:S(2)}) collective-permute-start(bf16[160,1024]{1,0:T(8,128)(2,1)S(1)} %collective-permute-done.3.behind.refs_2_), channel_id=1, source_target_pairs={{0,4},{4,0},{1,5},{5,1},{2,6},{6,2},{3,7},{7,3},{8,12},{12,8},{9,1... | collective-permute-start | bytes 983048 | tf_op jit(solution)/shard_map/ppermute | solution.py:282
  46.1 12.3 %collective-permute-start.16 = (bf16[160,1024]{1,0:T(8,128)(2,1)S(1)}, bf16[160,1024]{1,0:T(8,128)(2,1)S(1)}, u32[]{:S(2)}, u32[]{:S(2)}) collective-permute-start(bf16[160,1024]{1,0:T(8,128)(2,1)S(1)} %collective-permute-done.15.own_other.refs_9_), channel_id=1, source_target_pairs={{0,1},{1,2},{2,3},{3,0},{4,7},{5,4},{6,5},{7,6},{8,9},{9,10},{10,1... | collective-permute-start | bytes 983048 | tf_op jit(solution)/shard_map/ppermute | solution.py:293
  47.8 14.0 %collective-permute-start.19 = (bf16[160,1024]{1,0:T(8,128)(2,1)S(1)}, bf16[160,1024]{1,0:T(8,128)(2,1)S(1)}, u32[]{:S(2)}, u32[]{:S(2)}) collective-permute-start(bf16[160,1024]{1,0:T(8,128)(2,1)S(1)} %collective-permute-done.6.behind.refs_10_), channel_id=1, source_target_pairs={{0,1},{1,2},{2,3},{3,0},{4,7},{5,4},{6,5},{7,6},{8,9},{9,10},{10,1... | collective-permute-start | bytes 983048 | tf_op jit(solution)/shard_map/ppermute | solution.py:293
  54.9 7.5 %collective-permute-start.2 = (bf16[160,1024]{1,0:T(8,128)(2,1)S(1)}, bf16[160,1024]{1,0:T(8,128)(2,1)S(1)}, u32[]{:S(2)}, u32[]{:S(2)}) collective-permute-start(bf16[160,1024]{1,0:T(8,128)(2,1)S(1)} %collective-permute-done.1.behind_other.refs_3_), channel_id=1, source_target_pairs={{0,4},{4,0},{1,5},{5,1},{2,6},{6,2},{3,7},{7,3},{8,12},{12,8},{9,1... | collective-permute-start | bytes 983048 | tf_op jit(solution)/shard_map/ppermute | solution.py:282
  54.9 7.5 %collective-permute-start.7 = (bf16[160,1024]{1,0:T(8,128)(2,1)S(1)}, bf16[160,1024]{1,0:T(8,128)(2,1)S(1)}, u32[]{:S(2)}, u32[]{:S(2)}) collective-permute-start(bf16[160,1024]{1,0:T(8,128)(2,1)S(1)} %collective-permute-done.5.refs_2_.refs_6_), channel_id=1, source_target_pairs={{0,4},{4,0},{1,5},{5,1},{2,6},{6,2},{3,7},{7,3},{8,12},{12,8},{9,1... | collective-permute-start | bytes 983048 | tf_op jit(solution)/shard_map/ppermute | solution.py:282
  58.4 6.3 %collective-permute-start.18 = (bf16[160,1024]{1,0:T(8,128)(2,1)S(1)}, bf16[160,1024]{1,0:T(8,128)(2,1)S(1)}, u32[]{:S(2)}, u32[]{:S(2)}) collective-permute-start(bf16[160,1024]{1,0:T(8,128)(2,1)S(1)} %collective-permute-done.6.behind.refs_10_), channel_id=1, source_target_pairs={{0,4},{4,0},{1,5},{5,1},{2,6},{6,2},{3,7},{7,3},{8,12},{12,8},{9,1... | collective-permute-start | bytes 983048 | tf_op jit(solution)/shard_map/ppermute | solution.py:282
  61.9 2.9 %collective-permute-start.17 = (bf16[160,1024]{1,0:T(8,128)(2,1)S(1)}, bf16[160,1024]{1,0:T(8,128)(2,1)S(1)}, u32[]{:S(2)}, u32[]{:S(2)}) collective-permute-start(bf16[160,1024]{1,0:T(8,128)(2,1)S(1)} %collective-permute-done.16.behind_other.refs_11_), channel_id=1, source_target_pairs={{0,4},{4,0},{1,5},{5,1},{2,6},{6,2},{3,7},{7,3},{8,12},{12,8},{9,1... | collective-permute-start | bytes 983048 | tf_op jit(solution)/shard_map/ppermute | solution.py:282
  61.9 2.9 %collective-permute-start.20 = (bf16[160,1024]{1,0:T(8,128)(2,1)S(1)}, bf16[160,1024]{1,0:T(8,128)(2,1)S(1)}, u32[]{:S(2)}, u32[]{:S(2)}) collective-permute-start(bf16[160,1024]{1,0:T(8,128)(2,1)S(1)} %collective-permute-done.19.refs_2_.refs_14_), channel_id=1, source_target_pairs={{0,4},{4,0},{1,5},{5,1},{2,6},{6,2},{3,7},{7,3},{8,12},{12,8},{9,1... | collective-permute-start | bytes 983048 | tf_op jit(solution)/shard_map/ppermute | solution.py:282
  64.1 4.0 %collective-permute-start.9 = (bf16[160,1024]{1,0:T(8,128)(2,1)S(1)}, bf16[160,1024]{1,0:T(8,128)(2,1)S(1)}, u32[]{:S(2)}, u32[]{:S(2)}) collective-permute-start(bf16[160,1024]{1,0:T(8,128)(2,1)S(1)} %get-tuple-element.52), channel_id=1, source_target_pairs={{0,4},{4,0},{1,5},{5,1},{2,6},{6,2},{3,7},{7,3},{8,12},{12,8},{9,1... | collective-permute-start | bytes 983048 | tf_op jit(solution)/shard_map/ppermute | solution.py:282
  64.2 8.0 %collective-permute-start.8 = (bf16[160,1024]{1,0:T(8,128)(2,1)S(1)}, bf16[160,1024]{1,0:T(8,128)(2,1)S(1)}, u32[]{:S(2)}, u32[]{:S(2)}) collective-permute-start(bf16[160,1024]{1,0:T(8,128)(2,1)S(1)} %get-tuple-element.50), channel_id=1, source_target_pairs={{0,4},{4,0},{1,5},{5,1},{2,6},{6,2},{3,7},{7,3},{8,12},{12,8},{9,1... | collective-permute-start | bytes 983048 | tf_op jit(solution)/shard_map/ppermute | solution.py:282
  64.7 3.9 %collective-permute-start.12 = (bf16[160,1024]{1,0:T(8,128)(2,1)S(1)}, bf16[160,1024]{1,0:T(8,128)(2,1)S(1)}, u32[]{:S(2)}, u32[]{:S(2)}) collective-permute-start(bf16[160,1024]{1,0:T(8,128)(2,1)S(1)} %get-tuple-element.55), channel_id=1, source_target_pairs={{0,4},{4,0},{1,5},{5,1},{2,6},{6,2},{3,7},{7,3},{8,12},{12,8},{9,1... | collective-permute-start | bytes 983048 | tf_op jit(solution)/shard_map/ppermute | solution.py:282
  67.5 9.8 %collective-permute-start.21 = (bf16[160,1152]{1,0:T(8,128)(2,1)S(1)}, bf16[160,1152]{1,0:T(8,128)(2,1)S(1)}, u32[]{:S(2)}, u32[]{:S(2)}) collective-permute-start(bf16[160,1152]{1,0:T(8,128)(2,1)S(1)} %get-tuple-element.62), channel_id=1, source_target_pairs={{0,4},{4,0},{1,5},{5,1},{2,6},{6,2},{3,7},{7,3},{8,12},{12,8},{9,1... | collective-permute-start | bytes 1105928 | tf_op jit(solution)/shard_map/ppermute | solution.py:282
  68.0 1.8 %collective-permute-start.22 = (bf16[160,1152]{1,0:T(8,128)(2,1)S(1)}, bf16[160,1152]{1,0:T(8,128)(2,1)S(1)}, u32[]{:S(2)}, u32[]{:S(2)}) collective-permute-start(bf16[160,1152]{1,0:T(8,128)(2,1)S(1)} %get-tuple-element.64), channel_id=1, source_target_pairs={{0,4},{4,0},{1,5},{5,1},{2,6},{6,2},{3,7},{7,3},{8,12},{12,8},{9,1... | collective-permute-start | bytes 1105928 | tf_op jit(solution)/shard_map/ppermute | solution.py:282
  68.1 2.7 %collective-permute-start.25 = (bf16[160,1152]{1,0:T(8,128)(2,1)S(1)}, bf16[160,1152]{1,0:T(8,128)(2,1)S(1)}, u32[]{:S(2)}, u32[]{:S(2)}) collective-permute-start(bf16[160,1152]{1,0:T(8,128)(2,1)S(1)} %get-tuple-element.72), channel_id=1, source_target_pairs={{0,4},{4,0},{1,5},{5,1},{2,6},{6,2},{3,7},{7,3},{8,12},{12,8},{9,1... | collective-permute-start | bytes 1105928 | tf_op jit(solution)/shard_map/ppermute | solution.py:282
  68.6 8.4 %collective-permute-start.10 = (bf16[160,1024]{1,0:T(8,128)(2,1)S(1)}, bf16[160,1024]{1,0:T(8,128)(2,1)S(1)}, u32[]{:S(2)}, u32[]{:S(2)}) collective-permute-start(bf16[160,1024]{1,0:T(8,128)(2,1)S(1)} %add_convert_fusion.7), channel_id=1, source_target_pairs={{0,1},{1,2},{2,3},{3,0},{4,7},{5,4},{6,5},{7,6},{8,9},{9,10},{10,1... | collective-permute-start | bytes 983048 | tf_op jit(solution)/shard_map/ppermute | solution.py:293
  69.8 19.0 %collective-permute-start.13 = (bf16[160,1024]{1,0:T(8,128)(2,1)S(1)}, bf16[160,1024]{1,0:T(8,128)(2,1)S(1)}, u32[]{:S(2)}, u32[]{:S(2)}) collective-permute-start(bf16[160,1024]{1,0:T(8,128)(2,1)S(1)} %add_convert_fusion.5), channel_id=1, source_target_pairs={{0,1},{1,2},{2,3},{3,0},{4,7},{5,4},{6,5},{7,6},{8,9},{9,10},{10,1... | collective-permute-start | bytes 983048 | tf_op jit(solution)/shard_map/ppermute | solution.py:293
  70.8 13.7 %collective-permute-start.23 = (bf16[160,1152]{1,0:T(8,128)(2,1)S(1)}, bf16[160,1152]{1,0:T(8,128)(2,1)S(1)}, u32[]{:S(2)}, u32[]{:S(2)}) collective-permute-start(bf16[160,1152]{1,0:T(8,128)(2,1)S(1)} %add_convert_fusion.3), channel_id=1, source_target_pairs={{0,1},{1,2},{2,3},{3,0},{4,7},{5,4},{6,5},{7,6},{8,9},{9,10},{10,1... | collective-permute-start | bytes 1105928 | tf_op jit(solution)/shard_map/ppermute | solution.py:293
  72.2 16.2 %collective-permute-start.26 = (bf16[160,1152]{1,0:T(8,128)(2,1)S(1)}, bf16[160,1152]{1,0:T(8,128)(2,1)S(1)}, u32[]{:S(2)}, u32[]{:S(2)}) collective-permute-start(bf16[160,1152]{1,0:T(8,128)(2,1)S(1)} %add_convert_fusion.1), channel_id=1, source_target_pairs={{0,1},{1,2},{2,3},{3,0},{4,7},{5,4},{6,5},{7,6},{8,9},{9,10},{10,1... | collective-permute-start | bytes 1105928 | tf_op jit(solution)/shard_map/ppermute | solution.py:293
  77.2 18.7 %collective-permute-start.11 = (bf16[160,1024]{1,0:T(8,128)(2,1)S(1)}, bf16[160,1024]{1,0:T(8,128)(2,1)S(1)}, u32[]{:S(2)}, u32[]{:S(2)}) collective-permute-start(bf16[160,1024]{1,0:T(8,128)(2,1)S(1)} %add_convert_fusion.6), channel_id=1, source_target_pairs={{0,1},{1,2},{2,3},{3,0},{4,7},{5,4},{6,5},{7,6},{8,9},{9,10},{10,1... | collective-permute-start | bytes 983048 | tf_op jit(solution)/shard_map/ppermute | solution.py:293
  84.6 11.3 %collective-permute-start.24 = (bf16[160,1152]{1,0:T(8,128)(2,1)S(1)}, bf16[160,1152]{1,0:T(8,128)(2,1)S(1)}, u32[]{:S(2)}, u32[]{:S(2)}) collective-permute-start(bf16[160,1152]{1,0:T(8,128)(2,1)S(1)} %add_convert_fusion.2), channel_id=1, source_target_pairs={{0,1},{1,2},{2,3},{3,0},{4,7},{5,4},{6,5},{7,6},{8,9},{9,10},{10,1... | collective-permute-start | bytes 1105928 | tf_op jit(solution)/shard_map/ppermute | solution.py:293
  88.5 7.4 %collective-permute-start.27 = (bf16[160,1152]{1,0:T(8,128)(2,1)S(1)}, bf16[160,1152]{1,0:T(8,128)(2,1)S(1)}, u32[]{:S(2)}, u32[]{:S(2)}) collective-permute-start(bf16[160,1152]{1,0:T(8,128)(2,1)S(1)} %add_convert_fusion), channel_id=1, source_target_pairs={{0,4},{4,0},{1,5},{5,1},{2,6},{6,2},{3,7},{7,3},{8,12},{12,8},{9,1... | collective-permute-start | bytes 1105928 | tf_op jit(solution)/shard_map/ppermute | solution.py:282
  88.9 6.9 %collective-permute-start.14 = (bf16[160,1024]{1,0:T(8,128)(2,1)S(1)}, bf16[160,1024]{1,0:T(8,128)(2,1)S(1)}, u32[]{:S(2)}, u32[]{:S(2)}) collective-permute-start(bf16[160,1024]{1,0:T(8,128)(2,1)S(1)} %add_convert_fusion.4), channel_id=1, source_target_pairs={{0,4},{4,0},{1,5},{5,1},{2,6},{6,2},{3,7},{7,3},{8,12},{12,8},{9,1... | collective-permute-start | bytes 983048 | tf_op jit(solution)/shard_map/ppermute | solution.py:282
  95.9 27.4 %copy-start.4 = (s32[128,1]{0,1:T(1,128)S(1)}, s32[128,1]{0,1:T(1,128)}, u32[]{:S(2)}) copy-start(s32[128,1]{0,1:T(1,128)} %param.8) | copy-start | bytes 1540
  95.9 27.4 %copy-start.5 = (bf16[128,1]{0,1:T(2,128)(2,1)S(1)}, bf16[128,1]{0,1:T(2,128)(2,1)}, u32[]{:S(2)}) copy-start(bf16[128,1]{0,1:T(2,128)(2,1)} %param.9) | copy-start | bytes 772
  (2 other events, 9.0 us)
